TPU v7x, 256 devices: a whole 4x4x8 slice. The times are simulated.
256 devices in a mesh: wide: 16 (over z, core), narrow: 16 (over x, y).
Axes of the slice: x: 4, y: 4, z: 8, core: 2. Of those that a mesh axis runs over, the one named last changes fastest.
Arguments:
- traction: float32 [3, 64, 393216], P(None, None, ('wide', 'narrow')), may hold values from -6 to 6
- near_kernel: bfloat16 [768, 4, 512, 512], P(('wide', 'narrow')), may hold values from -0.125 to 0.125
- neighbours: int32 [768, 4], P(('wide', 'narrow')), may hold values from 0 to 767, as said below
- far_basis: bfloat16 [8, 393216, 128], P(None, ('wide', 'narrow')), may hold values from -4 to 4
- surface_gap: float32 [3, 393216], P(None, ('wide', 'narrow')), may hold values from -3 to 3
- friction: float32 [393216], P(('wide', 'narrow')), may hold values from 0.2 to 1
- contact_flags: int32 [393216], P(('wide', 'narrow')), may hold values 0 or 1
- cluster_order: int32 [393216], P(('wide', 'narrow')), may hold values from 0 to 393215, as said below
- approach: float32 [3, 64], replicated, may hold values from -1 to 2
Outputs:
- traction_new: float32 [3, 64, 393216], P(None, None, ('wide', 'narrow'))
- residual: float32 [3, 64, 393216], P(None, None, ('wide', 'narrow'))
- step_size: float32 [64], replicated
Inputs may be any that keep to these rules, and one draw needn't show every extreme that they name: `neighbours`: entry 0 of row b is b itself; the other 3 entries are distinct blocks other than b, each within 3 blocks of b. `cluster_order`: a permutation of the panels that maps every aligned group of 1536 panels onto itself.
All inputs are finite; a program needn't handle non-finite values. No bound on the sum of `contact_flags` on one device may be relied on, other than what follows from the above.
Results may differ from a plain program's by a relative error of at most 0.0034.
Values may be sent and summed in bfloat16 or wider, within the bound.
No kernel may reach another device: no remote copies, remote signals or barrier semaphores. Data moves between devices by JAX's collectives and lax.ppermute only.
A program may use at most 64 MiB of HBM per device.

v0:
```python
import functools
import math

import jax
import jax.numpy as jnp
from jax import lax
from jax.sharding import Mesh
from jax.sharding import PartitionSpec as P

WIDE_NARROW = ("wide_0", "wide_1", "narrow_0", "narrow_1")
NARROW = ("narrow_0", "narrow_1")
WIDE = ("wide_0", "wide_1")


SLIP_EPS = 0.01


def extended(array, sides, width):
    edges = {}
    for axis, dim in sides:
        size, length = (lax.axis_size(axis), array.shape[dim])
        up = [(i, (i + 1) % size) for i in range(size - 1)]
        last = lax.slice_in_dim(array, length - width, length, axis=dim)
        initial = lax.slice_in_dim(array, 0, width, axis=dim)
        edges[dim] = (
            lax.ppermute(last, axis, up),
            lax.ppermute(initial, axis, [(b, a) for a, b in up]),
        )
    done = []
    for _, dim in sides:
        low, high = edges[dim]
        around = [(width, width) if d in done else (0, 0) for d in range(array.ndim)]
        array = jnp.concatenate([jnp.pad(low, around), array, jnp.pad(high, around)], axis=dim)
        done.append(dim)
    return array


def from_partner(block, axis, stride):
    count = lax.axis_size(axis)
    route = []
    for low in range(count):
        high = low | 1 << stride
        if high != low and high < count:
            route += [(low, high), (high, low)]
    return lax.ppermute(block, axis, route)


def over_axes(array, axes):
    return functools.reduce(lax.psum, axes, array)


def near_field(field_low, near_kernel, neighbours):
    row_count, panel_count = field_low.shape
    blk_dev = near_kernel.shape[0]
    block_len = near_kernel.shape[2]
    padded = extended(field_low, ((WIDE_NARROW, 1),), panel_count)
    blocks = padded.reshape(row_count, 3 * blk_dev, block_len)
    local_ids = jnp.arange(blk_dev, dtype=jnp.int32)
    ext_slots = neighbours - neighbours[:, :1] + local_ids[:, None] + blk_dev
    picked = jnp.take(blocks, ext_slots.reshape(-1), axis=1)
    picked = picked.reshape(row_count, blk_dev, neighbours.shape[1], block_len)
    result = jnp.einsum("bkij,xbkj->xbi", near_kernel, picked, preferred_element_type=jnp.float32)
    return result.reshape(row_count, panel_count)


def tree_totals(coeffs):
    narrow_bits = lax.axis_size(NARROW).bit_length() - 1
    wide_bits = lax.axis_size(WIDE).bit_length() - 1
    for bit_pos in range(narrow_bits + wide_bits):
        partner = from_partner(coeffs[bit_pos:], WIDE_NARROW, bit_pos)
        coeffs = jnp.concatenate([coeffs[:bit_pos], coeffs[bit_pos:] + partner], axis=0)
    return coeffs


def level_gains(panel_count, level_count, rank_len):
    gain_list = [
        0.64 / math.sqrt(rank_len * panel_count * 2 ** (tree_level + 1))
        for tree_level in range(level_count)
    ]
    return jnp.array(gain_list, jnp.float32)


def far_field(field_low, far_basis):
    coeffs = jnp.einsum("xp,lpr->lxr", field_low, far_basis, preferred_element_type=jnp.float32)
    summed = tree_totals(coeffs)
    gains = level_gains(field_low.shape[1], far_basis.shape[0], far_basis.shape[2])
    scaled = (summed * gains[:, None, None]).astype(jnp.bfloat16)
    return jnp.einsum("lxr,lpr->xp", scaled, far_basis, preferred_element_type=jnp.float32)


def apply_operator(field, near_kernel, neighbours, far_basis):
    field_low = field.astype(jnp.bfloat16)
    return near_field(field_low, near_kernel, neighbours) + far_field(field_low, far_basis)


def project_cone(trial_point, mu_sorted):
    normal = trial_point[0]
    slide_a = trial_point[1]
    slide_b = trial_point[2]
    slip = jnp.sqrt(slide_a * slide_a + slide_b * slide_b + SLIP_EPS)
    coeff = mu_sorted[None, :]
    stick = slip <= coeff * normal
    pressed = jnp.where(
        stick, normal, jnp.maximum((normal + coeff * slip) / (1.0 + coeff * coeff), 0.0)
    )
    factor = jnp.where(stick, jnp.ones_like(slip), coeff * pressed / slip)
    return jnp.stack([pressed, factor * slide_a, factor * slide_b])


def body(
    traction,
    near_kernel,
    neighbours,
    far_basis,
    surface_gap,
    friction,
    contact_flags,
    cluster_order,
    approach,
):
    comp_count, load_count, panel_count = traction.shape
    row_count = comp_count * load_count
    local_order = cluster_order % panel_count
    gap_sorted = jnp.take(surface_gap, local_order, axis=1)
    mu_sorted = jnp.take(friction, local_order)
    live_mask = jnp.take(contact_flags, local_order).astype(jnp.float32)
    target = (approach[:, :, None] - gap_sorted[:, None, :]).reshape(row_count, panel_count)
    state_rows = traction.reshape(row_count, panel_count)
    residual = apply_operator(state_rows, near_kernel, neighbours, far_basis) - target
    image_rows = apply_operator(residual, near_kernel, neighbours, far_basis)
    residual_out = residual.reshape(comp_count, load_count, panel_count)
    image_out = image_rows.reshape(comp_count, load_count, panel_count)
    cross_local = jnp.sum(residual_out * image_out, axis=(0, 2))
    square_local = jnp.sum(image_out * image_out, axis=(0, 2))
    cross_sum, square_sum = (
        over_axes(cross_local, WIDE_NARROW),
        over_axes(square_local, WIDE_NARROW),
    )
    entries = comp_count * panel_count * lax.axis_size(WIDE_NARROW)
    step_size = cross_sum / entries / (square_sum / entries + 1e-06)
    trial_point = traction - step_size[None, :, None] * residual_out
    updated = project_cone(trial_point, mu_sorted) * live_mask[None, None, :]
    return (updated, residual_out, step_size)


def solution(mesh):
    finer = Mesh(mesh.devices.reshape(8, 2, 4, 4), ("wide_0", "wide_1", "narrow_0", "narrow_1"))
    placed = (
        P(None, None, WIDE_NARROW),
        P(WIDE_NARROW, None, None, None),
        P(WIDE_NARROW, None),
        P(None, WIDE_NARROW, None),
        P(None, WIDE_NARROW),
        P(WIDE_NARROW),
        P(WIDE_NARROW),
        P(WIDE_NARROW),
        P(),
    )
    return jax.shard_map(
        body,
        mesh=finer,
        in_specs=placed,
        out_specs=(P(None, None, WIDE_NARROW), P(None, None, WIDE_NARROW), P()),
        check_vma=False,
    )
```

profile of v0, /device:TPU:1, one launch (start us, length us, event | category | flops | bytes accessed | tf_op | source)
XLA Modules:
  0.0 305.8 jit_solution(11607132606364421142)
XLA Ops:
  0.6 2.3 convert_element_type.20
  2.9 1.8 convolution_bitcast_fusion.4
  4.8 2.2 collective-permute-start.2
  7.0 16.0 %collective-permute-done.2 = f32[8,192,128]{2,1,0:T(8,128)S(1)} collective-permute-done((f32[8,192,128]{2,1,0:T(8,128)S(1)}, f32[8,192,128]{2,1,0:T(8,128)S(1)}, u32[]{:S(2)}, u32[]{:S(2)}) %collective-permute-start.2) | collective-permute-done | bytes 786464 | tf_op jit(solution)/shard_map/ppermute | solution.py:45
  24.9 4.0 %collective-permute-start.3 = (f32[7,192,128]{2,1,0:T(8,128)}, f32[7,192,128]{2,1,0:T(8,128)}, u32[]{:S(2)}, u32[]{:S(2)}) collective-permute-start(f32[7,192,128]{2,1,0:T(8,128)} %slice.154), channel_id=1, source_target_pairs={{0,2},{2,0},{1,3},{3,1},{4,6},{6,4},{5,7},{7,5},{8,10},{10,8},{9,1... | collective-permute-start | bytes 2064392 | tf_op jit(solution)/shard_map/ppermute | solution.py:45
  29.0 6.6 %collective-permute-start.1 = (bf16[192,1536]{1,0:T(8,128)(2,1)}, bf16[192,1536]{1,0:T(8,128)(2,1)}, u32[]{:S(2)}, u32[]{:S(2)}) collective-permute-start(bf16[192,1536]{1,0:T(8,128)(2,1)} %bitcast), channel_id=1, source_target_pairs={{1,0},{2,1},{3,2},{4,3},{5,4},{6,5},{7,6},{8,7},{9,8},{10,9},{11,1... | collective-permute-start | bytes 1769480 | tf_op jit(solution)/shard_map/ppermute | solution.py:27
  35.5 1.9 collective-permute-start
  38.7 4.8 %gather_fusion = f32[1536,3]{1,0:T(8,128)} fusion(f32[3,1536]{0,1:T(8,128)} %copy.40, s32[2048]{0:T(1024)S(1)} %pad_clamp_fusion), kind=kCustom, calls=%fused_computation.2 | custom fusion | bytes 43008 | tf_op jit(solution)/shard_map/jit(_take)/gather | solution.py:124
  43.5 8.4 %gather_fusion.2 = s32[1536]{0:T(1024)S(1)} fusion(s32[1536]{0:T(1024)S(1)} %copy-done.1, s32[2048]{0:T(1024)S(1)} %pad_clamp_fusion), kind=kCustom, calls=%fused_computation.4 | custom fusion | bytes 18432 | tf_op jit(solution)/shard_map/jit(_take)/gather | solution.py:126
  59.2 11.3 %collective-permute-done.4 = f32[6,192,128]{2,1,0:T(8,128)} collective-permute-done((f32[6,192,128]{2,1,0:T(8,128)}, f32[6,192,128]{2,1,0:T(8,128)}, u32[]{:S(2)}, u32[]{:S(2)}) %collective-permute-start.4) | collective-permute-done | bytes 589856 | tf_op jit(solution)/shard_map/ppermute | solution.py:45
  73.1 12.3 %collective-permute-done.5 = f32[5,192,128]{2,1,0:T(8,128)S(1)} collective-permute-done((f32[5,192,128]{2,1,0:T(8,128)S(1)}, f32[5,192,128]{2,1,0:T(8,128)S(1)}, u32[]{:S(2)}, u32[]{:S(2)}) %collective-permute-start.5) | collective-permute-done | bytes 491552 | tf_op jit(solution)/shard_map/ppermute | solution.py:45
  88.1 2.8 pad_maximum_fusion
  90.9 4.0 %copy.37 = bf16[192,4608]{0,1:T(8,128)(2,1)} copy(bf16[192,4608]{1,0:T(8,128)(2,1)} %pad_maximum_fusion) | data formatting | bytes 3538944 | tf_op jit(solution)/shard_map/concatenate | solution.py:33
  94.9 4.0 %copy.38 = bf16[192,9,512]{2,0,1:T(8,128)(2,1)} copy(bf16[192,9,512]{0,2,1:T(8,128)(2,1)} %bitcast.60) | data formatting | bytes 3538944 | tf_op jit(solution)/shard_map/reshape | solution.py:57
  98.9 3.8 %gather_fusion.3 = bf16[12,192,512]{2,1,0:T(8,128)(2,1)} fusion(bf16[192,9,512]{2,0,1:T(8,128)(2,1)} %copy.38, s32[1024]{0:T(1024)} %pad_clamp_fusion.1), kind=kCustom, calls=%fused_computation.clone | custom fusion | bytes 4718640 | tf_op jit(solution)/shard_map/jit(_take)/gather | solution.py:60
  102.7 2.0 broadcast_select_fusion.1
  105.8 1.9 collective-permute-start.7
  107.7 5.0 %convolution_bitcast_fusion.3 = f32[3,24,8,512]{3,2,1,0:T(8,128)S(1)} fusion(bf16[192,3,4,512]{3,0,2,1:T(8,128)(2,1)S(1)} %bitcast.59, bf16[3,4,512,512]{3,2,1,0:T(8,128)(2,1)} %param.14), kind=kOutput, calls=%fused_computation.15 | convolution fusion | flops 1207959552 | bytes 9830400 | tf_op jit(solution)/shard_map/bkij,xbkj->xbi/dot_general | solution.py:62
  112.7 2.3 collective-permute-done.7
  115.1 2.9 collective-permute-start.8
  118.1 8.7 %collective-permute-done.8 = f32[2,192,128]{2,1,0:T(8,128)S(1)} collective-permute-done((f32[2,192,128]{2,1,0:T(8,128)S(1)}, f32[2,192,128]{2,1,0:T(8,128)S(1)}, u32[]{:S(2)}, u32[]{:S(2)}) %collective-permute-start.8) | collective-permute-done | bytes 196640 | tf_op jit(solution)/shard_map/ppermute | solution.py:45
  126.8 6.4 %collective-permute-start.9 = (f32[1,192,128]{2,1,0:T(8,128)S(1)}, f32[1,192,128]{2,1,0:T(8,128)S(1)}, u32[]{:S(2)}, u32[]{:S(2)}) collective-permute-start(f32[1,192,128]{2,1,0:T(8,128)S(1)} %slice.160), channel_id=1, source_target_pairs={{0,128},{128,0},{1,129},{129,1},{2,130},{130,2},{3,131},{131,3},{4... | collective-permute-start | bytes 294920 | tf_op jit(solution)/shard_map/ppermute | solution.py:45
  133.3 2.0 collective-permute-done.9
  135.3 2.4 fusion.12
  139.7 17.2 %collective-permute-done.12 = f32[8,192,128]{2,1,0:T(8,128)S(1)} collective-permute-done((f32[8,192,128]{2,1,0:T(8,128)S(1)}, f32[8,192,128]{2,1,0:T(8,128)S(1)}, u32[]{:S(2)}, u32[]{:S(2)}) %collective-permute-start.12) | collective-permute-done | bytes 786464 | tf_op jit(solution)/shard_map/ppermute | solution.py:45
  157.5 15.5 %collective-permute-done.13 = f32[7,192,128]{2,1,0:T(8,128)S(1)} collective-permute-done((f32[7,192,128]{2,1,0:T(8,128)S(1)}, f32[7,192,128]{2,1,0:T(8,128)S(1)}, u32[]{:S(2)}, u32[]{:S(2)}) %collective-permute-start.13) | collective-permute-done | bytes 688160 | tf_op jit(solution)/shard_map/ppermute | solution.py:45
  173.2 11.1 %collective-permute-done.14 = f32[6,192,128]{2,1,0:T(8,128)S(1)} collective-permute-done((f32[6,192,128]{2,1,0:T(8,128)S(1)}, f32[6,192,128]{2,1,0:T(8,128)S(1)}, u32[]{:S(2)}, u32[]{:S(2)}) %collective-permute-start.14) | collective-permute-done | bytes 589856 | tf_op jit(solution)/shard_map/ppermute | solution.py:45
  185.3 3.8 %collective-permute-start.15 = (f32[5,192,128]{2,1,0:T(8,128)}, f32[5,192,128]{2,1,0:T(8,128)}, u32[]{:S(2)}, u32[]{:S(2)}) collective-permute-start(f32[5,192,128]{2,1,0:T(8,128)} %slice.164), channel_id=1, source_target_pairs={{0,8},{8,0},{1,9},{9,1},{2,10},{10,2},{3,11},{11,3},{4,12},{12,4},... | collective-permute-start | bytes 1474568 | tf_op jit(solution)/shard_map/ppermute | solution.py:45
  189.1 8.3 %collective-permute-start.11 = (bf16[192,1536]{1,0:T(8,128)(2,1)}, bf16[192,1536]{1,0:T(8,128)(2,1)}, u32[]{:S(2)}, u32[]{:S(2)}) collective-permute-start(bf16[192,1536]{1,0:T(8,128)(2,1)} %get-tuple-element.21), channel_id=1, source_target_pairs={{1,0},{2,1},{3,2},{4,3},{5,4},{6,5},{7,6},{8,7},{9,8},{10,9},{11,1... | collective-permute-start | bytes 1769480 | tf_op jit(solution)/shard_map/ppermute | solution.py:27
  197.4 1.9 collective-permute-start.10
  199.3 8.4 %gather_fusion.1 = f32[1536]{0:T(1024)S(1)} fusion(f32[1536]{0:T(1024)S(1)} %copy-done.2, s32[2048]{0:T(1024)S(1)} %pad_clamp_fusion), kind=kCustom, calls=%fused_computation.3 | custom fusion | bytes 18432 | tf_op jit(solution)/shard_map/jit(_take)/gather | solution.py:125
  210.6 3.0 collective-permute-done.11
  213.5 2.8 pad_maximum_fusion.1
  216.3 4.0 %copy.42 = bf16[192,4608]{0,1:T(8,128)(2,1)} copy(bf16[192,4608]{1,0:T(8,128)(2,1)} %pad_maximum_fusion.1) | data formatting | bytes 3538944 | tf_op jit(solution)/shard_map/concatenate | solution.py:33
  220.3 4.0 %copy.43 = bf16[192,9,512]{2,0,1:T(8,128)(2,1)} copy(bf16[192,9,512]{0,2,1:T(8,128)(2,1)} %bitcast.61) | data formatting | bytes 3538944 | tf_op jit(solution)/shard_map/reshape | solution.py:57
  224.3 3.8 %gather_fusion.4 = bf16[12,192,512]{2,1,0:T(8,128)(2,1)} fusion(bf16[192,9,512]{2,0,1:T(8,128)(2,1)} %copy.43, s32[1024]{0:T(1024)} %pad_clamp_fusion.1), kind=kCustom, calls=%fused_computation.1.clone | custom fusion | bytes 4718640 | tf_op jit(solution)/shard_map/jit(_take)/gather | solution.py:60
  228.1 2.0 broadcast_select_fusion
  231.2 5.4 %collective-permute-start.17 = (f32[3,192,128]{2,1,0:T(8,128)S(1)}, f32[3,192,128]{2,1,0:T(8,128)S(1)}, u32[]{:S(2)}, u32[]{:S(2)}) collective-permute-start(f32[3,192,128]{2,1,0:T(8,128)S(1)} %slice.166), channel_id=1, source_target_pairs={{0,32},{32,0},{1,33},{33,1},{2,34},{34,2},{3,35},{35,3},{4,36},{36... | collective-permute-start | bytes 884744 | tf_op jit(solution)/shard_map/ppermute | solution.py:45
  236.6 5.0 %convolution_bitcast_fusion.2 = f32[3,24,8,512]{3,2,1,0:T(8,128)S(1)} fusion(bf16[192,3,4,512]{3,0,2,1:T(8,128)(2,1)S(1)} %bitcast.58, bf16[3,4,512,512]{3,2,1,0:T(8,128)(2,1)} %param.14), kind=kOutput, calls=%fused_computation.14 | convolution fusion | flops 1207959552 | bytes 9830400 | tf_op jit(solution)/shard_map/bkij,xbkj->xbi/dot_general | solution.py:62
  241.8 7.0 %collective-permute-start.18 = (f32[2,192,128]{2,1,0:T(8,128)S(1)}, f32[2,192,128]{2,1,0:T(8,128)S(1)}, u32[]{:S(2)}, u32[]{:S(2)}) collective-permute-start(f32[2,192,128]{2,1,0:T(8,128)S(1)} %slice.167), channel_id=1, source_target_pairs={{0,64},{64,0},{1,65},{65,1},{2,66},{66,2},{3,67},{67,3},{4,68},{68... | collective-permute-start | bytes 589832 | tf_op jit(solution)/shard_map/ppermute | solution.py:45
  248.9 4.9 %collective-permute-done.18 = f32[2,192,128]{2,1,0:T(8,128)S(1)} collective-permute-done((f32[2,192,128]{2,1,0:T(8,128)S(1)}, f32[2,192,128]{2,1,0:T(8,128)S(1)}, u32[]{:S(2)}, u32[]{:S(2)}) %collective-permute-start.18) | collective-permute-done | bytes 196640 | tf_op jit(solution)/shard_map/ppermute | solution.py:45
  253.8 3.8 %collective-permute-start.19 = (f32[1,192,128]{2,1,0:T(8,128)S(1)}, f32[1,192,128]{2,1,0:T(8,128)S(1)}, u32[]{:S(2)}, u32[]{:S(2)}) collective-permute-start(f32[1,192,128]{2,1,0:T(8,128)S(1)} %slice.168), channel_id=1, source_target_pairs={{0,128},{128,0},{1,129},{129,1},{2,130},{130,2},{3,131},{131,3},{4... | collective-permute-start | bytes 294920 | tf_op jit(solution)/shard_map/ppermute | solution.py:45
  257.7 3.6 %collective-permute-done.19 = f32[1,192,128]{2,1,0:T(8,128)S(1)} collective-permute-done((f32[1,192,128]{2,1,0:T(8,128)S(1)}, f32[1,192,128]{2,1,0:T(8,128)S(1)}, u32[]{:S(2)}, u32[]{:S(2)}) %collective-permute-start.19) | collective-permute-done | bytes 98336 | tf_op jit(solution)/shard_map/ppermute | solution.py:45
  262.9 15.7 %all-reduce = (f32[64]{0:T(128)S(1)}, f32[64]{0:T(128)S(1)}) all-reduce(f32[64]{0:T(128)S(1)} %reduce_sum.37, f32[64]{0:T(128)S(1)} %reduce_sum.25), channel_id=1, replica_groups=mesh['wide_0'=8,'wide_1'=2,'narrow_0'=4,'narrow_1'=4] {'wide_0'}, use_global_device_ids=true, to_apply=%region_8.10 | all-reduce | flops 128 | bytes 1024 | tf_op jit(solution)/shard_map/psum | solution.py:49
  278.6 2.5 all-reduce.3
  281.1 14.1 %all-reduce.2 = (f32[64]{0:T(128)S(1)}, f32[64]{0:T(128)S(1)}) all-reduce(f32[64]{0:T(128)S(1)} %get-tuple-element.12, f32[64]{0:T(128)S(1)} %get-tuple-element.13), channel_id=1, replica_groups=mesh['wide_0'=8,'wide_1'=2,'narrow_0'=4,'narrow_1'=4] {'narrow_0'}, use_global_device_ids=true, to_apply=%region_10.12 | all-reduce | flops 128 | bytes 1024 | tf_op jit(solution)/shard_map/psum | solution.py:49
  295.2 7.1 %all-reduce.1 = (f32[64]{0:T(128)S(1)}, f32[64]{0:T(128)S(1)}) all-reduce(f32[64]{0:T(128)S(1)} %get-tuple-element.10, f32[64]{0:T(128)S(1)} %get-tuple-element.11), channel_id=1, replica_groups=mesh['wide_0'=8,'wide_1'=2,'narrow_0'=4,'narrow_1'=4] {'narrow_1'}, use_global_device_ids=true, to_apply=%region_11.13 | all-reduce | flops 128 | bytes 1024 | tf_op jit(solution)/shard_map/psum | solution.py:49
  302.4 1.9 multiply_subtract_fusion
  (142 shorter events, 28.0 us)
Async XLA Ops:
  0.6 2.3 copy-start
  4.8 32.7 %copy-start.22 = (f32[3,1536]{1,0:T(4,128)S(1)}, f32[3,1536]{1,0:T(4,128)}, u32[]{:S(2)}) copy-start(f32[3,1536]{1,0:T(4,128)} %param.17) | copy-start | bytes 55300
  4.8 33.9 %copy-start.21 = (s32[1536]{0:T(1024)S(1)}, s32[1536]{0:T(1024)}, u32[]{:S(2)}) copy-start(s32[1536]{0:T(1024)} %param.20) | copy-start | bytes 18436
  4.8 18.2 %collective-permute-start.2 = (f32[8,192,128]{2,1,0:T(8,128)S(1)}, f32[8,192,128]{2,1,0:T(8,128)S(1)}, u32[]{:S(2)}, u32[]{:S(2)}) collective-permute-start(f32[8,192,128]{2,1,0:T(8,128)S(1)} %convolution_bitcast_fusion.4), channel_id=1, source_target_pairs={{0,1},{1,0},{2,3},{3,2},{4,5},{5,4},{6,7},{7,6},{8,9},{9,8},{10,11... | collective-permute-start | bytes 2359304 | tf_op jit(solution)/shard_map/ppermute | solution.py:45
  24.0 19.5 %copy-start.1 = (s32[1536]{0:T(1024)S(1)}, s32[1536]{0:T(1024)}, u32[]{:S(2)}) copy-start(s32[1536]{0:T(1024)} %param.19) | copy-start | bytes 18436
  24.9 27.0 %collective-permute-start.3 = (f32[7,192,128]{2,1,0:T(8,128)}, f32[7,192,128]{2,1,0:T(8,128)}, u32[]{:S(2)}, u32[]{:S(2)}) collective-permute-start(f32[7,192,128]{2,1,0:T(8,128)} %slice.154), channel_id=1, source_target_pairs={{0,2},{2,0},{1,3},{3,1},{4,6},{6,4},{5,7},{7,5},{8,10},{10,8},{9,1... | collective-permute-start | bytes 2064392 | tf_op jit(solution)/shard_map/ppermute | solution.py:45
  29.0 59.1 %collective-permute-start.1 = (bf16[192,1536]{1,0:T(8,128)(2,1)}, bf16[192,1536]{1,0:T(8,128)(2,1)}, u32[]{:S(2)}, u32[]{:S(2)}) collective-permute-start(bf16[192,1536]{1,0:T(8,128)(2,1)} %bitcast), channel_id=1, source_target_pairs={{1,0},{2,1},{3,2},{4,3},{5,4},{6,5},{7,6},{8,7},{9,8},{10,9},{11,1... | collective-permute-start | bytes 1769480 | tf_op jit(solution)/shard_map/ppermute | solution.py:27
  35.5 52.5 %collective-permute-start = (bf16[192,1536]{1,0:T(8,128)(2,1)}, bf16[192,1536]{1,0:T(8,128)(2,1)}, u32[]{:S(2)}, u32[]{:S(2)}) collective-permute-start(bf16[192,1536]{1,0:T(8,128)(2,1)} %bitcast), channel_id=1, source_target_pairs={{0,1},{1,2},{2,3},{3,4},{4,5},{5,6},{6,7},{7,8},{8,9},{9,10},{10,1... | collective-permute-start | bytes 1769480 | tf_op jit(solution)/shard_map/ppermute | solution.py:26
  51.9 3.3 %copy-start.19 = (f32[1536,3]{1,0:T(8,128)S(1)}, f32[1536,3]{1,0:T(8,128)}, u32[]{:S(2)}) copy-start(f32[1536,3]{1,0:T(8,128)} %gather_fusion) | copy-start | bytes 55300
  51.9 4.4 %copy-start.23 = (pred[1536]{0:T(1024)(128)(4,1)}, pred[1536]{0:T(1024)(128)(4,1)S(1)}, u32[]{:S(2)}) copy-start(pred[1536]{0:T(1024)(128)(4,1)S(1)} %get-tuple-element.15) | copy-start | bytes 4612
  54.3 3.4 %copy-start.28 = (f32[3,64]{1,0:T(4,128)S(1)}, f32[3,64]{1,0:T(4,128)}, u32[]{:S(2)}) copy-start(f32[3,64]{1,0:T(4,128)} %param.21) | copy-start | bytes 2308
  54.3 3.5 %copy-start.25 = (s32[3,4]{1,0:T(4,128)S(1)}, s32[3,4]{1,0:T(4,128)}, u32[]{:S(2)}) copy-start(s32[3,4]{1,0:T(4,128)} %param.15) | copy-start | bytes 148
  55.2 15.4 %collective-permute-start.4 = (f32[6,192,128]{2,1,0:T(8,128)}, f32[6,192,128]{2,1,0:T(8,128)}, u32[]{:S(2)}, u32[]{:S(2)}) collective-permute-start(f32[6,192,128]{2,1,0:T(8,128)} %slice.155), channel_id=1, source_target_pairs={{0,4},{4,0},{1,5},{5,1},{2,6},{6,2},{3,7},{7,3},{8,12},{12,8},{9,1... | collective-permute-start | bytes 1769480 | tf_op jit(solution)/shard_map/ppermute | solution.py:45
  71.8 13.6 %copy-start.10 = (f32[6,192,128]{2,1,0:T(8,128)}, f32[6,192,128]{2,1,0:T(8,128)S(1)}, u32[]{:S(2)}) copy-start(f32[6,192,128]{2,1,0:T(8,128)S(1)} %slice_add_fusion.11) | copy-start | bytes 1769476
  71.9 13.6 %collective-permute-start.5 = (f32[5,192,128]{2,1,0:T(8,128)S(1)}, f32[5,192,128]{2,1,0:T(8,128)S(1)}, u32[]{:S(2)}, u32[]{:S(2)}) collective-permute-start(f32[5,192,128]{2,1,0:T(8,128)S(1)} %slice.156), channel_id=1, source_target_pairs={{0,8},{8,0},{1,9},{9,1},{2,10},{10,2},{3,11},{11,3},{4,12},{12,4},... | collective-permute-start | bytes 1474568 | tf_op jit(solution)/shard_map/ppermute | solution.py:45
  86.4 18.3 %collective-permute-start.6 = (f32[4,192,128]{2,1,0:T(8,128)S(1)}, f32[4,192,128]{2,1,0:T(8,128)}, u32[]{:S(2)}, u32[]{:S(2)}) collective-permute-start(f32[4,192,128]{2,1,0:T(8,128)S(1)} %slice.157), channel_id=1, source_target_pairs={{0,16},{16,0},{1,17},{17,1},{2,18},{18,2},{3,19},{19,3},{4,20},{20... | collective-permute-start | bytes 1179656 | tf_op jit(solution)/shard_map/ppermute | solution.py:45
  102.7 2.0 copy-start.17
  105.8 9.2 %collective-permute-start.7 = (f32[3,192,128]{2,1,0:T(8,128)S(1)}, f32[3,192,128]{2,1,0:T(8,128)S(1)}, u32[]{:S(2)}, u32[]{:S(2)}) collective-permute-start(f32[3,192,128]{2,1,0:T(8,128)S(1)} %slice.158), channel_id=1, source_target_pairs={{0,32},{32,0},{1,33},{33,1},{2,34},{34,2},{3,35},{35,3},{4,36},{36... | collective-permute-start | bytes 884744 | tf_op jit(solution)/shard_map/ppermute | solution.py:45
  112.6 5.4 %copy-start.5 = (f32[7,192,128]{2,1,0:T(8,128)S(1)}, f32[7,192,128]{2,1,0:T(8,128)}, u32[]{:S(2)}) copy-start(f32[7,192,128]{2,1,0:T(8,128)} %copy-done.4) | copy-start | bytes 2064388
  112.6 5.4 %copy-start.11 = (f32[6,192,128]{2,1,0:T(8,128)S(1)}, f32[6,192,128]{2,1,0:T(8,128)}, u32[]{:S(2)}) copy-start(f32[6,192,128]{2,1,0:T(8,128)} %copy-done.10) | copy-start | bytes 1769476
  112.6 5.4 %slice-start = ((f32[8,192,128]{2,1,0:T(8,128)}), f32[1,192,128]{2,1,0:T(8,128)S(1)}, s32[]{:S(2)}) async-start(f32[8,192,128]{2,1,0:T(8,128)} %copy-done.12), calls=%async_computation | async-start | bytes 196608 | tf_op jit(solution)/shard_map/slice | solution.py:71
  115.1 11.7 %collective-permute-start.8 = (f32[2,192,128]{2,1,0:T(8,128)S(1)}, f32[2,192,128]{2,1,0:T(8,128)S(1)}, u32[]{:S(2)}, u32[]{:S(2)}) collective-permute-start(f32[2,192,128]{2,1,0:T(8,128)S(1)} %slice.159), channel_id=1, source_target_pairs={{0,64},{64,0},{1,65},{65,1},{2,66},{66,2},{3,67},{67,3},{4,68},{68... | collective-permute-start | bytes 589832 | tf_op jit(solution)/shard_map/ppermute | solution.py:45
  118.1 17.2 %copy-start.18 = (f32[192,1536]{1,0:T(8,128)S(1)}, f32[192,1536]{1,0:T(8,128)}, u32[]{:S(2)}) copy-start(f32[192,1536]{1,0:T(8,128)} %bitcast_subtract_fusion) | copy-start | bytes 3538948
  118.1 17.2 %copy-start.26 = (f32[8]{0:T(128)S(1)}, f32[8]{0:T(128)}, u32[]{:S(2)}) copy-start(f32[8]{0:T(128)} %constant.80.clone) | copy-start | bytes 100
  126.8 8.4 %collective-permute-start.9 = (f32[1,192,128]{2,1,0:T(8,128)S(1)}, f32[1,192,128]{2,1,0:T(8,128)S(1)}, u32[]{:S(2)}, u32[]{:S(2)}) collective-permute-start(f32[1,192,128]{2,1,0:T(8,128)S(1)} %slice.160), channel_id=1, source_target_pairs={{0,128},{128,0},{1,129},{129,1},{2,130},{130,2},{3,131},{131,3},{4... | collective-permute-start | bytes 294920 | tf_op jit(solution)/shard_map/ppermute | solution.py:45
  139.6 17.3 %collective-permute-start.12 = (f32[8,192,128]{2,1,0:T(8,128)S(1)}, f32[8,192,128]{2,1,0:T(8,128)S(1)}, u32[]{:S(2)}, u32[]{:S(2)}) collective-permute-start(f32[8,192,128]{2,1,0:T(8,128)S(1)} %convolution_bitcast_fusion.5), channel_id=1, source_target_pairs={{0,1},{1,0},{2,3},{3,2},{4,5},{5,4},{6,7},{7,6},{8,9},{9,8},{10,11... | collective-permute-start | bytes 2359304 | tf_op jit(solution)/shard_map/ppermute | solution.py:45
  156.9 16.2 %copy-start.13 = (f32[8,192,128]{2,1,0:T(8,128)}, f32[8,192,128]{2,1,0:T(8,128)S(1)}, u32[]{:S(2)}) copy-start(f32[8,192,128]{2,1,0:T(8,128)S(1)} %add.159) | copy-start | bytes 2359300
  157.0 15.9 %collective-permute-start.13 = (f32[7,192,128]{2,1,0:T(8,128)S(1)}, f32[7,192,128]{2,1,0:T(8,128)S(1)}, u32[]{:S(2)}, u32[]{:S(2)}) collective-permute-start(f32[7,192,128]{2,1,0:T(8,128)S(1)} %slice.162), channel_id=1, source_target_pairs={{0,2},{2,0},{1,3},{3,1},{4,6},{6,4},{5,7},{7,5},{8,10},{10,8},{9,1... | collective-permute-start | bytes 2064392 | tf_op jit(solution)/shard_map/ppermute | solution.py:45
  173.0 12.3 %copy-start.6 = (f32[7,192,128]{2,1,0:T(8,128)}, f32[7,192,128]{2,1,0:T(8,128)S(1)}, u32[]{:S(2)}) copy-start(f32[7,192,128]{2,1,0:T(8,128)S(1)} %slice_add_fusion.12) | copy-start | bytes 2064388
  173.0 26.3 %copy-start.2 = (f32[1536]{0:T(1024)S(1)}, f32[1536]{0:T(1024)}, u32[]{:S(2)}) copy-start(f32[1536]{0:T(1024)} %param.18) | copy-start | bytes 18436
  173.1 11.2 %collective-permute-start.14 = (f32[6,192,128]{2,1,0:T(8,128)S(1)}, f32[6,192,128]{2,1,0:T(8,128)S(1)}, u32[]{:S(2)}, u32[]{:S(2)}) collective-permute-start(f32[6,192,128]{2,1,0:T(8,128)S(1)} %slice.163), channel_id=1, source_target_pairs={{0,4},{4,0},{1,5},{5,1},{2,6},{6,2},{3,7},{7,3},{8,12},{12,8},{9,1... | collective-permute-start | bytes 1769480 | tf_op jit(solution)/shard_map/ppermute | solution.py:45
  184.4 4.7 %copy-start.8 = (f32[6,192,128]{2,1,0:T(8,128)}, f32[6,192,128]{2,1,0:T(8,128)S(1)}, u32[]{:S(2)}) copy-start(f32[6,192,128]{2,1,0:T(8,128)S(1)} %slice_add_fusion.10) | copy-start | bytes 1769476
  185.3 22.5 %copy-start.24 = (pred[1536]{0:T(1024)(128)(4,1)S(1)}, pred[1536]{0:T(1024)(128)(4,1)}, u32[]{:S(2)}) copy-start(pred[1536]{0:T(1024)(128)(4,1)} %copy-done.23) | copy-start | bytes 4612
  185.3 23.1 %collective-permute-start.15 = (f32[5,192,128]{2,1,0:T(8,128)}, f32[5,192,128]{2,1,0:T(8,128)}, u32[]{:S(2)}, u32[]{:S(2)}) collective-permute-start(f32[5,192,128]{2,1,0:T(8,128)} %slice.164), channel_id=1, source_target_pairs={{0,8},{8,0},{1,9},{9,1},{2,10},{10,2},{3,11},{11,3},{4,12},{12,4},... | collective-permute-start | bytes 1474568 | tf_op jit(solution)/shard_map/ppermute | solution.py:45
  189.1 24.4 %collective-permute-start.11 = (bf16[192,1536]{1,0:T(8,128)(2,1)}, bf16[192,1536]{1,0:T(8,128)(2,1)}, u32[]{:S(2)}, u32[]{:S(2)}) collective-permute-start(bf16[192,1536]{1,0:T(8,128)(2,1)} %get-tuple-element.21), channel_id=1, source_target_pairs={{1,0},{2,1},{3,2},{4,3},{5,4},{6,5},{7,6},{8,7},{9,8},{10,9},{11,1... | collective-permute-start | bytes 1769480 | tf_op jit(solution)/shard_map/ppermute | solution.py:27
  197.4 16.1 %collective-permute-start.10 = (bf16[192,1536]{1,0:T(8,128)(2,1)}, bf16[192,1536]{1,0:T(8,128)(2,1)}, u32[]{:S(2)}, u32[]{:S(2)}) collective-permute-start(bf16[192,1536]{1,0:T(8,128)(2,1)} %get-tuple-element.21), channel_id=1, source_target_pairs={{0,1},{1,2},{2,3},{3,4},{4,5},{5,6},{6,7},{7,8},{8,9},{9,10},{10,1... | collective-permute-start | bytes 1769480 | tf_op jit(solution)/shard_map/ppermute | solution.py:26
  210.4 19.7 %collective-permute-start.16 = (f32[4,192,128]{2,1,0:T(8,128)S(1)}, f32[4,192,128]{2,1,0:T(8,128)}, u32[]{:S(2)}, u32[]{:S(2)}) collective-permute-start(f32[4,192,128]{2,1,0:T(8,128)S(1)} %slice.165), channel_id=1, source_target_pairs={{0,16},{16,0},{1,17},{17,1},{2,18},{18,2},{3,19},{19,3},{4,20},{20... | collective-permute-start | bytes 1179656 | tf_op jit(solution)/shard_map/ppermute | solution.py:45
  228.1 2.0 copy-start.15
  231.2 10.5 %collective-permute-start.17 = (f32[3,192,128]{2,1,0:T(8,128)S(1)}, f32[3,192,128]{2,1,0:T(8,128)S(1)}, u32[]{:S(2)}, u32[]{:S(2)}) collective-permute-start(f32[3,192,128]{2,1,0:T(8,128)S(1)} %slice.166), channel_id=1, source_target_pairs={{0,32},{32,0},{1,33},{33,1},{2,34},{34,2},{3,35},{35,3},{4,36},{36... | collective-permute-start | bytes 884744 | tf_op jit(solution)/shard_map/ppermute | solution.py:45
  241.6 7.2 %copy-start.7 = (f32[7,192,128]{2,1,0:T(8,128)S(1)}, f32[7,192,128]{2,1,0:T(8,128)}, u32[]{:S(2)}) copy-start(f32[7,192,128]{2,1,0:T(8,128)} %copy-done.6) | copy-start | bytes 2064388
  241.6 7.2 %copy-start.9 = (f32[6,192,128]{2,1,0:T(8,128)S(1)}, f32[6,192,128]{2,1,0:T(8,128)}, u32[]{:S(2)}) copy-start(f32[6,192,128]{2,1,0:T(8,128)} %copy-done.8) | copy-start | bytes 1769476
  241.6 7.2 %slice-start.1 = ((f32[8,192,128]{2,1,0:T(8,128)}), f32[1,192,128]{2,1,0:T(8,128)S(1)}, s32[]{:S(2)}) async-start(f32[8,192,128]{2,1,0:T(8,128)} %copy-done.13), calls=%async_computation.1 | async-start | bytes 196608 | tf_op jit(solution)/shard_map/slice | solution.py:71
  241.8 12.0 %collective-permute-start.18 = (f32[2,192,128]{2,1,0:T(8,128)S(1)}, f32[2,192,128]{2,1,0:T(8,128)S(1)}, u32[]{:S(2)}, u32[]{:S(2)}) collective-permute-start(f32[2,192,128]{2,1,0:T(8,128)S(1)} %slice.167), channel_id=1, source_target_pairs={{0,64},{64,0},{1,65},{65,1},{2,66},{66,2},{3,67},{67,3},{4,68},{68... | collective-permute-start | bytes 589832 | tf_op jit(solution)/shard_map/ppermute | solution.py:45
  248.8 12.5 %copy-start.3 = (f32[192,1536]{1,0:T(8,128)S(1)}, f32[192,1536]{1,0:T(8,128)}, u32[]{:S(2)}) copy-start(f32[192,1536]{1,0:T(8,128)} %get-tuple-element.22) | copy-start | bytes 3538948
  248.8 12.5 %copy-start.27 = (f32[8]{0:T(128)S(1)}, f32[8]{0:T(128)}, u32[]{:S(2)}) copy-start(f32[8]{0:T(128)} %constant.80.clone) | copy-start | bytes 100
  253.8 7.5 %collective-permute-start.19 = (f32[1,192,128]{2,1,0:T(8,128)S(1)}, f32[1,192,128]{2,1,0:T(8,128)S(1)}, u32[]{:S(2)}, u32[]{:S(2)}) collective-permute-start(f32[1,192,128]{2,1,0:T(8,128)S(1)} %slice.168), channel_id=1, source_target_pairs={{0,128},{128,0},{1,129},{129,1},{2,130},{130,2},{3,131},{131,3},{4... | collective-permute-start | bytes 294920 | tf_op jit(solution)/shard_map/ppermute | solution.py:45
  302.4 1.9 copy-start.29
  302.4 1.9 copy-start.20
  (4 other events, 3.4 us)
where the time goes:
time: 310 us; the launch traced here: 306 us
  waiting for transfers between devices  108 us (35%)
  starting transfers between devices  58.8 us (19%)
  local copies, waits for them, and re-layouts  54.8 us (18%)
  blocking collectives  39.5 us (13%)
  other arithmetic  26.3 us (8%)
  matrix products  17.4 us (6%)
    ppermute x16, waiting for transfers between devices, from_partner(): return lax.ppermute(block, axis, route)  105 us
    ppermute x16, starting transfers between devices, from_partner(): return lax.ppermute(block, axis, route)  40.1 us
    psum x4, blocking collectives, over_axes(): return functools.reduce(lax.psum, axes, array)  39.5 us
    ppermute x2, starting transfers between devices, extended(): lax.ppermute(initial, axis, [(b, a) for a, b in up])  14.9 us
    dot_general x2, matrix products, near_field(): jnp.einsum('bkij,xbkj->xbi', near_kernel, picked, preferred_element_type=...  9.91 us
    gather x1, local copies, waits for them, and re-layouts, body(): mu_sorted = jnp.take(friction, local_order)  8.39 us
    gather x1, local copies, waits for them, and re-layouts, body(): live_mask = jnp.take(contact_flags, local_order).astype(jnp.float32)  8.38 us
    reshape x2, local copies, waits for them, and re-layouts, near_field(): blocks = padded.reshape(row_count, 3 * blk_dev, block_len)  8.08 us
  transfers between devices with their start and end apart: 20, of which 12 were waited for; matrix products, arithmetic and copies ran while one was open for 25% of the time, Pallas kernels for 0%

commit v1 on v0

v1 whole, which is shorter than its diff:
```python
import functools
import math

import jax
import jax.numpy as jnp
from jax import lax
from jax.experimental import pallas as pl
from jax.experimental.pallas import tpu as pltpu
from jax.sharding import Mesh
from jax.sharding import PartitionSpec as P

WIDE_NARROW = ("wide_0", "wide_1", "narrow_0", "narrow_1")
NARROW = ("narrow_0", "narrow_1")
WIDE = ("wide_0", "wide_1")

SLIP_EPS = 0.01
COMP = 3
LOADS = 64
ROWS = COMP * LOADS
PAN = 1536
BLK = 512
CHUNKS = PAN // BLK
LEVELS = 8
HALF = LEVELS // 2
RANK = 128
GROUP = 16
QUARTERS = 4
PART = ROWS // QUARTERS

F32 = jnp.float32
BF16 = jnp.bfloat16
NT = (((1,), (1,)), ((), ()))
LIMIT = 48 * 2**20


def gain(level):
    return 0.64 / math.sqrt(RANK * PAN * 2 ** (level + 1))


def call(kernel, name, **kw):
    return pl.pallas_call(
        kernel,
        name=name,
        compiler_params=pltpu.CompilerParams(vmem_limit_bytes=LIMIT),
        **kw,
    )


def whole(shape):
    return pl.BlockSpec(shape, lambda *_: (0,) * len(shape))


SCALARS = pl.BlockSpec(memory_space=pltpu.SMEM)
CHUNK = pl.BlockSpec((ROWS, BLK), lambda b: (0, b))
BASIS = pl.BlockSpec((LEVELS, BLK, RANK), lambda b: (0, b, 0))
PANEL_ROWS = pl.BlockSpec((8, BLK), lambda b: (0, b))
BLOCKWISE = pl.BlockSpec((1, ROWS, BLK), lambda b: (b, 0, 0))


def add_coefs(values, basis_ref, acc_ref, sent_ref):
    step = pl.program_id(0)

    @pl.when(step == 0)
    def _():
        acc_ref[...] = jnp.zeros_like(acc_ref)

    for level in range(HALF):
        pair = jnp.concatenate([basis_ref[level], basis_ref[HALF + level]], axis=1)
        acc_ref[level] += jnp.dot(values, pair, preferred_element_type=F32)

    @pl.when(step == CHUNKS - 1)
    def _():
        for level in range(HALF):
            for quarter in range(QUARTERS):
                rows = pl.ds(quarter * PART, PART)
                slot = level * QUARTERS + quarter
                sent_ref[slot, 0:PART, :] = acc_ref[level, rows, 0:RANK].astype(BF16)
                sent_ref[slot, PART : 2 * PART, :] = acc_ref[level, rows, RANK : 2 * RANK].astype(
                    BF16
                )


def coef_kernel(field_ref, basis_ref, low_ref, sent_ref, acc_ref):
    values = field_ref[...].astype(BF16)
    low_ref[0] = values
    add_coefs(values, basis_ref, acc_ref, sent_ref)


ACC = pltpu.VMEM((HALF, ROWS, 2 * RANK), F32)
SENT = jax.ShapeDtypeStruct((GROUP, 2 * PART, RANK), BF16)
BLOCKS = jax.ShapeDtypeStruct((CHUNKS, ROWS, BLK), BF16)
FIELD = jax.ShapeDtypeStruct((ROWS, PAN), F32)
SUMS = jax.ShapeDtypeStruct((1, 2 * LOADS), F32)


def first_coefs(field, far_basis):
    return call(
        coef_kernel,
        "first_coefs",
        grid=(CHUNKS,),
        in_specs=[CHUNK, BASIS],
        out_specs=[BLOCKWISE, whole(SENT.shape)],
        out_shape=[BLOCKS, SENT],
        scratch_shapes=[ACC],
    )(field, far_basis)


def lower_kernel(place_ref, got_ref, low_ref, up_ref):
    level = place_ref[0] // QUARTERS
    width = 1
    sums = [got_ref[k, 0:PART, :].astype(F32) for k in range(GROUP)]
    while width < GROUP:
        sums = [sums[2 * k] + sums[2 * k + 1] for k in range(len(sums) // 2)]
        width *= 2
        own_level = width.bit_length() - 2

        @pl.when(level == own_level)
        def _(sums=sums, width=width, own_level=own_level):
            for k in range(GROUP):
                low_ref[k] = (sums[k // width] * gain(own_level)).astype(BF16)

    total = got_ref[0, PART : 2 * PART, :].astype(F32)
    for k in range(1, GROUP):
        total += got_ref[k, PART : 2 * PART, :].astype(F32)
    for k in range(GROUP):
        up_ref[k] = total.astype(BF16)


def lower_sums(place, got):
    part = jax.ShapeDtypeStruct((GROUP, PART, RANK), BF16)
    return call(
        lower_kernel,
        "lower_sums",
        in_specs=[SCALARS, whole(SENT.shape)],
        out_specs=[whole(part.shape)] * 2,
        out_shape=[part] * 2,
        grid=(1,),
    )(place, got)


def upper_kernel(place_ref, got_ref, low_ref, sent_ref):
    level = place_ref[0] // QUARTERS
    shift = level + 1
    own = lax.shift_right_logical(place_ref[1], shift)
    total = jnp.zeros((PART, RANK), F32)
    for k in range(GROUP):
        same = (lax.shift_right_logical(jnp.int32(k), shift) == own).astype(F32)
        total += got_ref[k].astype(F32) * same
    scale = jnp.float32(gain(HALF))
    for other in range(1, HALF):
        scale = jnp.where(level == other, jnp.float32(gain(HALF + other)), scale)
    total = (total * scale).astype(BF16)
    for k in range(GROUP):
        sent_ref[k, 0:PART, :] = low_ref[k]
        sent_ref[k, PART : 2 * PART, :] = total


def upper_sums(place, got, low):
    return call(
        upper_kernel,
        "upper_sums",
        in_specs=[SCALARS, whole(got.shape), whole(low.shape)],
        out_specs=whole(SENT.shape),
        out_shape=SENT,
        grid=(1,),
    )(place, got, low)


def near_kernel_body(slots_ref, left_ref, own_ref, right_ref, kernel_ref, *rest):
    out_ref, ext_ref = rest[-2:]
    block = pl.program_id(0)

    @pl.when(block == 0)
    def _():
        ext_ref[0:CHUNKS] = left_ref[...]
        ext_ref[CHUNKS : 2 * CHUNKS] = own_ref[...]
        ext_ref[2 * CHUNKS : 3 * CHUNKS] = right_ref[...]

    total = jnp.zeros((ROWS, BLK), F32)
    for k in range(kernel_ref.shape[1]):
        slot = slots_ref[block, k] - slots_ref[block, 0] + block + CHUNKS
        total += lax.dot_general(ext_ref[slot], kernel_ref[0, k], NT, preferred_element_type=F32)
    if len(rest) == 2:
        out_ref[...] = total
        return
    approach_ref, gap_ref = rest[:2]
    for comp in range(COMP):
        rows = slice(comp * LOADS, (comp + 1) * LOADS)
        out_ref[rows, :] = total[rows] - (approach_ref[rows, :] - gap_ref[comp : comp + 1, :])


def near_field(neighbours, left, own, right, near_kernel, *target):
    specs = [whole((ROWS, 1)), PANEL_ROWS] if target else []
    return call(
        near_kernel_body,
        "near_field",
        grid=(CHUNKS,),
        in_specs=[SCALARS]
        + [whole(BLOCKS.shape)] * 3
        + [pl.BlockSpec((1,) + near_kernel.shape[1:], lambda b: (b, 0, 0, 0))]
        + specs,
        out_specs=CHUNK,
        out_shape=FIELD,
        scratch_shapes=[pltpu.VMEM((3 * CHUNKS, ROWS, BLK), BF16)],
    )(neighbours, left, own, right, near_kernel, *target)


def unpack(got_ref, coef_ref):
    for level in range(HALF):
        for quarter in range(QUARTERS):
            rows = pl.ds(quarter * PART, PART)
            slot = level * QUARTERS + quarter
            coef_ref[rows, level * RANK : (level + 1) * RANK] = got_ref[slot, 0:PART, :]
            coef_ref[rows, (HALF + level) * RANK : (HALF + level + 1) * RANK] = got_ref[
                slot, PART : 2 * PART, :
            ]


def far_field(coef_ref, basis_ref):
    basis = jnp.concatenate([basis_ref[level] for level in range(LEVELS)], axis=1)
    return lax.dot_general(coef_ref[...], basis, NT, preferred_element_type=F32)


COEFS = pltpu.VMEM((ROWS, LEVELS * RANK), BF16)


def residual_kernel(got_ref, near_ref, basis_ref, out_ref, low_ref, sent_ref, coef_ref, acc_ref):
    @pl.when(pl.program_id(0) == 0)
    def _():
        unpack(got_ref, coef_ref)

    residual = far_field(coef_ref, basis_ref) + near_ref[...]
    out_ref[...] = residual
    values = residual.astype(BF16)
    low_ref[0] = values
    add_coefs(values, basis_ref, acc_ref, sent_ref)


def residual_step(got, near, far_basis):
    return call(
        residual_kernel,
        "residual",
        grid=(CHUNKS,),
        in_specs=[whole(SENT.shape), CHUNK, BASIS],
        out_specs=[CHUNK, BLOCKWISE, whole(SENT.shape)],
        out_shape=[FIELD, BLOCKS, SENT],
        scratch_shapes=[COEFS, ACC],
    )(got, near, far_basis)


def product_kernel(got_ref, near_ref, residual_ref, basis_ref, sums_ref, coef_ref, acc_ref):
    step = pl.program_id(0)

    @pl.when(step == 0)
    def _():
        unpack(got_ref, coef_ref)
        acc_ref[...] = jnp.zeros_like(acc_ref)

    image = far_field(coef_ref, basis_ref) + near_ref[...]
    for place, product in enumerate((residual_ref[...] * image, image * image)):
        by_load = product[0:LOADS] + product[LOADS : 2 * LOADS] + product[2 * LOADS : ROWS]
        folded = by_load[:, 0:128]
        for lane in range(128, BLK, 128):
            folded += by_load[:, lane : lane + 128]
        acc_ref[place * LOADS : (place + 1) * LOADS, :] += folded

    @pl.when(step == CHUNKS - 1)
    def _():
        sums_ref[...] = jnp.sum(acc_ref[...].T, axis=0, keepdims=True)


def local_products(got, near, residual, far_basis):
    return call(
        product_kernel,
        "products",
        grid=(CHUNKS,),
        in_specs=[whole(SENT.shape), CHUNK, CHUNK, BASIS],
        out_specs=whole(SUMS.shape),
        out_shape=SUMS,
        scratch_shapes=[COEFS, pltpu.VMEM((2 * LOADS, 128), F32)],
    )(got, near, residual, far_basis)


def sort_kernel(order_ref, values_ref, out_ref):
    rows, cols = values_ref.shape[1], order_ref.shape[1]
    local = lax.rem(order_ref[...], PAN)
    chosen = lax.broadcasted_iota(jnp.int32, (rows, cols), 0) == local
    matrix = jnp.where(chosen, 1.0, 0.0).astype(BF16)
    values = values_ref[...]
    high = values.astype(BF16)
    left_over = values - high.astype(F32)
    middle = left_over.astype(BF16)
    low = (left_over - middle.astype(F32)).astype(BF16)
    out_ref[...] = (
        jnp.dot(high, matrix, preferred_element_type=F32)
        + jnp.dot(middle, matrix, preferred_element_type=F32)
    ) + jnp.dot(low, matrix, preferred_element_type=F32)


def sort_panels(order, values):
    return call(
        sort_kernel,
        "sort_panels",
        grid=(CHUNKS,),
        in_specs=[pl.BlockSpec((1, BLK), lambda b: (0, b)), whole(values.shape)],
        out_specs=PANEL_ROWS,
        out_shape=jax.ShapeDtypeStruct(values.shape, F32),
    )(order, values)


def final_kernel(entries, got_ref, field_ref, residual_ref, sorted_ref, out_ref, step_ref):
    sums = jnp.sum(got_ref[...], axis=0) * (1.0 / entries)
    sums = jnp.broadcast_to(sums, (8, 2 * LOADS))
    square = jnp.concatenate([sums[:, LOADS:], sums[:, LOADS:]], axis=1)
    steps = sums / (square + 1e-06)
    step_ref[...] = steps[0:1]
    column = jnp.concatenate([steps] * 16, axis=0).T[0:LOADS, 0:1]
    normal, slide_a, slide_b = (
        field_ref[rows, :] - column * residual_ref[rows, :]
        for rows in (slice(c * LOADS, (c + 1) * LOADS) for c in range(COMP))
    )
    coeff = sorted_ref[3:4, :]
    live = sorted_ref[4:5, :]
    slip = jnp.sqrt(slide_a * slide_a + slide_b * slide_b + SLIP_EPS)
    stick = slip <= coeff * normal
    slid = jnp.maximum((normal + coeff * slip) / (1.0 + coeff * coeff), 0.0)
    pressed = jnp.where(stick, normal, slid)
    factor = jnp.where(stick, jnp.ones_like(slip), coeff * pressed / slip)
    out_ref[0:LOADS, :] = pressed * live
    out_ref[LOADS : 2 * LOADS, :] = factor * slide_a * live
    out_ref[2 * LOADS : ROWS, :] = factor * slide_b * live


def final_step(got, field, residual, panel_rows, entries):
    return call(
        functools.partial(final_kernel, entries),
        "final",
        grid=(CHUNKS,),
        in_specs=[whole(got.shape), CHUNK, CHUNK, PANEL_ROWS],
        out_specs=[CHUNK, whole(SUMS.shape)],
        out_shape=[FIELD, SUMS],
    )(got, field, residual, panel_rows)


def swap(blocks, axes):
    return lax.all_to_all(blocks, axes, 0, 0)


def beside(blocks):
    size = lax.axis_size(WIDE_NARROW)
    up = [(i, i + 1) for i in range(size - 1)]
    down = [(b, a) for a, b in up]
    return lax.ppermute(blocks, WIDE_NARROW, up), lax.ppermute(blocks, WIDE_NARROW, down)


def tree(place, sent):
    low, up = lower_sums(place, swap(sent, NARROW))
    return swap(upper_sums(place, swap(up, WIDE), low), NARROW)


def body(
    traction,
    near_kernel,
    neighbours,
    far_basis,
    surface_gap,
    friction,
    contact_flags,
    cluster_order,
    approach,
):
    field = traction.reshape(ROWS, PAN)
    place = jnp.stack([lax.axis_index(NARROW), lax.axis_index(WIDE)]).astype(jnp.int32)
    panel_rows = jnp.concatenate(
        [
            surface_gap,
            friction[None],
            contact_flags.astype(F32)[None],
            jnp.zeros((3, PAN), F32),
        ]
    )
    panel_rows = sort_panels(cluster_order[None], panel_rows)

    low, sent = first_coefs(field, far_basis)
    left, right = beside(low)
    near = near_field(
        neighbours, left, low, right, near_kernel, approach.reshape(ROWS, 1), panel_rows
    )
    residual, low, sent = residual_step(tree(place, sent), near, far_basis)
    left, right = beside(low)
    near = near_field(neighbours, left, low, right, near_kernel)
    sums = local_products(tree(place, sent), near, residual, far_basis)

    for axes in (NARROW, WIDE):
        copies = jnp.broadcast_to(sums[None], (GROUP, 1, 2 * LOADS))
        sums = swap(copies, axes)
        if axes is NARROW:
            sums = jnp.sum(sums, axis=0)
    entries = COMP * PAN * lax.axis_size(WIDE_NARROW)
    updated, steps = final_step(sums, field, residual, panel_rows, entries)
    shape = (COMP, LOADS, PAN)
    return updated.reshape(shape), residual.reshape(shape), steps[0, :LOADS]


def solution(mesh):
    finer = Mesh(mesh.devices.reshape(8, 2, 4, 4), ("wide_0", "wide_1", "narrow_0", "narrow_1"))
    placed = (
        P(None, None, WIDE_NARROW),
        P(WIDE_NARROW, None, None, None),
        P(WIDE_NARROW, None),
        P(None, WIDE_NARROW, None),
        P(None, WIDE_NARROW),
        P(WIDE_NARROW),
        P(WIDE_NARROW),
        P(WIDE_NARROW),
        P(),
    )
    return jax.shard_map(
        body,
        mesh=finer,
        in_specs=placed,
        out_specs=(P(None, None, WIDE_NARROW), P(None, None, WIDE_NARROW), P()),
        check_vma=False,
    )
```

time: 310 us -> 170 us (0.55)
  waiting for transfers between devices: 108 us -> 19.9 us
  local copies, waits for them, and re-layouts: 54.8 us -> 21.9 us
  Pallas kernels: 0 us -> 28.2 us
  other arithmetic: 26.3 us -> 0.17 us
  matrix products: 17.4 us -> 0 us
  starting transfers between devices: 58.8 us -> 50.1 us
  blocking collectives: 39.5 us -> 47.5 us
    ppermute x20 -> x4, waiting for transfers between devices: 108 us -> 2.71 us  [the longest x2 1.84 us: beside(): lax.ppermute(blocks, WIDE_NARROW, down)]
    ppermute x20 -> x4, starting transfers between devices: 58.8 us -> 10.6 us  [the longest x2 5.99 us: beside(): lax.ppermute(blocks, WIDE_NARROW, down)]
    all_to_all x0 -> x3, blocking collectives: none -> 47.5 us  [swap(): return lax.all_to_all(blocks, axes, 0, 0)]
    all_to_all x0 -> x5, starting transfers between devices: none -> 39.5 us  [swap(): return lax.all_to_all(blocks, axes, 0, 0)]
    psum x4 -> x0, blocking collectives: 39.5 us -> none  [over_axes(): return functools.reduce(lax.psum, axes, array)]
    gather x5 -> x0, local copies, waits for them, and re-layouts: 29.2 us -> none  [the longest x1 8.39 us: body(): mu_sorted = jnp.take(friction, local_order)]
    pallas_call x0 -> x11, Pallas kernels: none -> 28.2 us  [the longest x2 10.5 us: near_field(): call(near_kernel_body, 'near_field', grid=(CHUNKS,), in_specs=[SCALARS] +...]
    dot_general x6 -> x0, matrix products: 17.4 us -> none  [the longest x2 9.91 us: near_field(): jnp.einsum('bkij,xbkj->xbi', near_kernel, picked, preferred_element_type=...]
  transfers between devices with their start and end apart: 20 -> 9, of which waited for: 12 -> 5; matrix products, arithmetic and copies ran while one was open for 25% -> 1% of each run, Pallas kernels for 0% -> 9%
where the time goes in v1:
time: 170 us; the launch traced here: 169 us
  starting transfers between devices  50.1 us (29%)
  blocking collectives  47.5 us (28%)
  Pallas kernels  28.2 us (17%)
  local copies, waits for them, and re-layouts  21.9 us (13%)
  waiting for transfers between devices  19.9 us (12%)
    all_to_all x3, blocking collectives, swap(): return lax.all_to_all(blocks, axes, 0, 0)  47.5 us
    all_to_all x5, starting transfers between devices, swap(): return lax.all_to_all(blocks, axes, 0, 0)  39.5 us
    unnamed x56, local copies, waits for them, and re-layouts  20.5 us
    all_to_all x5, waiting for transfers between devices, swap(): return lax.all_to_all(blocks, axes, 0, 0)  17.2 us
    pallas_call x2, Pallas kernels, near_field(): call(near_kernel_body, 'near_field', grid=(CHUNKS,), in_specs=[SCALARS] +...  10.5 us
    ppermute x2, starting transfers between devices, beside(): lax.ppermute(blocks, WIDE_NARROW, down)  5.99 us
    ppermute x2, starting transfers between devices, beside(): lax.ppermute(blocks, WIDE_NARROW, up)  4.62 us
    pallas_call x1, Pallas kernels, residual_step(): call(residual_kernel, 'residual', grid=(CHUNKS,), in_specs=[whole(SENT.sh...  3.88 us
  transfers between devices with their start and end apart: 9, of which 5 were waited for; matrix products, arithmetic and copies ran while one was open for 1% of the time, Pallas kernels for 9%

profile of v1, /device:TPU:1, one launch (start us, length us, event | category | flops | bytes accessed | tf_op | source)
XLA Modules:
  0.0 168.7 jit_solution(11908327253224707296)
XLA Ops:
  0.6 1.9 %copy-done = bf16[8,1536,128]{2,1,0:T(8,128)(2,1)S(1)} copy-done((bf16[8,1536,128]{2,1,0:T(8,128)(2,1)S(1)}, bf16[8,1536,128]{2,1,0:T(8,128)(2,1)}, u32[]{:S(2)}) %copy-start) | copy-done | bytes 3145752
  2.5 1.3 copy-done.6
  3.8 2.4 %first_coefs.1 = (bf16[3,192,512]{2,1,0:T(8,128)(2,1)S(1)}, bf16[16,96,128]{2,1,0:T(8,128)(2,1)}) custom-call(f32[192,1536]{1,0:T(8,128)S(1)} %bitcast.9, bf16[8,1536,128]{2,1,0:T(8,128)(2,1)S(1)} %copy-done), custom_call_target="tpu_custom_call" | custom-call | tf_op jit(solution)/shard_map/first_coefs/pallas_call | solution.py:97
  6.2 7.7 %all-to-all-start = ((bf16[16,96,128]{2,1,0:T(8,128)(2,1)}), bf16[16,96,128]{2,1,0:T(8,128)(2,1)S(1)}, u32[]{:S(2)}, u32[]{:S(2)}) async-start(bf16[16,96,128]{2,1,0:T(8,128)(2,1)} %get-tuple-element.14), calls=%async_computation | async-start | bytes 786432 | tf_op jit(solution)/shard_map/all_to_all | solution.py:346
  14.0 8.2 %all-to-all-done.got_ref = bf16[16,96,128]{2,1,0:T(8,128)(2,1)S(1)} async-done(((bf16[16,96,128]{2,1,0:T(8,128)(2,1)}), bf16[16,96,128]{2,1,0:T(8,128)(2,1)S(1)}, u32[]{:S(2)}, u32[]{:S(2)}) %all-to-all-start) | async-done | bytes 393248 | tf_op jit(solution)/shard_map/all_to_all | solution.py:346
  22.2 1.3 lower_sums.2
  23.5 11.1 %all-to-all-start.1 = ((bf16[16,48,128]{2,1,0:T(8,128)(2,1)}), bf16[16,48,128]{2,1,0:T(8,128)(2,1)S(1)}, u32[]{:S(2)}, u32[]{:S(2)}) async-start(bf16[16,48,128]{2,1,0:T(8,128)(2,1)} %get-tuple-element.15), calls=%async_computation.1 | async-start | bytes 393216 | tf_op jit(solution)/shard_map/all_to_all | solution.py:346
  34.6 3.0 %collective-permute-start.1 = (bf16[3,192,512]{2,1,0:T(8,128)(2,1)S(1)}, bf16[3,192,512]{2,1,0:T(8,128)(2,1)S(1)}, u32[]{:S(2)}, u32[]{:S(2)}) collective-permute-start(bf16[3,192,512]{2,1,0:T(8,128)(2,1)S(1)} %get-tuple-element.17.own_ref), channel_id=1, source_target_pairs={{1,0},{2,1},{3,2},{4,3},{5,4},{6,5},{7,6},{8,7},{9,8},{10,9},{11,1... | collective-permute-start | bytes 1769480 | tf_op jit(solution)/shard_map/ppermute | solution.py:353
  37.6 2.3 %collective-permute-start = (bf16[3,192,512]{2,1,0:T(8,128)(2,1)S(1)}, bf16[3,192,512]{2,1,0:T(8,128)(2,1)S(1)}, u32[]{:S(2)}, u32[]{:S(2)}) collective-permute-start(bf16[3,192,512]{2,1,0:T(8,128)(2,1)S(1)} %get-tuple-element.17.own_ref), channel_id=1, source_target_pairs={{0,1},{1,2},{2,3},{3,4},{4,5},{5,6},{6,7},{7,8},{8,9},{9,10},{10,1... | collective-permute-start | bytes 1769480 | tf_op jit(solution)/shard_map/ppermute | solution.py:353
  40.0 0.8 reshape.30.rest_0_
  40.9 4.0 %all-to-all-done.1.got_ref = bf16[16,48,128]{2,1,0:T(8,128)(2,1)S(1)} async-done(((bf16[16,48,128]{2,1,0:T(8,128)(2,1)}), bf16[16,48,128]{2,1,0:T(8,128)(2,1)S(1)}, u32[]{:S(2)}, u32[]{:S(2)}) %all-to-all-start.1) | async-done | bytes 196640 | tf_op jit(solution)/shard_map/all_to_all | solution.py:346
  44.9 1.4 upper_sums.2
  46.3 3.6 %all-to-all-start.2 = ((bf16[16,96,128]{2,1,0:T(8,128)(2,1)}), bf16[16,96,128]{2,1,0:T(8,128)(2,1)S(1)}, u32[]{:S(2)}, u32[]{:S(2)}) async-start(bf16[16,96,128]{2,1,0:T(8,128)(2,1)} %upper_sums.2), calls=%async_computation.2 | async-start | bytes 786432 | tf_op jit(solution)/shard_map/all_to_all | solution.py:346
  49.9 2.3 %sort_panels.1.rest_1_.sorted_ref = f32[8,1536]{1,0:T(8,128)S(1)} custom-call(s32[1,1536]{1,0:T(1,128)S(1)} %broadcast_in_dim.26.order_ref, f32[8,1536]{1,0:T(8,128)S(1)} %maximum_maximum_fusion.values_ref), custom_call_target="tpu_custom_call" | custom-call | tf_op jit(solution)/shard_map/sort_panels/pallas_call | solution.py:301
  52.2 0.8 copy-done.15
  53.1 0.8 copy-done.17
  53.9 1.1 copy-done.12
  55.0 1.1 copy-done.16
  56.0 1.1 copy-done.18
  57.1 0.9 copy-done.21
  58.0 5.2 %near_field.2.near_ref = f32[192,1536]{1,0:T(8,128)S(1)} custom-call(s32[3,4]{1,0:T(4,128)S(1)} %copy-done.22, bf16[3,192,512]{2,1,0:T(8,128)(2,1)S(1)} %copy-done.18, bf16[3,192,512]{2,1,0:T(8,128)(2,1)S(1)} %copy-done.12, bf16[3,192,512]{2,1,0:T(8,128)(2,1)S(1)} %copy-done.16, bf16[3,4,512,512]{3,2,1,0:T(8,128)(2,1)} %kernel_ref.3, ...), custom_call_target="tpu_custom_call" | custom-call | tf_op jit(solution)/shard_map/near_field/pallas_call | solution.py:194
  63.2 1.0 copy-done.2
  64.2 0.6 copy-done.19
  64.8 1.3 copy-done.3
  66.1 3.9 %residual.1 = (f32[192,1536]{1,0:T(8,128)}, bf16[3,192,512]{2,1,0:T(8,128)(2,1)S(1)}, bf16[16,96,128]{2,1,0:T(8,128)(2,1)S(1)}) custom-call(bf16[16,96,128]{2,1,0:T(8,128)(2,1)S(1)} %all-to-all-done.2.got_ref, f32[192,1536]{1,0:T(8,128)S(1)} %copy-done.3, bf16[8,1536,128]{2,1,0:T(8,128)(2,1)S(1)} %copy-done.1), custom_call_target="tpu_custom_call" | custom-call | tf_op jit(solution)/shard_map/residual/pallas_call | solution.py:240
  70.0 14.4 %all_to_all.40.got_ref = bf16[16,96,128]{2,1,0:T(8,128)(2,1)S(1)} all-to-all(bf16[16,96,128]{2,1,0:T(8,128)(2,1)S(1)} %get-tuple-element.18), channel_id=1, replica_groups=mesh['wide_0'=8,'wide_1'=2,'narrow_0'=4,'narrow_1'=4] {'narrow_0','narro..., dimensions={0} | all-to-all | bytes 786432 | tf_op jit(solution)/shard_map/all_to_all | solution.py:346
  84.4 1.3 lower_sums.3
  85.7 13.6 %all-to-all-start.4 = ((bf16[16,48,128]{2,1,0:T(8,128)(2,1)}), bf16[16,48,128]{2,1,0:T(8,128)(2,1)S(1)}, u32[]{:S(2)}, u32[]{:S(2)}) async-start(bf16[16,48,128]{2,1,0:T(8,128)(2,1)} %get-tuple-element.19), calls=%async_computation.4 | async-start | bytes 393216 | tf_op jit(solution)/shard_map/all_to_all | solution.py:346
  99.2 3.0 %collective-permute-start.3 = (bf16[3,192,512]{2,1,0:T(8,128)(2,1)}, bf16[3,192,512]{2,1,0:T(8,128)(2,1)}, u32[]{:S(2)}, u32[]{:S(2)}) collective-permute-start(bf16[3,192,512]{2,1,0:T(8,128)(2,1)} %copy-done.13), channel_id=1, source_target_pairs={{1,0},{2,1},{3,2},{4,3},{5,4},{6,5},{7,6},{8,7},{9,8},{10,9},{11,1... | collective-permute-start | bytes 1769480 | tf_op jit(solution)/shard_map/ppermute | solution.py:353
  102.2 2.3 %collective-permute-start.2 = (bf16[3,192,512]{2,1,0:T(8,128)(2,1)}, bf16[3,192,512]{2,1,0:T(8,128)(2,1)}, u32[]{:S(2)}, u32[]{:S(2)}) collective-permute-start(bf16[3,192,512]{2,1,0:T(8,128)(2,1)} %copy-done.13), channel_id=1, source_target_pairs={{0,1},{1,2},{2,3},{3,4},{4,5},{5,6},{6,7},{7,8},{8,9},{9,10},{10,1... | collective-permute-start | bytes 1769480 | tf_op jit(solution)/shard_map/ppermute | solution.py:353
  104.6 5.0 %all-to-all-done.4.got_ref = bf16[16,48,128]{2,1,0:T(8,128)(2,1)S(1)} async-done(((bf16[16,48,128]{2,1,0:T(8,128)(2,1)}), bf16[16,48,128]{2,1,0:T(8,128)(2,1)S(1)}, u32[]{:S(2)}, u32[]{:S(2)}) %all-to-all-start.4) | async-done | bytes 196640 | tf_op jit(solution)/shard_map/all_to_all | solution.py:346
  109.6 0.6 upper_sums.3
  110.2 0.8 copy-done.10
  110.9 3.6 %all-to-all-start.5 = ((bf16[16,96,128]{2,1,0:T(8,128)(2,1)}), bf16[16,96,128]{2,1,0:T(8,128)(2,1)S(1)}, u32[]{:S(2)}, u32[]{:S(2)}) async-start(bf16[16,96,128]{2,1,0:T(8,128)(2,1)} %copy-done.10), calls=%async_computation.5 | async-start | bytes 786432 | tf_op jit(solution)/shard_map/all_to_all | solution.py:346
  114.5 1.8 %collective-permute-done.3.right_ref = bf16[3,192,512]{2,1,0:T(8,128)(2,1)} collective-permute-done((bf16[3,192,512]{2,1,0:T(8,128)(2,1)}, bf16[3,192,512]{2,1,0:T(8,128)(2,1)}, u32[]{:S(2)}, u32[]{:S(2)}) %collective-permute-start.3) | collective-permute-done | bytes 589856 | tf_op jit(solution)/shard_map/ppermute | solution.py:353
  116.3 0.9 collective-permute-done.2.left_ref
  117.2 1.1 copy-done.14
  118.3 5.3 %near_field.3.near_ref = f32[192,1536]{1,0:T(8,128)S(1)} custom-call(s32[3,4]{1,0:T(4,128)S(1)} %copy-done.22, bf16[3,192,512]{2,1,0:T(8,128)(2,1)} %collective-permute-done.2.left_ref, bf16[3,192,512]{2,1,0:T(8,128)(2,1)S(1)} %copy-done.14, bf16[3,192,512]{2,1,0:T(8,128)(2,1)} %collective-permute-done.3.right_ref, bf16[3,4,512,512]{3,2,1,0:T(8,128)(2,1)} %kernel_ref.3), custom_call_target="tpu_custom_call" | custom-call | tf_op jit(solution)/shard_map/near_field/pallas_call | solution.py:194
  123.6 1.0 copy-done.4
  124.6 1.3 copy-done.5
  125.9 1.3 copy-done.8
  127.2 2.2 %products.1 = f32[1,128]{1,0:T(1,128)S(1)} custom-call(bf16[16,96,128]{2,1,0:T(8,128)(2,1)S(1)} %all-to-all-done.5.got_ref, f32[192,1536]{1,0:T(8,128)S(1)} %copy-done.5, f32[192,1536]{1,0:T(8,128)S(1)} %copy-done.8, bf16[8,1536,128]{2,1,0:T(8,128)(2,1)S(1)} %copy-done.1), custom_call_target="tpu_custom_call" | custom-call | tf_op jit(solution)/shard_map/products/pallas_call | solution.py:273
  129.4 13.5 %all_to_all.41 = f32[16,1,128]{2,1,0:T(1,128)S(1)} all-to-all(f32[16,1,128]{2,1,0:T(1,128)S(1)} %broadcast_in_dim.31), channel_id=1, replica_groups=mesh['wide_0'=8,'wide_1'=2,'narrow_0'=4,'narrow_1'=4] {'narrow_0','narro..., dimensions={0} | all-to-all | bytes 16384 | tf_op jit(solution)/shard_map/all_to_all | solution.py:346
  142.9 19.6 %all_to_all.42.got_ref = f32[16,1,128]{2,1,0:T(1,128)S(1)} all-to-all(f32[16,1,128]{2,1,0:T(1,128)S(1)} %broadcast_in_dim.32), channel_id=1, replica_groups=mesh['wide_0'=8,'wide_1'=2,'narrow_0'=4,'narrow_1'=4] {'wide_0','wide_1'}, dimensions={0} | all-to-all | bytes 16384 | tf_op jit(solution)/shard_map/all_to_all | solution.py:346
  162.5 1.3 copy-done.7
  163.7 1.3 copy-done.9
  165.0 0.8 copy-done.20
  165.8 2.4 %final.1 = (f32[192,1536]{1,0:T(8,128)}, f32[1,128]{1,0:T(1,128)S(1)}) custom-call(f32[16,1,128]{2,1,0:T(1,128)S(1)} %all_to_all.42.got_ref, f32[192,1536]{1,0:T(8,128)S(1)} %bitcast.10, f32[192,1536]{1,0:T(8,128)S(1)} %copy-done.9, f32[8,1536]{1,0:T(8,128)S(1)} %copy-done.20), custom_call_target="tpu_custom_call" | custom-call | tf_op jit(solution)/shard_map/final/pallas_call | solution.py:335
  (53 shorter events, 0.9 us)
Async XLA Ops:
  0.6 1.9 %copy-start = (bf16[8,1536,128]{2,1,0:T(8,128)(2,1)S(1)}, bf16[8,1536,128]{2,1,0:T(8,128)(2,1)}, u32[]{:S(2)}) copy-start(bf16[8,1536,128]{2,1,0:T(8,128)(2,1)} %basis_ref.5) | copy-start | bytes 9437188
  2.5 1.3 copy-start.6
  6.2 40.1 %copy-start.11 = (bf16[3,192,512]{2,1,0:T(8,128)(2,1)}, bf16[3,192,512]{2,1,0:T(8,128)(2,1)S(1)}, u32[]{:S(2)}) copy-start(bf16[3,192,512]{2,1,0:T(8,128)(2,1)S(1)} %get-tuple-element.17.own_ref) | copy-start | bytes 1769476
  6.2 33.8 %copy-start.24 = (f32[1536]{0:T(1024)S(1)}, f32[1536]{0:T(1024)}, u32[]{:S(2)}) copy-start(f32[1536]{0:T(1024)} %param.14) | copy-start | bytes 18436
  6.2 33.8 %copy-start.25 = (s32[1536]{0:T(1024)S(1)}, s32[1536]{0:T(1024)}, u32[]{:S(2)}) copy-start(s32[1536]{0:T(1024)} %param.16) | copy-start | bytes 18436
  6.2 33.8 %copy-start.26 = (s32[1536]{0:T(1024)S(1)}, s32[1536]{0:T(1024)}, u32[]{:S(2)}) copy-start(s32[1536]{0:T(1024)} %param.15) | copy-start | bytes 18436
  6.2 33.8 %copy-start.27 = (f32[3,64]{1,0:T(4,128)S(1)}, f32[3,64]{1,0:T(4,128)}, u32[]{:S(2)}) copy-start(f32[3,64]{1,0:T(4,128)} %param.17) | copy-start | bytes 2308
  6.2 16.0 %all-to-all-start = ((bf16[16,96,128]{2,1,0:T(8,128)(2,1)}), bf16[16,96,128]{2,1,0:T(8,128)(2,1)S(1)}, u32[]{:S(2)}, u32[]{:S(2)}) async-start(bf16[16,96,128]{2,1,0:T(8,128)(2,1)} %get-tuple-element.14), calls=%async_computation | async-start | bytes 786432 | tf_op jit(solution)/shard_map/all_to_all | solution.py:346
  14.0 35.9 %copy-start.23 = (f32[3,1536]{1,0:T(4,128)S(1)}, f32[3,1536]{1,0:T(4,128)}, u32[]{:S(2)}) copy-start(f32[3,1536]{1,0:T(4,128)} %param.13) | copy-start | bytes 55300
  23.5 30.4 %copy-start.22 = (s32[3,4]{1,0:T(4,128)S(1)}, s32[3,4]{1,0:T(4,128)}, u32[]{:S(2)}) copy-start(s32[3,4]{1,0:T(4,128)} %slots_ref.3) | copy-start | bytes 148
  23.5 21.4 %all-to-all-start.1 = ((bf16[16,48,128]{2,1,0:T(8,128)(2,1)}), bf16[16,48,128]{2,1,0:T(8,128)(2,1)S(1)}, u32[]{:S(2)}, u32[]{:S(2)}) async-start(bf16[16,48,128]{2,1,0:T(8,128)(2,1)} %get-tuple-element.15), calls=%async_computation.1 | async-start | bytes 393216 | tf_op jit(solution)/shard_map/all_to_all | solution.py:346
  34.6 17.6 %collective-permute-start.1 = (bf16[3,192,512]{2,1,0:T(8,128)(2,1)S(1)}, bf16[3,192,512]{2,1,0:T(8,128)(2,1)S(1)}, u32[]{:S(2)}, u32[]{:S(2)}) collective-permute-start(bf16[3,192,512]{2,1,0:T(8,128)(2,1)S(1)} %get-tuple-element.17.own_ref), channel_id=1, source_target_pairs={{1,0},{2,1},{3,2},{4,3},{5,4},{6,5},{7,6},{8,7},{9,8},{10,9},{11,1... | collective-permute-start | bytes 1769480 | tf_op jit(solution)/shard_map/ppermute | solution.py:353
  37.6 15.5 %collective-permute-start = (bf16[3,192,512]{2,1,0:T(8,128)(2,1)S(1)}, bf16[3,192,512]{2,1,0:T(8,128)(2,1)S(1)}, u32[]{:S(2)}, u32[]{:S(2)}) collective-permute-start(bf16[3,192,512]{2,1,0:T(8,128)(2,1)S(1)} %get-tuple-element.17.own_ref), channel_id=1, source_target_pairs={{0,1},{1,2},{2,3},{3,4},{4,5},{5,6},{6,7},{7,8},{8,9},{9,10},{10,1... | collective-permute-start | bytes 1769480 | tf_op jit(solution)/shard_map/ppermute | solution.py:353
  46.3 18.5 %all-to-all-start.2 = ((bf16[16,96,128]{2,1,0:T(8,128)(2,1)}), bf16[16,96,128]{2,1,0:T(8,128)(2,1)S(1)}, u32[]{:S(2)}, u32[]{:S(2)}) async-start(bf16[16,96,128]{2,1,0:T(8,128)(2,1)} %upper_sums.2), calls=%async_computation.2 | async-start | bytes 786432 | tf_op jit(solution)/shard_map/all_to_all | solution.py:346
  52.2 0.8 copy-start.15
  53.1 0.8 copy-start.17
  53.9 1.1 copy-start.12
  55.0 1.1 copy-start.16
  56.0 1.1 copy-start.18
  57.1 0.9 copy-start.21
  58.0 6.8 %copy-start.1 = (bf16[8,1536,128]{2,1,0:T(8,128)(2,1)S(1)}, bf16[8,1536,128]{2,1,0:T(8,128)(2,1)}, u32[]{:S(2)}) copy-start(bf16[8,1536,128]{2,1,0:T(8,128)(2,1)} %basis_ref.5) | copy-start | bytes 9437188
  63.2 1.0 copy-start.2
  64.2 0.6 copy-start.19
  64.8 1.3 copy-start.3
  70.0 15.7 %copy-start.13 = (bf16[3,192,512]{2,1,0:T(8,128)(2,1)}, bf16[3,192,512]{2,1,0:T(8,128)(2,1)S(1)}, u32[]{:S(2)}) copy-start(bf16[3,192,512]{2,1,0:T(8,128)(2,1)S(1)} %get-tuple-element.21.own_ref) | copy-start | bytes 1769476
  85.7 23.9 %all-to-all-start.4 = ((bf16[16,48,128]{2,1,0:T(8,128)(2,1)}), bf16[16,48,128]{2,1,0:T(8,128)(2,1)S(1)}, u32[]{:S(2)}, u32[]{:S(2)}) async-start(bf16[16,48,128]{2,1,0:T(8,128)(2,1)} %get-tuple-element.19), calls=%async_computation.4 | async-start | bytes 393216 | tf_op jit(solution)/shard_map/all_to_all | solution.py:346
  99.2 17.1 %collective-permute-start.3 = (bf16[3,192,512]{2,1,0:T(8,128)(2,1)}, bf16[3,192,512]{2,1,0:T(8,128)(2,1)}, u32[]{:S(2)}, u32[]{:S(2)}) collective-permute-start(bf16[3,192,512]{2,1,0:T(8,128)(2,1)} %copy-done.13), channel_id=1, source_target_pairs={{1,0},{2,1},{3,2},{4,3},{5,4},{6,5},{7,6},{8,7},{9,8},{10,9},{11,1... | collective-permute-start | bytes 1769480 | tf_op jit(solution)/shard_map/ppermute | solution.py:353
  102.2 15.0 %collective-permute-start.2 = (bf16[3,192,512]{2,1,0:T(8,128)(2,1)}, bf16[3,192,512]{2,1,0:T(8,128)(2,1)}, u32[]{:S(2)}, u32[]{:S(2)}) collective-permute-start(bf16[3,192,512]{2,1,0:T(8,128)(2,1)} %copy-done.13), channel_id=1, source_target_pairs={{0,1},{1,2},{2,3},{3,4},{4,5},{5,6},{6,7},{7,8},{8,9},{9,10},{10,1... | collective-permute-start | bytes 1769480 | tf_op jit(solution)/shard_map/ppermute | solution.py:353
  110.2 0.8 copy-start.10
  110.9 13.7 %all-to-all-start.5 = ((bf16[16,96,128]{2,1,0:T(8,128)(2,1)}), bf16[16,96,128]{2,1,0:T(8,128)(2,1)S(1)}, u32[]{:S(2)}, u32[]{:S(2)}) async-start(bf16[16,96,128]{2,1,0:T(8,128)(2,1)} %copy-done.10), calls=%async_computation.5 | async-start | bytes 786432 | tf_op jit(solution)/shard_map/all_to_all | solution.py:346
  117.2 1.1 copy-start.14
  123.6 1.0 copy-start.4
  124.6 1.3 copy-start.5
  125.9 1.3 copy-start.8
  162.5 1.3 copy-start.7
  163.7 1.3 copy-start.9
  165.0 0.8 copy-start.20

commit v2 on v1

--- a/solution.py
+++ b/solution.py
@@ -30,7 +30,7 @@
 F32 = jnp.float32
 BF16 = jnp.bfloat16
 NT = (((1,), (1,)), ((), ()))
-LIMIT = 48 * 2**20
+LIMIT = 16 * 2**20
 
 
 def gain(level):
@@ -57,33 +57,43 @@
 BLOCKWISE = pl.BlockSpec((1, ROWS, BLK), lambda b: (b, 0, 0))
 
 
-def add_coefs(values, basis_ref, acc_ref, sent_ref):
-    step = pl.program_id(0)
-
-    @pl.when(step == 0)
-    def _():
-        acc_ref[...] = jnp.zeros_like(acc_ref)
-
+def add_coefs(chunk, values, basis_ref, acc_ref, sent_ref):
     for level in range(HALF):
         pair = jnp.concatenate([basis_ref[level], basis_ref[HALF + level]], axis=1)
-        acc_ref[level] += jnp.dot(values, pair, preferred_element_type=F32)
-
-    @pl.when(step == CHUNKS - 1)
-    def _():
-        for level in range(HALF):
-            for quarter in range(QUARTERS):
-                rows = pl.ds(quarter * PART, PART)
-                slot = level * QUARTERS + quarter
-                sent_ref[slot, 0:PART, :] = acc_ref[level, rows, 0:RANK].astype(BF16)
-                sent_ref[slot, PART : 2 * PART, :] = acc_ref[level, rows, RANK : 2 * RANK].astype(
-                    BF16
-                )
-
-
-def coef_kernel(field_ref, basis_ref, low_ref, sent_ref, acc_ref):
-    values = field_ref[...].astype(BF16)
-    low_ref[0] = values
-    add_coefs(values, basis_ref, acc_ref, sent_ref)
+        part = jnp.dot(values, pair, preferred_element_type=F32)
+        acc_ref[level] = part if chunk == 0 else acc_ref[level] + part
+    if chunk < CHUNKS - 1:
+        return
+    for level in range(HALF):
+        for quarter in range(QUARTERS):
+            rows = pl.ds(quarter * PART, PART)
+            slot = level * QUARTERS + quarter
+            sent_ref[slot, 0:PART, :] = acc_ref[level, rows, 0:RANK].astype(BF16)
+            sent_ref[slot, PART : 2 * PART, :] = acc_ref[level, rows, RANK : 2 * RANK].astype(BF16)
+
+
+def coef_kernel(field_hbm, basis_hbm, low_ref, sent_ref, field_ref, basis_ref, acc_ref, sems):
+    copies = []
+    for chunk in range(CHUNKS):
+        panels = pl.ds(chunk * BLK, BLK)
+        copies.append(
+            (
+                pltpu.make_async_copy(
+                    field_hbm.at[:, panels], field_ref.at[chunk], sems.at[0, chunk]
+                ),
+                pltpu.make_async_copy(
+                    basis_hbm.at[:, panels, :], basis_ref.at[chunk], sems.at[1, chunk]
+                ),
+            )
+        )
+        for copy in copies[-1]:
+            copy.start()
+    for chunk in range(CHUNKS):
+        for copy in copies[chunk]:
+            copy.wait()
+        values = field_ref[chunk].astype(BF16)
+        low_ref[chunk] = values
+        add_coefs(chunk, values, basis_ref.at[chunk], acc_ref, sent_ref)
 
 
 ACC = pltpu.VMEM((HALF, ROWS, 2 * RANK), F32)
@@ -97,11 +107,15 @@
     return call(
         coef_kernel,
         "first_coefs",
-        grid=(CHUNKS,),
-        in_specs=[CHUNK, BASIS],
-        out_specs=[BLOCKWISE, whole(SENT.shape)],
+        in_specs=[pl.BlockSpec(memory_space=pltpu.HBM)] * 2,
+        out_specs=[pl.BlockSpec(memory_space=pltpu.VMEM)] * 2,
         out_shape=[BLOCKS, SENT],
-        scratch_shapes=[ACC],
+        scratch_shapes=[
+            pltpu.VMEM((CHUNKS, ROWS, BLK), F32),
+            pltpu.VMEM((CHUNKS, LEVELS, BLK, RANK), BF16),
+            ACC,
+            pltpu.SemaphoreType.DMA((2, CHUNKS)),
+        ],
     )(field, far_basis)
 
 
@@ -225,24 +239,26 @@
 
 
 def residual_kernel(got_ref, near_ref, basis_ref, out_ref, low_ref, sent_ref, coef_ref, acc_ref):
-    @pl.when(pl.program_id(0) == 0)
-    def _():
-        unpack(got_ref, coef_ref)
-
-    residual = far_field(coef_ref, basis_ref) + near_ref[...]
-    out_ref[...] = residual
-    values = residual.astype(BF16)
-    low_ref[0] = values
-    add_coefs(values, basis_ref, acc_ref, sent_ref)
+    unpack(got_ref, coef_ref)
+    for chunk in range(CHUNKS):
+        panels = pl.ds(chunk * BLK, BLK)
+        part = basis_ref.at[:, panels, :]
+        residual = far_field(coef_ref, part) + near_ref[:, panels]
+        out_ref[:, panels] = residual
+        values = residual.astype(BF16)
+        low_ref[chunk] = values
+        add_coefs(chunk, values, part, acc_ref, sent_ref)
+
+
+IN_VMEM = pl.BlockSpec(memory_space=pltpu.VMEM)
 
 
 def residual_step(got, near, far_basis):
     return call(
         residual_kernel,
         "residual",
-        grid=(CHUNKS,),
-        in_specs=[whole(SENT.shape), CHUNK, BASIS],
-        out_specs=[CHUNK, BLOCKWISE, whole(SENT.shape)],
+        in_specs=[IN_VMEM] * 3,
+        out_specs=[IN_VMEM] * 3,
         out_shape=[FIELD, BLOCKS, SENT],
         scratch_shapes=[COEFS, ACC],
     )(got, near, far_basis)
@@ -391,12 +407,9 @@
     near = near_field(neighbours, left, low, right, near_kernel)
     sums = local_products(tree(place, sent), near, residual, far_basis)
 
-    for axes in (NARROW, WIDE):
-        copies = jnp.broadcast_to(sums[None], (GROUP, 1, 2 * LOADS))
-        sums = swap(copies, axes)
-        if axes is NARROW:
-            sums = jnp.sum(sums, axis=0)
-    entries = COMP * PAN * lax.axis_size(WIDE_NARROW)
+    devices = lax.axis_size(WIDE_NARROW)
+    sums = swap(jnp.broadcast_to(sums[None], (devices, 1, 2 * LOADS)), WIDE_NARROW)
+    entries = COMP * PAN * devices
     updated, steps = final_step(sums, field, residual, panel_rows, entries)
     shape = (COMP, LOADS, PAN)
     return updated.reshape(shape), residual.reshape(shape), steps[0, :LOADS]

time: 170 us -> 166 us (0.976)
  Pallas kernels: 28.2 us -> 24 us
  local copies, waits for them, and re-layouts: 21.9 us -> 24.2 us
  blocking collectives: 47.5 us -> 45.3 us
    pallas_call x2, Pallas kernels: 10.5 us -> 7.26 us  [near_field(): call(near_kernel_body, 'near_field', grid=(CHUNKS,), in_specs=[SCALARS] +...]
    unnamed x56 -> x60, local copies, waits for them, and re-layouts: 20.5 us -> 22.8 us
    all_to_all x3 -> x2, blocking collectives: 47.5 us -> 45.3 us  [swap(): return lax.all_to_all(blocks, axes, 0, 0)]
  transfers between devices with their start and end apart: 9 -> 9, of which waited for: 5 -> 5; matrix products, arithmetic and copies ran while one was open for 1% -> 1% of each run, Pallas kernels for 9% -> 7%
where the time goes in v2:
time: 166 us; the launch traced here: 165 us
  starting transfers between devices  50.1 us (30%)
  blocking collectives  45.3 us (27%)
  local copies, waits for them, and re-layouts  24.2 us (15%)
  Pallas kernels  24 us (14%)
  waiting for transfers between devices  19.9 us (12%)
    all_to_all x2, blocking collectives, swap(): return lax.all_to_all(blocks, axes, 0, 0)  45.3 us
    all_to_all x5, starting transfers between devices, swap(): return lax.all_to_all(blocks, axes, 0, 0)  39.5 us
    unnamed x60, local copies, waits for them, and re-layouts  22.8 us
    all_to_all x5, waiting for transfers between devices, swap(): return lax.all_to_all(blocks, axes, 0, 0)  17.2 us
    pallas_call x2, Pallas kernels, near_field(): call(near_kernel_body, 'near_field', grid=(CHUNKS,), in_specs=[SCALARS] +...  7.26 us
    ppermute x2, starting transfers between devices, beside(): lax.ppermute(blocks, WIDE_NARROW, down)  6.04 us
    ppermute x2, starting transfers between devices, beside(): lax.ppermute(blocks, WIDE_NARROW, up)  4.56 us
  transfers between devices with their start and end apart: 9, of which 5 were waited for; matrix products, arithmetic and copies ran while one was open for 1% of the time, Pallas kernels for 7%

profile of v2, /device:TPU:1, one launch (start us, length us, event | category | flops | bytes accessed | tf_op | source)
XLA Modules:
  0.0 164.6 jit_solution(2533681904101788112)
XLA Ops:
  0.6 1.9 %copy-done = bf16[8,1536,128]{2,1,0:T(8,128)(2,1)S(1)} copy-done((bf16[8,1536,128]{2,1,0:T(8,128)(2,1)S(1)}, bf16[8,1536,128]{2,1,0:T(8,128)(2,1)}, u32[]{:S(2)}) %copy-start) | copy-done | bytes 3145752
  2.5 1.3 copy-done.8
  3.8 2.0 %first_coefs.1 = (bf16[3,192,512]{2,1,0:T(8,128)(2,1)S(1)}, bf16[16,96,128]{2,1,0:T(8,128)(2,1)}) custom-call(f32[192,1536]{1,0:T(8,128)S(1)} %bitcast.8, bf16[8,1536,128]{2,1,0:T(8,128)(2,1)S(1)} %copy-done), custom_call_target="tpu_custom_call" | custom-call | tf_op jit(solution)/shard_map/first_coefs/pallas_call | solution.py:107
  5.9 7.7 %all-to-all-start = ((bf16[16,96,128]{2,1,0:T(8,128)(2,1)}), bf16[16,96,128]{2,1,0:T(8,128)(2,1)S(1)}, u32[]{:S(2)}, u32[]{:S(2)}) async-start(bf16[16,96,128]{2,1,0:T(8,128)(2,1)} %get-tuple-element.14), calls=%async_computation | async-start | bytes 786432 | tf_op jit(solution)/shard_map/all_to_all | solution.py:362
  13.7 8.2 %all-to-all-done.got_ref = bf16[16,96,128]{2,1,0:T(8,128)(2,1)S(1)} async-done(((bf16[16,96,128]{2,1,0:T(8,128)(2,1)}), bf16[16,96,128]{2,1,0:T(8,128)(2,1)S(1)}, u32[]{:S(2)}, u32[]{:S(2)}) %all-to-all-start) | async-done | bytes 393248 | tf_op jit(solution)/shard_map/all_to_all | solution.py:362
  21.9 1.3 lower_sums.2
  23.2 11.1 %all-to-all-start.1 = ((bf16[16,48,128]{2,1,0:T(8,128)(2,1)}), bf16[16,48,128]{2,1,0:T(8,128)(2,1)S(1)}, u32[]{:S(2)}, u32[]{:S(2)}) async-start(bf16[16,48,128]{2,1,0:T(8,128)(2,1)} %get-tuple-element.15), calls=%async_computation.1 | async-start | bytes 393216 | tf_op jit(solution)/shard_map/all_to_all | solution.py:362
  34.3 3.0 %collective-permute-start.1 = (bf16[3,192,512]{2,1,0:T(8,128)(2,1)S(1)}, bf16[3,192,512]{2,1,0:T(8,128)(2,1)S(1)}, u32[]{:S(2)}, u32[]{:S(2)}) collective-permute-start(bf16[3,192,512]{2,1,0:T(8,128)(2,1)S(1)} %get-tuple-element.17.own_ref), channel_id=1, source_target_pairs={{1,0},{2,1},{3,2},{4,3},{5,4},{6,5},{7,6},{8,7},{9,8},{10,9},{11,1... | collective-permute-start | bytes 1769480 | tf_op jit(solution)/shard_map/ppermute | solution.py:369
  37.3 2.3 %collective-permute-start = (bf16[3,192,512]{2,1,0:T(8,128)(2,1)S(1)}, bf16[3,192,512]{2,1,0:T(8,128)(2,1)S(1)}, u32[]{:S(2)}, u32[]{:S(2)}) collective-permute-start(bf16[3,192,512]{2,1,0:T(8,128)(2,1)S(1)} %get-tuple-element.17.own_ref), channel_id=1, source_target_pairs={{0,1},{1,2},{2,3},{3,4},{4,5},{5,6},{6,7},{7,8},{8,9},{9,10},{10,1... | collective-permute-start | bytes 1769480 | tf_op jit(solution)/shard_map/ppermute | solution.py:369
  39.7 0.8 reshape.25.rest_0_
  40.5 0.1 pad.3.clone
  40.6 4.1 %all-to-all-done.1.got_ref = bf16[16,48,128]{2,1,0:T(8,128)(2,1)S(1)} async-done(((bf16[16,48,128]{2,1,0:T(8,128)(2,1)}), bf16[16,48,128]{2,1,0:T(8,128)(2,1)S(1)}, u32[]{:S(2)}, u32[]{:S(2)}) %all-to-all-start.1) | async-done | bytes 196640 | tf_op jit(solution)/shard_map/all_to_all | solution.py:362
  44.6 1.4 upper_sums.2
  46.0 3.6 %all-to-all-start.2 = ((bf16[16,96,128]{2,1,0:T(8,128)(2,1)}), bf16[16,96,128]{2,1,0:T(8,128)(2,1)S(1)}, u32[]{:S(2)}, u32[]{:S(2)}) async-start(bf16[16,96,128]{2,1,0:T(8,128)(2,1)} %upper_sums.2), calls=%async_computation.2 | async-start | bytes 786432 | tf_op jit(solution)/shard_map/all_to_all | solution.py:362
  49.7 2.3 %sort_panels.1.rest_1_.sorted_ref = f32[8,1536]{1,0:T(8,128)S(1)} custom-call(s32[1,1536]{1,0:T(1,128)S(1)} %broadcast_in_dim.20.order_ref, f32[8,1536]{1,0:T(8,128)S(1)} %maximum_maximum_fusion.values_ref), custom_call_target="tpu_custom_call" | custom-call | tf_op jit(solution)/shard_map/sort_panels/pallas_call | solution.py:317
  52.0 0.8 copy-done.17
  52.8 0.8 copy-done.19
  53.6 2.8 %copy-done.2 = bf16[3,4,512,512]{3,2,1,0:T(8,128)(2,1)S(1)} copy-done((bf16[3,4,512,512]{3,2,1,0:T(8,128)(2,1)S(1)}, bf16[3,4,512,512]{3,2,1,0:T(8,128)(2,1)}, u32[]{:S(2)}) %copy-start.2) | copy-done | bytes 6291480
  56.4 1.1 copy-done.14
  57.4 1.1 copy-done.18
  58.5 1.1 copy-done.20
  59.6 0.9 copy-done.23
  60.5 3.3 %near_field.2.near_ref = f32[192,1536]{1,0:T(8,128)S(1)} custom-call(s32[3,4]{1,0:T(4,128)S(1)} %copy-done.24, bf16[3,192,512]{2,1,0:T(8,128)(2,1)S(1)} %copy-done.20, bf16[3,192,512]{2,1,0:T(8,128)(2,1)S(1)} %copy-done.14, bf16[3,192,512]{2,1,0:T(8,128)(2,1)S(1)} %copy-done.18, bf16[3,4,512,512]{3,2,1,0:T(8,128)(2,1)S(1)} %copy-done.2, ...), custom_call_target="tpu_custom_call" | custom-call | tf_op jit(solution)/shard_map/near_field/pallas_call | solution.py:208
  63.8 1.0 copy-done.4
  64.8 0.6 copy-done.21
  65.4 1.3 copy-done.5
  66.7 2.8 %residual.1 = (f32[192,1536]{1,0:T(8,128)}, bf16[3,192,512]{2,1,0:T(8,128)(2,1)S(1)}, bf16[16,96,128]{2,1,0:T(8,128)(2,1)S(1)}) custom-call(bf16[16,96,128]{2,1,0:T(8,128)(2,1)S(1)} %all-to-all-done.2.got_ref, f32[192,1536]{1,0:T(8,128)S(1)} %copy-done.5, bf16[8,1536,128]{2,1,0:T(8,128)(2,1)S(1)} %copy-done.1), custom_call_target="tpu_custom_call" | custom-call | tf_op jit(solution)/shard_map/residual/pallas_call | solution.py:257
  69.5 14.4 %all_to_all.35.got_ref = bf16[16,96,128]{2,1,0:T(8,128)(2,1)S(1)} all-to-all(bf16[16,96,128]{2,1,0:T(8,128)(2,1)S(1)} %get-tuple-element.18), channel_id=1, replica_groups=mesh['wide_0'=8,'wide_1'=2,'narrow_0'=4,'narrow_1'=4] {'narrow_0','narro..., dimensions={0} | all-to-all | bytes 786432 | tf_op jit(solution)/shard_map/all_to_all | solution.py:362
  83.8 1.3 lower_sums.3
  85.2 13.6 %all-to-all-start.4 = ((bf16[16,48,128]{2,1,0:T(8,128)(2,1)}), bf16[16,48,128]{2,1,0:T(8,128)(2,1)S(1)}, u32[]{:S(2)}, u32[]{:S(2)}) async-start(bf16[16,48,128]{2,1,0:T(8,128)(2,1)} %get-tuple-element.19), calls=%async_computation.4 | async-start | bytes 393216 | tf_op jit(solution)/shard_map/all_to_all | solution.py:362
  98.7 3.0 %collective-permute-start.3 = (bf16[3,192,512]{2,1,0:T(8,128)(2,1)}, bf16[3,192,512]{2,1,0:T(8,128)(2,1)}, u32[]{:S(2)}, u32[]{:S(2)}) collective-permute-start(bf16[3,192,512]{2,1,0:T(8,128)(2,1)} %copy-done.15), channel_id=1, source_target_pairs={{1,0},{2,1},{3,2},{4,3},{5,4},{6,5},{7,6},{8,7},{9,8},{10,9},{11,1... | collective-permute-start | bytes 1769480 | tf_op jit(solution)/shard_map/ppermute | solution.py:369
  101.8 2.3 %collective-permute-start.2 = (bf16[3,192,512]{2,1,0:T(8,128)(2,1)}, bf16[3,192,512]{2,1,0:T(8,128)(2,1)}, u32[]{:S(2)}, u32[]{:S(2)}) collective-permute-start(bf16[3,192,512]{2,1,0:T(8,128)(2,1)} %copy-done.15), channel_id=1, source_target_pairs={{0,1},{1,2},{2,3},{3,4},{4,5},{5,6},{6,7},{7,8},{8,9},{9,10},{10,1... | collective-permute-start | bytes 1769480 | tf_op jit(solution)/shard_map/ppermute | solution.py:369
  104.1 5.0 %all-to-all-done.4.got_ref = bf16[16,48,128]{2,1,0:T(8,128)(2,1)S(1)} async-done(((bf16[16,48,128]{2,1,0:T(8,128)(2,1)}), bf16[16,48,128]{2,1,0:T(8,128)(2,1)S(1)}, u32[]{:S(2)}, u32[]{:S(2)}) %all-to-all-start.4) | async-done | bytes 196640 | tf_op jit(solution)/shard_map/all_to_all | solution.py:362
  109.1 0.6 upper_sums.3
  109.7 0.8 copy-done.12
  110.5 3.6 %all-to-all-start.5 = ((bf16[16,96,128]{2,1,0:T(8,128)(2,1)}), bf16[16,96,128]{2,1,0:T(8,128)(2,1)S(1)}, u32[]{:S(2)}, u32[]{:S(2)}) async-start(bf16[16,96,128]{2,1,0:T(8,128)(2,1)} %copy-done.12), calls=%async_computation.5 | async-start | bytes 786432 | tf_op jit(solution)/shard_map/all_to_all | solution.py:362
  114.0 1.8 %collective-permute-done.3.right_ref = bf16[3,192,512]{2,1,0:T(8,128)(2,1)} collective-permute-done((bf16[3,192,512]{2,1,0:T(8,128)(2,1)}, bf16[3,192,512]{2,1,0:T(8,128)(2,1)}, u32[]{:S(2)}, u32[]{:S(2)}) %collective-permute-start.3) | collective-permute-done | bytes 589856 | tf_op jit(solution)/shard_map/ppermute | solution.py:369
  115.8 0.9 collective-permute-done.2.left_ref
  116.7 2.8 %copy-done.3 = bf16[3,4,512,512]{3,2,1,0:T(8,128)(2,1)S(1)} copy-done((bf16[3,4,512,512]{3,2,1,0:T(8,128)(2,1)S(1)}, bf16[3,4,512,512]{3,2,1,0:T(8,128)(2,1)}, u32[]{:S(2)}) %copy-start.3) | copy-done | bytes 6291480
  119.5 1.1 copy-done.16
  120.6 4.0 %near_field.3.near_ref = f32[192,1536]{1,0:T(8,128)S(1)} custom-call(s32[3,4]{1,0:T(4,128)S(1)} %copy-done.24, bf16[3,192,512]{2,1,0:T(8,128)(2,1)} %collective-permute-done.2.left_ref, bf16[3,192,512]{2,1,0:T(8,128)(2,1)S(1)} %copy-done.16, bf16[3,192,512]{2,1,0:T(8,128)(2,1)} %collective-permute-done.3.right_ref, bf16[3,4,512,512]{3,2,1,0:T(8,128)(2,1)S(1)} %copy-done.3), custom_call_target="tpu_custom_call" | custom-call | tf_op jit(solution)/shard_map/near_field/pallas_call | solution.py:208
  124.5 1.0 copy-done.6
  125.5 1.3 copy-done.7
  126.8 1.3 copy-done.10
  128.1 2.2 %products.1 = f32[1,128]{1,0:T(1,128)S(1)} custom-call(bf16[16,96,128]{2,1,0:T(8,128)(2,1)S(1)} %all-to-all-done.5.got_ref, f32[192,1536]{1,0:T(8,128)S(1)} %copy-done.7, f32[192,1536]{1,0:T(8,128)S(1)} %copy-done.10, bf16[8,1536,128]{2,1,0:T(8,128)(2,1)S(1)} %copy-done.1), custom_call_target="tpu_custom_call" | custom-call | tf_op jit(solution)/shard_map/products/pallas_call | solution.py:289
  130.3 30.9 %all_to_all.36.got_ref = f32[256,1,128]{2,1,0:T(1,128)S(1)} all-to-all(f32[256,1,128]{2,1,0:T(1,128)S(1)} %broadcast_in_dim.25), channel_id=1, replica_groups=mesh['wide_0'=8,'wide_1'=2,'narrow_0'=4,'narrow_1'=4] {'wide_0','wide_1'..., dimensions={0} | all-to-all | bytes 262144 | tf_op jit(solution)/shard_map/all_to_all | solution.py:362
  161.2 2.9 %final.1 = (f32[192,1536]{1,0:T(8,128)}, f32[1,128]{1,0:T(1,128)S(1)}) custom-call(f32[256,1,128]{2,1,0:T(1,128)S(1)} %all_to_all.36.got_ref, f32[192,1536]{1,0:T(8,128)S(1)} %bitcast.9, f32[192,1536]{1,0:T(8,128)S(1)} %copy-done.11, f32[8,1536]{1,0:T(8,128)S(1)} %copy-done.22), custom_call_target="tpu_custom_call" | custom-call | tf_op jit(solution)/shard_map/final/pallas_call | solution.py:351
  164.1 0.5 slice_bitcast_fusion
  (54 shorter events, 0.3 us)
Async XLA Ops:
  0.6 1.9 %copy-start = (bf16[8,1536,128]{2,1,0:T(8,128)(2,1)S(1)}, bf16[8,1536,128]{2,1,0:T(8,128)(2,1)}, u32[]{:S(2)}) copy-start(bf16[8,1536,128]{2,1,0:T(8,128)(2,1)} %basis_ref.3) | copy-start | bytes 9437188
  2.5 1.3 copy-start.8
  5.8 40.2 %copy-start.13 = (bf16[3,192,512]{2,1,0:T(8,128)(2,1)}, bf16[3,192,512]{2,1,0:T(8,128)(2,1)S(1)}, u32[]{:S(2)}) copy-start(bf16[3,192,512]{2,1,0:T(8,128)(2,1)S(1)} %get-tuple-element.17.own_ref) | copy-start | bytes 1769476
  5.8 33.8 %copy-start.26 = (f32[1536]{0:T(1024)S(1)}, f32[1536]{0:T(1024)}, u32[]{:S(2)}) copy-start(f32[1536]{0:T(1024)} %param.14) | copy-start | bytes 18436
  5.8 33.8 %copy-start.27 = (s32[1536]{0:T(1024)S(1)}, s32[1536]{0:T(1024)}, u32[]{:S(2)}) copy-start(s32[1536]{0:T(1024)} %param.16) | copy-start | bytes 18436
  5.9 33.8 %copy-start.28 = (s32[1536]{0:T(1024)S(1)}, s32[1536]{0:T(1024)}, u32[]{:S(2)}) copy-start(s32[1536]{0:T(1024)} %param.15) | copy-start | bytes 18436
  5.9 33.8 %copy-start.29 = (f32[3,64]{1,0:T(4,128)S(1)}, f32[3,64]{1,0:T(4,128)}, u32[]{:S(2)}) copy-start(f32[3,64]{1,0:T(4,128)} %param.17) | copy-start | bytes 2308
  5.9 16.0 %all-to-all-start = ((bf16[16,96,128]{2,1,0:T(8,128)(2,1)}), bf16[16,96,128]{2,1,0:T(8,128)(2,1)S(1)}, u32[]{:S(2)}, u32[]{:S(2)}) async-start(bf16[16,96,128]{2,1,0:T(8,128)(2,1)} %get-tuple-element.14), calls=%async_computation | async-start | bytes 786432 | tf_op jit(solution)/shard_map/all_to_all | solution.py:362
  13.7 35.9 %copy-start.25 = (f32[3,1536]{1,0:T(4,128)S(1)}, f32[3,1536]{1,0:T(4,128)}, u32[]{:S(2)}) copy-start(f32[3,1536]{1,0:T(4,128)} %param.13) | copy-start | bytes 55300
  23.2 30.4 %copy-start.24 = (s32[3,4]{1,0:T(4,128)S(1)}, s32[3,4]{1,0:T(4,128)}, u32[]{:S(2)}) copy-start(s32[3,4]{1,0:T(4,128)} %slots_ref.3) | copy-start | bytes 148
  23.2 21.5 %all-to-all-start.1 = ((bf16[16,48,128]{2,1,0:T(8,128)(2,1)}), bf16[16,48,128]{2,1,0:T(8,128)(2,1)S(1)}, u32[]{:S(2)}, u32[]{:S(2)}) async-start(bf16[16,48,128]{2,1,0:T(8,128)(2,1)} %get-tuple-element.15), calls=%async_computation.1 | async-start | bytes 393216 | tf_op jit(solution)/shard_map/all_to_all | solution.py:362
  34.3 17.6 %collective-permute-start.1 = (bf16[3,192,512]{2,1,0:T(8,128)(2,1)S(1)}, bf16[3,192,512]{2,1,0:T(8,128)(2,1)S(1)}, u32[]{:S(2)}, u32[]{:S(2)}) collective-permute-start(bf16[3,192,512]{2,1,0:T(8,128)(2,1)S(1)} %get-tuple-element.17.own_ref), channel_id=1, source_target_pairs={{1,0},{2,1},{3,2},{4,3},{5,4},{6,5},{7,6},{8,7},{9,8},{10,9},{11,1... | collective-permute-start | bytes 1769480 | tf_op jit(solution)/shard_map/ppermute | solution.py:369
  37.3 15.5 %collective-permute-start = (bf16[3,192,512]{2,1,0:T(8,128)(2,1)S(1)}, bf16[3,192,512]{2,1,0:T(8,128)(2,1)S(1)}, u32[]{:S(2)}, u32[]{:S(2)}) collective-permute-start(bf16[3,192,512]{2,1,0:T(8,128)(2,1)S(1)} %get-tuple-element.17.own_ref), channel_id=1, source_target_pairs={{0,1},{1,2},{2,3},{3,4},{4,5},{5,6},{6,7},{7,8},{8,9},{9,10},{10,1... | collective-permute-start | bytes 1769480 | tf_op jit(solution)/shard_map/ppermute | solution.py:369
  46.0 19.4 %all-to-all-start.2 = ((bf16[16,96,128]{2,1,0:T(8,128)(2,1)}), bf16[16,96,128]{2,1,0:T(8,128)(2,1)S(1)}, u32[]{:S(2)}, u32[]{:S(2)}) async-start(bf16[16,96,128]{2,1,0:T(8,128)(2,1)} %upper_sums.2), calls=%async_computation.2 | async-start | bytes 786432 | tf_op jit(solution)/shard_map/all_to_all | solution.py:362
  51.9 0.8 copy-start.17
  52.8 0.8 copy-start.19
  53.6 2.8 %copy-start.2 = (bf16[3,4,512,512]{3,2,1,0:T(8,128)(2,1)S(1)}, bf16[3,4,512,512]{3,2,1,0:T(8,128)(2,1)}, u32[]{:S(2)}) copy-start(bf16[3,4,512,512]{3,2,1,0:T(8,128)(2,1)} %kernel_ref.3) | copy-start | bytes 18874372
  56.4 1.1 copy-start.14
  57.4 1.1 copy-start.18
  58.5 1.1 copy-start.20
  59.6 0.9 copy-start.23
  60.5 4.9 %copy-start.1 = (bf16[8,1536,128]{2,1,0:T(8,128)(2,1)S(1)}, bf16[8,1536,128]{2,1,0:T(8,128)(2,1)}, u32[]{:S(2)}) copy-start(bf16[8,1536,128]{2,1,0:T(8,128)(2,1)} %basis_ref.3) | copy-start | bytes 9437188
  63.8 1.0 copy-start.4
  64.8 0.6 copy-start.21
  65.4 1.3 copy-start.5
  69.5 15.7 %copy-start.15 = (bf16[3,192,512]{2,1,0:T(8,128)(2,1)}, bf16[3,192,512]{2,1,0:T(8,128)(2,1)S(1)}, u32[]{:S(2)}) copy-start(bf16[3,192,512]{2,1,0:T(8,128)(2,1)S(1)} %get-tuple-element.21.own_ref) | copy-start | bytes 1769476
  85.2 23.9 %all-to-all-start.4 = ((bf16[16,48,128]{2,1,0:T(8,128)(2,1)}), bf16[16,48,128]{2,1,0:T(8,128)(2,1)S(1)}, u32[]{:S(2)}, u32[]{:S(2)}) async-start(bf16[16,48,128]{2,1,0:T(8,128)(2,1)} %get-tuple-element.19), calls=%async_computation.4 | async-start | bytes 393216 | tf_op jit(solution)/shard_map/all_to_all | solution.py:362
  98.7 17.1 %collective-permute-start.3 = (bf16[3,192,512]{2,1,0:T(8,128)(2,1)}, bf16[3,192,512]{2,1,0:T(8,128)(2,1)}, u32[]{:S(2)}, u32[]{:S(2)}) collective-permute-start(bf16[3,192,512]{2,1,0:T(8,128)(2,1)} %copy-done.15), channel_id=1, source_target_pairs={{1,0},{2,1},{3,2},{4,3},{5,4},{6,5},{7,6},{8,7},{9,8},{10,9},{11,1... | collective-permute-start | bytes 1769480 | tf_op jit(solution)/shard_map/ppermute | solution.py:369
  101.8 14.9 %collective-permute-start.2 = (bf16[3,192,512]{2,1,0:T(8,128)(2,1)}, bf16[3,192,512]{2,1,0:T(8,128)(2,1)}, u32[]{:S(2)}, u32[]{:S(2)}) collective-permute-start(bf16[3,192,512]{2,1,0:T(8,128)(2,1)} %copy-done.15), channel_id=1, source_target_pairs={{0,1},{1,2},{2,3},{3,4},{4,5},{5,6},{6,7},{7,8},{8,9},{9,10},{10,1... | collective-permute-start | bytes 1769480 | tf_op jit(solution)/shard_map/ppermute | solution.py:369
  109.7 0.8 copy-start.12
  110.5 15.1 %all-to-all-start.5 = ((bf16[16,96,128]{2,1,0:T(8,128)(2,1)}), bf16[16,96,128]{2,1,0:T(8,128)(2,1)S(1)}, u32[]{:S(2)}, u32[]{:S(2)}) async-start(bf16[16,96,128]{2,1,0:T(8,128)(2,1)} %copy-done.12), calls=%async_computation.5 | async-start | bytes 786432 | tf_op jit(solution)/shard_map/all_to_all | solution.py:362
  116.7 2.8 %copy-start.3 = (bf16[3,4,512,512]{3,2,1,0:T(8,128)(2,1)S(1)}, bf16[3,4,512,512]{3,2,1,0:T(8,128)(2,1)}, u32[]{:S(2)}) copy-start(bf16[3,4,512,512]{3,2,1,0:T(8,128)(2,1)} %kernel_ref.3) | copy-start | bytes 18874372
  119.5 1.1 copy-start.16
  124.5 1.0 copy-start.6
  125.5 1.3 copy-start.7
  126.8 1.3 copy-start.10
  128.1 33.1 %copy-start.9 = (f32[3,64,1536]{2,1,0:T(8,128)S(1)}, f32[3,64,1536]{2,1,0:T(8,128)}, u32[]{:S(2)}) copy-start(f32[3,64,1536]{2,1,0:T(8,128)} %param.9) | copy-start | bytes 3538948
  128.1 33.1 %copy-start.11 = (f32[192,1536]{1,0:T(8,128)S(1)}, f32[192,1536]{1,0:T(8,128)}, u32[]{:S(2)}) copy-start(f32[192,1536]{1,0:T(8,128)} %get-tuple-element.22.residual_ref) | copy-start | bytes 3538948
  128.1 33.1 %copy-start.22 = (f32[8,1536]{1,0:T(8,128)S(1)}, f32[8,1536]{1,0:T(8,128)}, u32[]{:S(2)}) copy-start(f32[8,1536]{1,0:T(8,128)} %copy-done.21) | copy-start | bytes 147460

commit v3 on v2

--- a/solution.py
+++ b/solution.py
@@ -46,11 +46,21 @@
     )
 
 
+def in_vmem(array):
+    return pltpu.with_memory_space_constraint(array, pltpu.VMEM)
+
+
+def in_hbm(array):
+    return pltpu.with_memory_space_constraint(array, pltpu.HBM)
+
+
 def whole(shape):
     return pl.BlockSpec(shape, lambda *_: (0,) * len(shape))
 
 
 SCALARS = pl.BlockSpec(memory_space=pltpu.SMEM)
+IN_VMEM = pl.BlockSpec(memory_space=pltpu.VMEM)
+IN_HBM = pl.BlockSpec(memory_space=pltpu.HBM)
 CHUNK = pl.BlockSpec((ROWS, BLK), lambda b: (0, b))
 BASIS = pl.BlockSpec((LEVELS, BLK, RANK), lambda b: (0, b, 0))
 PANEL_ROWS = pl.BlockSpec((8, BLK), lambda b: (0, b))
@@ -97,9 +107,9 @@
 
 
 ACC = pltpu.VMEM((HALF, ROWS, 2 * RANK), F32)
-SENT = jax.ShapeDtypeStruct((GROUP, 2 * PART, RANK), BF16)
-BLOCKS = jax.ShapeDtypeStruct((CHUNKS, ROWS, BLK), BF16)
-FIELD = jax.ShapeDtypeStruct((ROWS, PAN), F32)
+SENT = pltpu.HBM((GROUP, 2 * PART, RANK), BF16)
+BLOCKS = pltpu.HBM((CHUNKS, ROWS, BLK), BF16)
+FIELD = pltpu.HBM((ROWS, PAN), F32)
 SUMS = jax.ShapeDtypeStruct((1, 2 * LOADS), F32)
 
 
@@ -107,8 +117,8 @@
     return call(
         coef_kernel,
         "first_coefs",
-        in_specs=[pl.BlockSpec(memory_space=pltpu.HBM)] * 2,
-        out_specs=[pl.BlockSpec(memory_space=pltpu.VMEM)] * 2,
+        in_specs=[IN_HBM] * 2,
+        out_specs=[IN_VMEM] * 2,
         out_shape=[BLOCKS, SENT],
         scratch_shapes=[
             pltpu.VMEM((CHUNKS, ROWS, BLK), F32),
@@ -116,7 +126,7 @@
             ACC,
             pltpu.SemaphoreType.DMA((2, CHUNKS)),
         ],
-    )(field, far_basis)
+    )(in_hbm(field), in_hbm(far_basis))
 
 
 def lower_kernel(place_ref, got_ref, low_ref, up_ref):
@@ -141,7 +151,7 @@
 
 
 def lower_sums(place, got):
-    part = jax.ShapeDtypeStruct((GROUP, PART, RANK), BF16)
+    part = pltpu.HBM((GROUP, PART, RANK), BF16)
     return call(
         lower_kernel,
         "lower_sums",
@@ -180,43 +190,67 @@
     )(place, got, low)
 
 
-def near_kernel_body(slots_ref, left_ref, own_ref, right_ref, kernel_ref, *rest):
-    out_ref, ext_ref = rest[-2:]
+def near_kernel_body(slots_ref, left_hbm, own_hbm, right_hbm, kernel_hbm, *rest):
+    out_ref, ext_ref, kernel_ref, ext_sems, kernel_sems = rest[-5:]
     block = pl.program_id(0)
+
+    def sides():
+        for side, source in enumerate((own_hbm, left_hbm, right_hbm)):
+            place = ((1, 0, 2)[side]) * CHUNKS
+            yield pltpu.make_async_copy(
+                source, ext_ref.at[pl.ds(place, CHUNKS)], ext_sems.at[side]
+            )
+
+    def kernel_copy(at):
+        return pltpu.make_async_copy(kernel_hbm.at[at], kernel_ref.at[at], kernel_sems.at[at])
 
     @pl.when(block == 0)
     def _():
-        ext_ref[0:CHUNKS] = left_ref[...]
-        ext_ref[CHUNKS : 2 * CHUNKS] = own_ref[...]
-        ext_ref[2 * CHUNKS : 3 * CHUNKS] = right_ref[...]
-
+        for copy in sides():
+            copy.start()
+        for at in range(CHUNKS):
+            kernel_copy(at).start()
+        for copy in sides():
+            copy.wait()
+
+    kernel_copy(block).wait()
     total = jnp.zeros((ROWS, BLK), F32)
     for k in range(kernel_ref.shape[1]):
         slot = slots_ref[block, k] - slots_ref[block, 0] + block + CHUNKS
-        total += lax.dot_general(ext_ref[slot], kernel_ref[0, k], NT, preferred_element_type=F32)
-    if len(rest) == 2:
+        total += lax.dot_general(
+            ext_ref[slot], kernel_ref[block, k], NT, preferred_element_type=F32
+        )
+    if len(rest) == 5:
         out_ref[...] = total
         return
     approach_ref, gap_ref = rest[:2]
+    square = (LOADS, LOADS)
+    diagonal = lax.broadcasted_iota(jnp.int32, square, 0) == lax.broadcasted_iota(
+        jnp.int32, square, 1
+    )
     for comp in range(COMP):
         rows = slice(comp * LOADS, (comp + 1) * LOADS)
-        out_ref[rows, :] = total[rows] - (approach_ref[rows, :] - gap_ref[comp : comp + 1, :])
+        row = jnp.broadcast_to(approach_ref[comp : comp + 1, :], square)
+        column = jnp.sum(jnp.where(diagonal, row, 0.0), axis=1, keepdims=True)
+        out_ref[rows, :] = total[rows] - (column - gap_ref[comp : comp + 1, :])
 
 
 def near_field(neighbours, left, own, right, near_kernel, *target):
-    specs = [whole((ROWS, 1)), PANEL_ROWS] if target else []
+    specs = [whole((COMP, LOADS)), PANEL_ROWS] if target else []
     return call(
         near_kernel_body,
         "near_field",
         grid=(CHUNKS,),
-        in_specs=[SCALARS]
-        + [whole(BLOCKS.shape)] * 3
-        + [pl.BlockSpec((1,) + near_kernel.shape[1:], lambda b: (b, 0, 0, 0))]
-        + specs,
+        in_specs=[SCALARS] + [IN_HBM] * 4 + specs,
         out_specs=CHUNK,
         out_shape=FIELD,
-        scratch_shapes=[pltpu.VMEM((3 * CHUNKS, ROWS, BLK), BF16)],
-    )(neighbours, left, own, right, near_kernel, *target)
+        scratch_shapes=[
+            pltpu.VMEM((3 * CHUNKS, ROWS, BLK), BF16),
+            pltpu.VMEM(near_kernel.shape, BF16),
+            pltpu.SemaphoreType.DMA((3,)),
+            pltpu.SemaphoreType.DMA((CHUNKS,)),
+        ],
+    )(neighbours, *map(in_hbm, (left, own, right, near_kernel)), *target)
 
 
 def unpack(got_ref, coef_ref):
@@ -238,30 +272,56 @@
 COEFS = pltpu.VMEM((ROWS, LEVELS * RANK), BF16)
 
 
-def residual_kernel(got_ref, near_ref, basis_ref, out_ref, low_ref, sent_ref, coef_ref, acc_ref):
+def residual_kernel(
+    got_ref, near_hbm, basis_ref, out_hbm, low_hbm, sent_ref, *scratch
+):
+    near_ref, out_ref, low_ref, coef_ref, acc_ref, sems = scratch
+
+    arriving, leaving = [], []
+    for chunk in range(CHUNKS):
+        panels = pl.ds(chunk * BLK, BLK)
+        copy = pltpu.make_async_copy(
+            near_hbm.at[:, panels], near_ref.at[chunk], sems.at[0, chunk]
+        )
+        copy.start()
+        arriving.append(copy)
     unpack(got_ref, coef_ref)
     for chunk in range(CHUNKS):
         panels = pl.ds(chunk * BLK, BLK)
         part = basis_ref.at[:, panels, :]
-        residual = far_field(coef_ref, part) + near_ref[:, panels]
-        out_ref[:, panels] = residual
+        far = far_field(coef_ref, part)
+        arriving[chunk].wait()
+        residual = far + near_ref[chunk]
+        out_ref[chunk] = residual
         values = residual.astype(BF16)
         low_ref[chunk] = values
+        for copy in (
+            pltpu.make_async_copy(out_ref.at[chunk], out_hbm.at[:, panels], sems.at[1, chunk]),
+            pltpu.make_async_copy(low_ref.at[chunk], low_hbm.at[chunk], sems.at[2, chunk]),
+        ):
+            copy.start()
+            leaving.append(copy)
         add_coefs(chunk, values, part, acc_ref, sent_ref)
-
-
-IN_VMEM = pl.BlockSpec(memory_space=pltpu.VMEM)
+    for copy in leaving:
+        copy.wait()
 
 
 def residual_step(got, near, far_basis):
     return call(
         residual_kernel,
         "residual",
-        in_specs=[IN_VMEM] * 3,
-        out_specs=[IN_VMEM] * 3,
+        in_specs=[IN_VMEM, IN_HBM, IN_VMEM],
+        out_specs=[IN_HBM, IN_HBM, IN_VMEM],
         out_shape=[FIELD, BLOCKS, SENT],
-        scratch_shapes=[COEFS, ACC],
-    )(got, near, far_basis)
+        scratch_shapes=[
+            pltpu.VMEM((CHUNKS, ROWS, BLK), F32),
+            pltpu.VMEM((CHUNKS, ROWS, BLK), F32),
+            pltpu.VMEM((CHUNKS, ROWS, BLK), BF16),
+            COEFS,
+            ACC,
+            pltpu.SemaphoreType.DMA((3, CHUNKS)),
+        ],
+    )(in_vmem(got), in_hbm(near), in_vmem(far_basis))
 
 
 def product_kernel(got_ref, near_ref, residual_ref, basis_ref, sums_ref, coef_ref, acc_ref):
@@ -294,7 +354,7 @@
         out_specs=whole(SUMS.shape),
         out_shape=SUMS,
         scratch_shapes=[COEFS, pltpu.VMEM((2 * LOADS, 128), F32)],
-    )(got, near, residual, far_basis)
+    )(in_vmem(got), in_hbm(near), in_hbm(residual), in_vmem(far_basis))
 
 
 def sort_kernel(order_ref, values_ref, out_ref):
@@ -329,7 +389,7 @@
     sums = jnp.broadcast_to(sums, (8, 2 * LOADS))
     square = jnp.concatenate([sums[:, LOADS:], sums[:, LOADS:]], axis=1)
     steps = sums / (square + 1e-06)
-    step_ref[...] = steps[0:1]
+    step_ref[...] = steps[0, 0:LOADS]
     column = jnp.concatenate([steps] * 16, axis=0).T[0:LOADS, 0:1]
     normal, slide_a, slide_b = (
         field_ref[rows, :] - column * residual_ref[rows, :]
@@ -353,9 +413,9 @@
         "final",
         grid=(CHUNKS,),
         in_specs=[whole(got.shape), CHUNK, CHUNK, PANEL_ROWS],
-        out_specs=[CHUNK, whole(SUMS.shape)],
-        out_shape=[FIELD, SUMS],
-    )(got, field, residual, panel_rows)
+        out_specs=[CHUNK, whole((LOADS,))],
+        out_shape=[FIELD, jax.ShapeDtypeStruct((LOADS,), F32)],
+    )(got, in_hbm(field), in_hbm(residual), panel_rows)
 
 
 def swap(blocks, axes):
@@ -369,9 +429,12 @@
     return lax.ppermute(blocks, WIDE_NARROW, up), lax.ppermute(blocks, WIDE_NARROW, down)
 
 
-def tree(place, sent):
-    low, up = lower_sums(place, swap(sent, NARROW))
-    return swap(upper_sums(place, swap(up, WIDE), low), NARROW)
+def operator(place, low, sent, near_field_of):
+    left, right = beside(low)
+    lower, up = lower_sums(place, swap(sent, NARROW))
+    near = near_field_of(left, low, right)
+    upper, near = lax.optimization_barrier((swap(up, WIDE), near))
+    return near, swap(upper_sums(place, upper, lower), NARROW)
 
 
 def body(
@@ -397,22 +460,23 @@
     )
     panel_rows = sort_panels(cluster_order[None], panel_rows)
 
+    def near_of(*target):
+        return lambda left, own, right: near_field(
+            neighbours, left, own, right, near_kernel, *target
+        )
+
     low, sent = first_coefs(field, far_basis)
-    left, right = beside(low)
-    near = near_field(
-        neighbours, left, low, right, near_kernel, approach.reshape(ROWS, 1), panel_rows
-    )
-    residual, low, sent = residual_step(tree(place, sent), near, far_basis)
-    left, right = beside(low)
-    near = near_field(neighbours, left, low, right, near_kernel)
-    sums = local_products(tree(place, sent), near, residual, far_basis)
+    near, coefs = operator(place, low, sent, near_of(approach, panel_rows))
+    residual, low, sent = residual_step(coefs, near, far_basis)
+    near, coefs = operator(place, low, sent, near_of())
+    sums = local_products(coefs, near, residual, far_basis)
 
     devices = lax.axis_size(WIDE_NARROW)
     sums = swap(jnp.broadcast_to(sums[None], (devices, 1, 2 * LOADS)), WIDE_NARROW)
     entries = COMP * PAN * devices
     updated, steps = final_step(sums, field, residual, panel_rows, entries)
     shape = (COMP, LOADS, PAN)
-    return updated.reshape(shape), residual.reshape(shape), steps[0, :LOADS]
+    return updated.reshape(shape), residual.reshape(shape), steps
 
 
 def solution(mesh):

time: 166 us -> 150 us (0.904)
  local copies, waits for them, and re-layouts: 24.2 us -> 1.65 us
  waiting for transfers between devices: 19.9 us -> 3.73 us
  Pallas kernels: 24 us -> 37.1 us
  blocking collectives: 45.3 us -> 53.7 us
  starting transfers between devices: 50.1 us -> 52.1 us
    unnamed x60 -> x24, local copies, waits for them, and re-layouts: 22.8 us -> 1.49 us
    all_to_all x5 -> x4, waiting for transfers between devices: 17.2 us -> 3.63 us  [swap(): return lax.all_to_all(blocks, axes, 0, 0)]
    ppermute x2, starting transfers between devices: 6.04 us -> 15.9 us  [beside(): lax.ppermute(blocks, WIDE_NARROW, down)]
    all_to_all x2 -> x3, blocking collectives: 45.3 us -> 53.7 us  [swap(): return lax.all_to_all(blocks, axes, 0, 0)]
    all_to_all x5 -> x4, starting transfers between devices: 39.5 us -> 32.3 us  [swap(): return lax.all_to_all(blocks, axes, 0, 0)]
    pallas_call x2, Pallas kernels: 7.26 us -> 13.5 us  [near_field(): call(near_kernel_body, 'near_field', grid=(CHUNKS,), in_specs=[SCALARS] +...]
    pallas_call x2, Pallas kernels: 4.79 us -> 8 us  [the longest x1 4.59 us: residual_step(): call(residual_kernel, 'residual', in_specs=[IN_VMEM, IN_HBM, IN_VMEM], ou...]
    ppermute x2, waiting for transfers between devices: 1.82 us -> 0.01 us  [beside(): lax.ppermute(blocks, WIDE_NARROW, down)]
  transfers between devices with their start and end apart: 9 -> 8, of which waited for: 5 -> 2; matrix products, arithmetic and copies ran while one was open for 1% -> 0% of each run, Pallas kernels for 7% -> 12%
where the time goes in v3:
time: 150 us; the launch traced here: 149 us
  blocking collectives  53.7 us (36%)
  starting transfers between devices  52.1 us (35%)
  Pallas kernels  37.1 us (25%)
  waiting for transfers between devices  3.73 us (2%)
  local copies, waits for them, and re-layouts  1.65 us (1%)
    all_to_all x3, blocking collectives, swap(): return lax.all_to_all(blocks, axes, 0, 0)  53.7 us
    all_to_all x4, starting transfers between devices, swap(): return lax.all_to_all(blocks, axes, 0, 0)  32.3 us
    ppermute x2, starting transfers between devices, beside(): lax.ppermute(blocks, WIDE_NARROW, down)  15.9 us
    pallas_call x2, Pallas kernels, near_field(): call(near_kernel_body, 'near_field', grid=(CHUNKS,), in_specs=[SCALARS] +...  13.5 us
    pallas_call x1, Pallas kernels, residual_step(): call(residual_kernel, 'residual', in_specs=[IN_VMEM, IN_HBM, IN_VMEM], ou...  4.59 us
    pallas_call x1, Pallas kernels, final_step(): call(functools.partial(final_kernel, entries), 'final', grid=(CHUNKS,), i...  4.4 us
    ppermute x2, starting transfers between devices, beside(): lax.ppermute(blocks, WIDE_NARROW, up)  3.84 us
    all_to_all x4, waiting for transfers between devices, swap(): return lax.all_to_all(blocks, axes, 0, 0)  3.63 us
  transfers between devices with their start and end apart: 8, of which 2 were waited for; matrix products, arithmetic and copies ran while one was open for 0% of the time, Pallas kernels for 12%

profile of v3, /device:TPU:1, one launch (start us, length us, event | category | flops | bytes accessed | tf_op | source)
XLA Modules:
  0.0 149.3 jit_solution(19185142415545227)
XLA Ops:
  0.6 0.0 copy-start.9
  0.6 0.0 copy-start.10
  0.7 0.0 copy-start.11
  0.7 3.4 %first_coefs.1 = (bf16[3,192,512]{2,1,0:T(8,128)(2,1)}, bf16[16,96,128]{2,1,0:T(8,128)(2,1)}) custom-call(f32[192,1536]{1,0:T(8,128)} %bitcast.7, bf16[8,1536,128]{2,1,0:T(8,128)(2,1)} %basis_ref.3), custom_call_target="tpu_custom_call" | custom-call | tf_op jit(solution)/shard_map/first_coefs/pallas_call | solution.py:117
  4.1 0.0 copy-start.8
  4.1 0.0 copy-start.5
  4.1 0.0 copy-start.6
  4.1 7.7 %all-to-all-start = ((bf16[16,96,128]{2,1,0:T(8,128)(2,1)}), bf16[16,96,128]{2,1,0:T(8,128)(2,1)S(1)}, u32[]{:S(2)}, u32[]{:S(2)}) async-start(bf16[16,96,128]{2,1,0:T(8,128)(2,1)} %get-tuple-element.18), calls=%async_computation | async-start | bytes 786432 | tf_op jit(solution)/shard_map/all_to_all | solution.py:422
  11.9 7.7 %collective-permute-start.1 = (bf16[3,192,512]{2,1,0:T(8,128)(2,1)}, bf16[3,192,512]{2,1,0:T(8,128)(2,1)S(1)}, u32[]{:S(2)}, u32[]{:S(2)}) collective-permute-start(bf16[3,192,512]{2,1,0:T(8,128)(2,1)} %get-tuple-element.20.own_hbm), channel_id=1, source_target_pairs={{1,0},{2,1},{3,2},{4,3},{5,4},{6,5},{7,6},{8,7},{9,8},{10,9},{11,1... | collective-permute-start | bytes 1769480 | tf_op jit(solution)/shard_map/ppermute | solution.py:429
  19.6 1.9 %collective-permute-start = (bf16[3,192,512]{2,1,0:T(8,128)(2,1)}, bf16[3,192,512]{2,1,0:T(8,128)(2,1)}, u32[]{:S(2)}, u32[]{:S(2)}) collective-permute-start(bf16[3,192,512]{2,1,0:T(8,128)(2,1)} %get-tuple-element.20.own_hbm), channel_id=1, source_target_pairs={{0,1},{1,2},{2,3},{3,4},{4,5},{5,6},{6,7},{7,8},{8,9},{9,10},{10,1... | collective-permute-start | bytes 1769480 | tf_op jit(solution)/shard_map/ppermute | solution.py:429
  21.5 0.0 copy-done.9
  21.5 0.0 copy-done.10
  21.6 0.0 copy-done.11
  21.6 0.1 pad.3.clone
  21.7 0.1 pad_add_fusion.place_ref
  21.8 0.0 all-to-all-done.got_ref
  21.8 1.3 lower_sums.2
  23.1 9.3 %all-to-all-start.1 = ((bf16[16,48,128]{2,1,0:T(8,128)(2,1)}), bf16[16,48,128]{2,1,0:T(8,128)(2,1)S(1)}, u32[]{:S(2)}, u32[]{:S(2)}) async-start(bf16[16,48,128]{2,1,0:T(8,128)(2,1)} %get-tuple-element.19), calls=%async_computation.1 | async-start | bytes 393216 | tf_op jit(solution)/shard_map/all_to_all | solution.py:422
  32.5 0.1 maximum_maximum_fusion.values_ref
  32.5 2.3 %sort_panels.1.rest_1_.sorted_ref = f32[8,1536]{1,0:T(8,128)S(1)} custom-call(s32[1,1536]{1,0:T(1,128)S(1)} %broadcast_in_dim.20.order_ref, f32[8,1536]{1,0:T(8,128)S(1)} %maximum_maximum_fusion.values_ref), custom_call_target="tpu_custom_call" | custom-call | tf_op jit(solution)/shard_map/sort_panels/pallas_call | solution.py:377
  34.8 0.0 collective-permute-done.1.right_hbm
  34.8 0.0 copy-start.7
  34.8 0.8 copy-done.7
  35.7 0.0 collective-permute-done.left_hbm
  35.7 0.0 copy-start
  35.7 6.9 %near_field.2.near_hbm = f32[192,1536]{1,0:T(8,128)} custom-call(s32[3,4]{1,0:T(4,128)S(1)} %copy-done.5, bf16[3,192,512]{2,1,0:T(8,128)(2,1)} %collective-permute-done.left_hbm, bf16[3,192,512]{2,1,0:T(8,128)(2,1)} %get-tuple-element.20.own_hbm, bf16[3,192,512]{2,1,0:T(8,128)(2,1)} %copy-done.7, bf16[3,4,512,512]{3,2,1,0:T(8,128)(2,1)} %kernel_hbm.3, ...), custom_call_target="tpu_custom_call" | custom-call | tf_op jit(solution)/shard_map/near_field/pallas_call | solution.py:240
  42.6 0.6 copy-done.1
  43.2 0.0 all-to-all-done.1.got_ref
  43.2 1.4 upper_sums.2
  44.6 14.9 %all_to_all.35.got_ref = bf16[16,96,128]{2,1,0:T(8,128)(2,1)S(1)} all-to-all(bf16[16,96,128]{2,1,0:T(8,128)(2,1)} %upper_sums.2), channel_id=1, replica_groups=mesh['wide_0'=8,'wide_1'=2,'narrow_0'=4,'narrow_1'=4] {'narrow_0','narro..., dimensions={0} | all-to-all | bytes 786432 | tf_op jit(solution)/shard_map/all_to_all | solution.py:422
  59.5 4.6 %residual.1 = (f32[192,1536]{1,0:T(8,128)}, bf16[3,192,512]{2,1,0:T(8,128)(2,1)}, bf16[16,96,128]{2,1,0:T(8,128)(2,1)}) custom-call(bf16[16,96,128]{2,1,0:T(8,128)(2,1)S(1)} %all_to_all.35.got_ref, f32[192,1536]{1,0:T(8,128)} %near_field.2.near_hbm, bf16[8,1536,128]{2,1,0:T(8,128)(2,1)S(1)} %copy-done), custom_call_target="tpu_custom_call" | custom-call | tf_op jit(solution)/shard_map/residual/pallas_call | solution.py:310
  64.1 3.9 %all-to-all-start.3 = ((bf16[16,96,128]{2,1,0:T(8,128)(2,1)}), bf16[16,96,128]{2,1,0:T(8,128)(2,1)S(1)}, u32[]{:S(2)}, u32[]{:S(2)}) async-start(bf16[16,96,128]{2,1,0:T(8,128)(2,1)} %get-tuple-element.24), calls=%async_computation.3 | async-start | bytes 786432 | tf_op jit(solution)/shard_map/all_to_all | solution.py:422
  68.0 8.2 %collective-permute-start.3 = (bf16[3,192,512]{2,1,0:T(8,128)(2,1)}, bf16[3,192,512]{2,1,0:T(8,128)(2,1)}, u32[]{:S(2)}, u32[]{:S(2)}) collective-permute-start(bf16[3,192,512]{2,1,0:T(8,128)(2,1)} %get-tuple-element.26.own_hbm), channel_id=1, source_target_pairs={{1,0},{2,1},{3,2},{4,3},{5,4},{6,5},{7,6},{8,7},{9,8},{10,9},{11,1... | collective-permute-start | bytes 1769480 | tf_op jit(solution)/shard_map/ppermute | solution.py:429
  76.2 1.9 %collective-permute-start.2 = (bf16[3,192,512]{2,1,0:T(8,128)(2,1)}, bf16[3,192,512]{2,1,0:T(8,128)(2,1)}, u32[]{:S(2)}, u32[]{:S(2)}) collective-permute-start(bf16[3,192,512]{2,1,0:T(8,128)(2,1)} %get-tuple-element.26.own_hbm), channel_id=1, source_target_pairs={{0,1},{1,2},{2,3},{3,4},{4,5},{5,6},{6,7},{7,8},{8,9},{9,10},{10,1... | collective-permute-start | bytes 1769480 | tf_op jit(solution)/shard_map/ppermute | solution.py:429
  78.1 0.0 all-to-all-done.3.got_ref
  78.1 1.4 lower_sums.3
  79.5 11.4 %all-to-all-start.4 = ((bf16[16,48,128]{2,1,0:T(8,128)(2,1)}), bf16[16,48,128]{2,1,0:T(8,128)(2,1)S(1)}, u32[]{:S(2)}, u32[]{:S(2)}) async-start(bf16[16,48,128]{2,1,0:T(8,128)(2,1)} %get-tuple-element.25), calls=%async_computation.4 | async-start | bytes 393216 | tf_op jit(solution)/shard_map/all_to_all | solution.py:422
  90.9 0.0 collective-permute-done.3.right_hbm
  90.9 0.1 collective-permute-done.2.left_hbm
  91.0 6.6 %near_field.3.near_ref = f32[192,1536]{1,0:T(8,128)} custom-call(s32[3,4]{1,0:T(4,128)S(1)} %copy-done.5, bf16[3,192,512]{2,1,0:T(8,128)(2,1)} %collective-permute-done.2.left_hbm, bf16[3,192,512]{2,1,0:T(8,128)(2,1)} %get-tuple-element.26.own_hbm, bf16[3,192,512]{2,1,0:T(8,128)(2,1)} %collective-permute-done.3.right_hbm, bf16[3,4,512,512]{3,2,1,0:T(8,128)(2,1)} %kernel_hbm.3), custom_call_target="tpu_custom_call" | custom-call | tf_op jit(solution)/shard_map/near_field/pallas_call | solution.py:240
  97.6 3.6 %all-to-all-done.4.got_ref = bf16[16,48,128]{2,1,0:T(8,128)(2,1)S(1)} async-done(((bf16[16,48,128]{2,1,0:T(8,128)(2,1)}), bf16[16,48,128]{2,1,0:T(8,128)(2,1)S(1)}, u32[]{:S(2)}, u32[]{:S(2)}) %all-to-all-start.4) | async-done | bytes 196640 | tf_op jit(solution)/shard_map/all_to_all | solution.py:422
  101.2 0.0 copy-done.4
  101.2 1.4 upper_sums.3
  102.6 14.1 %all_to_all.36.got_ref = bf16[16,96,128]{2,1,0:T(8,128)(2,1)S(1)} all-to-all(bf16[16,96,128]{2,1,0:T(8,128)(2,1)} %upper_sums.3), channel_id=1, replica_groups=mesh['wide_0'=8,'wide_1'=2,'narrow_0'=4,'narrow_1'=4] {'narrow_0','narro..., dimensions={0} | all-to-all | bytes 786432 | tf_op jit(solution)/shard_map/all_to_all | solution.py:422
  116.7 3.5 %products.1 = f32[1,128]{1,0:T(1,128)S(1)} custom-call(bf16[16,96,128]{2,1,0:T(8,128)(2,1)S(1)} %all_to_all.36.got_ref, f32[192,1536]{1,0:T(8,128)} %near_field.3.near_ref, f32[192,1536]{1,0:T(8,128)} %get-tuple-element.30.residual_ref, bf16[8,1536,128]{2,1,0:T(8,128)(2,1)S(1)} %copy-done), custom_call_target="tpu_custom_call" | custom-call | tf_op jit(solution)/shard_map/products/pallas_call | solution.py:349
  120.2 0.1 broadcast_in_dim.25
  120.3 24.7 %all_to_all.37.got_ref = f32[256,1,128]{2,1,0:T(1,128)S(1)} all-to-all(f32[256,1,128]{2,1,0:T(1,128)S(1)} %broadcast_in_dim.25), channel_id=1, replica_groups=mesh['wide_0'=8,'wide_1'=2,'narrow_0'=4,'narrow_1'=4] {'wide_0','wide_1'..., dimensions={0} | all-to-all | bytes 262144 | tf_op jit(solution)/shard_map/all_to_all | solution.py:422
  144.9 4.4 %final.1 = (f32[192,1536]{1,0:T(8,128)}, f32[64]{0:T(128)}) custom-call(f32[256,1,128]{2,1,0:T(1,128)S(1)} %all_to_all.37.got_ref, f32[192,1536]{1,0:T(8,128)} %bitcast.8, f32[192,1536]{1,0:T(8,128)} %get-tuple-element.30.residual_ref, f32[8,1536]{1,0:T(8,128)S(1)} %copy-done.2), custom_call_target="tpu_custom_call" | custom-call | tf_op jit(solution)/shard_map/final/pallas_call | solution.py:411
  (15 shorter events, 0.0 us)
Async XLA Ops:
  0.6 20.9 %copy-start.9 = (f32[1536]{0:T(1024)S(1)}, f32[1536]{0:T(1024)}, u32[]{:S(2)}) copy-start(f32[1536]{0:T(1024)} %param.14) | copy-start | bytes 18436
  0.6 20.9 %copy-start.10 = (s32[1536]{0:T(1024)S(1)}, s32[1536]{0:T(1024)}, u32[]{:S(2)}) copy-start(s32[1536]{0:T(1024)} %param.16) | copy-start | bytes 18436
  0.7 20.9 %copy-start.11 = (s32[1536]{0:T(1024)S(1)}, s32[1536]{0:T(1024)}, u32[]{:S(2)}) copy-start(s32[1536]{0:T(1024)} %param.15) | copy-start | bytes 18436
  4.1 28.4 %copy-start.8 = (f32[3,1536]{1,0:T(4,128)S(1)}, f32[3,1536]{1,0:T(4,128)}, u32[]{:S(2)}) copy-start(f32[3,1536]{1,0:T(4,128)} %param.13) | copy-start | bytes 55300
  4.1 31.6 %copy-start.5 = (s32[3,4]{1,0:T(4,128)S(1)}, s32[3,4]{1,0:T(4,128)}, u32[]{:S(2)}) copy-start(s32[3,4]{1,0:T(4,128)} %slots_ref.3) | copy-start | bytes 148
  4.1 31.6 %copy-start.6 = (f32[3,64]{1,0:T(4,128)S(1)}, f32[3,64]{1,0:T(4,128)}, u32[]{:S(2)}) copy-start(f32[3,64]{1,0:T(4,128)} %rest_0_.1) | copy-start | bytes 2308
  4.1 17.7 %all-to-all-start = ((bf16[16,96,128]{2,1,0:T(8,128)(2,1)}), bf16[16,96,128]{2,1,0:T(8,128)(2,1)S(1)}, u32[]{:S(2)}, u32[]{:S(2)}) async-start(bf16[16,96,128]{2,1,0:T(8,128)(2,1)} %get-tuple-element.18), calls=%async_computation | async-start | bytes 786432 | tf_op jit(solution)/shard_map/all_to_all | solution.py:422
  11.9 23.0 %collective-permute-start.1 = (bf16[3,192,512]{2,1,0:T(8,128)(2,1)}, bf16[3,192,512]{2,1,0:T(8,128)(2,1)S(1)}, u32[]{:S(2)}, u32[]{:S(2)}) collective-permute-start(bf16[3,192,512]{2,1,0:T(8,128)(2,1)} %get-tuple-element.20.own_hbm), channel_id=1, source_target_pairs={{1,0},{2,1},{3,2},{4,3},{5,4},{6,5},{7,6},{8,7},{9,8},{10,9},{11,1... | collective-permute-start | bytes 1769480 | tf_op jit(solution)/shard_map/ppermute | solution.py:429
  19.6 16.1 %collective-permute-start = (bf16[3,192,512]{2,1,0:T(8,128)(2,1)}, bf16[3,192,512]{2,1,0:T(8,128)(2,1)}, u32[]{:S(2)}, u32[]{:S(2)}) collective-permute-start(bf16[3,192,512]{2,1,0:T(8,128)(2,1)} %get-tuple-element.20.own_hbm), channel_id=1, source_target_pairs={{0,1},{1,2},{2,3},{3,4},{4,5},{5,6},{6,7},{7,8},{8,9},{9,10},{10,1... | collective-permute-start | bytes 1769480 | tf_op jit(solution)/shard_map/ppermute | solution.py:429
  23.1 20.1 %all-to-all-start.1 = ((bf16[16,48,128]{2,1,0:T(8,128)(2,1)}), bf16[16,48,128]{2,1,0:T(8,128)(2,1)S(1)}, u32[]{:S(2)}, u32[]{:S(2)}) async-start(bf16[16,48,128]{2,1,0:T(8,128)(2,1)} %get-tuple-element.19), calls=%async_computation.1 | async-start | bytes 393216 | tf_op jit(solution)/shard_map/all_to_all | solution.py:422
  34.8 8.4 %copy-start.3 = (bf16[16,48,128]{2,1,0:T(8,128)(2,1)S(1)}, bf16[16,48,128]{2,1,0:T(8,128)(2,1)}, u32[]{:S(2)}) copy-start(bf16[16,48,128]{2,1,0:T(8,128)(2,1)} %get-tuple-element.22.low_ref) | copy-start | bytes 589828
  34.8 0.8 copy-start.7
  35.7 23.8 %copy-start = (bf16[8,1536,128]{2,1,0:T(8,128)(2,1)S(1)}, bf16[8,1536,128]{2,1,0:T(8,128)(2,1)}, u32[]{:S(2)}) copy-start(bf16[8,1536,128]{2,1,0:T(8,128)(2,1)} %basis_ref.3) | copy-start | bytes 9437188
  42.6 0.6 copy-start.1
  64.1 14.0 %all-to-all-start.3 = ((bf16[16,96,128]{2,1,0:T(8,128)(2,1)}), bf16[16,96,128]{2,1,0:T(8,128)(2,1)S(1)}, u32[]{:S(2)}, u32[]{:S(2)}) async-start(bf16[16,96,128]{2,1,0:T(8,128)(2,1)} %get-tuple-element.24), calls=%async_computation.3 | async-start | bytes 786432 | tf_op jit(solution)/shard_map/all_to_all | solution.py:422
  68.0 23.0 %collective-permute-start.3 = (bf16[3,192,512]{2,1,0:T(8,128)(2,1)}, bf16[3,192,512]{2,1,0:T(8,128)(2,1)}, u32[]{:S(2)}, u32[]{:S(2)}) collective-permute-start(bf16[3,192,512]{2,1,0:T(8,128)(2,1)} %get-tuple-element.26.own_hbm), channel_id=1, source_target_pairs={{1,0},{2,1},{3,2},{4,3},{5,4},{6,5},{7,6},{8,7},{9,8},{10,9},{11,1... | collective-permute-start | bytes 1769480 | tf_op jit(solution)/shard_map/ppermute | solution.py:429
  76.2 14.8 %collective-permute-start.2 = (bf16[3,192,512]{2,1,0:T(8,128)(2,1)}, bf16[3,192,512]{2,1,0:T(8,128)(2,1)}, u32[]{:S(2)}, u32[]{:S(2)}) collective-permute-start(bf16[3,192,512]{2,1,0:T(8,128)(2,1)} %get-tuple-element.26.own_hbm), channel_id=1, source_target_pairs={{0,1},{1,2},{2,3},{3,4},{4,5},{5,6},{6,7},{7,8},{8,9},{9,10},{10,1... | collective-permute-start | bytes 1769480 | tf_op jit(solution)/shard_map/ppermute | solution.py:429
  79.5 21.8 %all-to-all-start.4 = ((bf16[16,48,128]{2,1,0:T(8,128)(2,1)}), bf16[16,48,128]{2,1,0:T(8,128)(2,1)S(1)}, u32[]{:S(2)}, u32[]{:S(2)}) async-start(bf16[16,48,128]{2,1,0:T(8,128)(2,1)} %get-tuple-element.25), calls=%async_computation.4 | async-start | bytes 393216 | tf_op jit(solution)/shard_map/all_to_all | solution.py:422
  90.9 10.3 %copy-start.4 = (bf16[16,48,128]{2,1,0:T(8,128)(2,1)S(1)}, bf16[16,48,128]{2,1,0:T(8,128)(2,1)}, u32[]{:S(2)}) copy-start(bf16[16,48,128]{2,1,0:T(8,128)(2,1)} %get-tuple-element.28.low_ref) | copy-start | bytes 589828
  116.7 28.2 %copy-start.2 = (f32[8,1536]{1,0:T(8,128)S(1)}, f32[8,1536]{1,0:T(8,128)}, u32[]{:S(2)}) copy-start(f32[8,1536]{1,0:T(8,128)} %copy-done.1) | copy-start | bytes 147460

commit v4 on v3

--- a/solution.py
+++ b/solution.py
@@ -62,51 +62,58 @@
 IN_VMEM = pl.BlockSpec(memory_space=pltpu.VMEM)
 IN_HBM = pl.BlockSpec(memory_space=pltpu.HBM)
 CHUNK = pl.BlockSpec((ROWS, BLK), lambda b: (0, b))
-BASIS = pl.BlockSpec((LEVELS, BLK, RANK), lambda b: (0, b, 0))
 PANEL_ROWS = pl.BlockSpec((8, BLK), lambda b: (0, b))
-BLOCKWISE = pl.BlockSpec((1, ROWS, BLK), lambda b: (b, 0, 0))
-
-
-def add_coefs(chunk, values, basis_ref, acc_ref, sent_ref):
-    for level in range(HALF):
-        pair = jnp.concatenate([basis_ref[level], basis_ref[HALF + level]], axis=1)
-        part = jnp.dot(values, pair, preferred_element_type=F32)
-        acc_ref[level] = part if chunk == 0 else acc_ref[level] + part
-    if chunk < CHUNKS - 1:
-        return
-    for level in range(HALF):
-        for quarter in range(QUARTERS):
-            rows = pl.ds(quarter * PART, PART)
-            slot = level * QUARTERS + quarter
-            sent_ref[slot, 0:PART, :] = acc_ref[level, rows, 0:RANK].astype(BF16)
-            sent_ref[slot, PART : 2 * PART, :] = acc_ref[level, rows, RANK : 2 * RANK].astype(BF16)
-
-
-def coef_kernel(field_hbm, basis_hbm, low_ref, sent_ref, field_ref, basis_ref, acc_ref, sems):
-    copies = []
+
+
+def send_coefs(level, values, pair, sent_ref, sent_hbm, sem):
+    coefs = jnp.dot(values, pair, preferred_element_type=F32).astype(BF16)
+    for quarter in range(QUARTERS):
+        rows = slice(quarter * PART, (quarter + 1) * PART)
+        slot = level * QUARTERS + quarter
+        sent_ref[slot, 0:PART, :] = coefs[rows, 0:RANK]
+        sent_ref[slot, PART : 2 * PART, :] = coefs[rows, RANK : 2 * RANK]
+    slots = pl.ds(level * QUARTERS, QUARTERS)
+    copy = pltpu.make_async_copy(sent_ref.at[slots], sent_hbm.at[slots], sem)
+    copy.start()
+    return copy
+
+
+def coef_kernel(field_hbm, basis_hbm, low_hbm, sent_hbm, *scratch):
+    field_ref, low_ref, basis_ref, sent_ref, field_sems, basis_sems, low_sems, sent_sems = scratch
+    fields, bases, leaving = [], [], []
     for chunk in range(CHUNKS):
         panels = pl.ds(chunk * BLK, BLK)
-        copies.append(
-            (
-                pltpu.make_async_copy(
-                    field_hbm.at[:, panels], field_ref.at[chunk], sems.at[0, chunk]
-                ),
-                pltpu.make_async_copy(
-                    basis_hbm.at[:, panels, :], basis_ref.at[chunk], sems.at[1, chunk]
-                ),
+        fields.append(
+            pltpu.make_async_copy(
+                field_hbm.at[:, panels], field_ref.at[chunk], field_sems.at[chunk]
             )
         )
-        for copy in copies[-1]:
+        fields[-1].start()
+    for level in range(HALF):
+        bases.append(
+            [
+                pltpu.make_async_copy(basis_hbm.at[at], basis_ref.at[at], basis_sems.at[at])
+                for at in (level, HALF + level)
+            ]
+        )
+        for copy in bases[-1]:
             copy.start()
     for chunk in range(CHUNKS):
-        for copy in copies[chunk]:
+        fields[chunk].wait()
+        low_ref[chunk] = field_ref[chunk].astype(BF16)
+        copy = pltpu.make_async_copy(low_ref.at[chunk], low_hbm.at[chunk], low_sems.at[chunk])
+        copy.start()
+        leaving.append(copy)
+    values = jnp.concatenate([low_ref[chunk] for chunk in range(CHUNKS)], axis=1)
+    for level in range(HALF):
+        for copy in bases[level]:
             copy.wait()
-        values = field_ref[chunk].astype(BF16)
-        low_ref[chunk] = values
-        add_coefs(chunk, values, basis_ref.at[chunk], acc_ref, sent_ref)
-
-
-ACC = pltpu.VMEM((HALF, ROWS, 2 * RANK), F32)
+        pair = jnp.concatenate([basis_ref[level], basis_ref[HALF + level]], axis=1)
+        leaving.append(send_coefs(level, values, pair, sent_ref, sent_hbm, sent_sems.at[level]))
+    for copy in leaving:
+        copy.wait()
+
+
 SENT = pltpu.HBM((GROUP, 2 * PART, RANK), BF16)
 BLOCKS = pltpu.HBM((CHUNKS, ROWS, BLK), BF16)
 FIELD = pltpu.HBM((ROWS, PAN), F32)
@@ -118,21 +125,36 @@
         coef_kernel,
         "first_coefs",
         in_specs=[IN_HBM] * 2,
-        out_specs=[IN_VMEM] * 2,
+        out_specs=[IN_HBM] * 2,
         out_shape=[BLOCKS, SENT],
         scratch_shapes=[
             pltpu.VMEM((CHUNKS, ROWS, BLK), F32),
-            pltpu.VMEM((CHUNKS, LEVELS, BLK, RANK), BF16),
-            ACC,
-            pltpu.SemaphoreType.DMA((2, CHUNKS)),
+            pltpu.VMEM(BLOCKS.shape, BF16),
+            pltpu.VMEM((LEVELS, PAN, RANK), BF16),
+            pltpu.VMEM(SENT.shape, BF16),
+            pltpu.SemaphoreType.DMA((CHUNKS,)),
+            pltpu.SemaphoreType.DMA((LEVELS,)),
+            pltpu.SemaphoreType.DMA((CHUNKS,)),
+            pltpu.SemaphoreType.DMA((HALF,)),
         ],
     )(in_hbm(field), in_hbm(far_basis))
 
 
-def lower_kernel(place_ref, got_ref, low_ref, up_ref):
+LOWER, UPPER = pl.ds(0, PART), pl.ds(PART, PART)
+
+
+def lower_kernel(place_ref, got_ref, back_hbm, up_hbm, low_ref, up_ref, sems):
+    total = got_ref[0, UPPER, :].astype(F32)
+    for k in range(1, GROUP):
+        total += got_ref[k, UPPER, :].astype(F32)
+    total = total.astype(BF16)
+    for k in range(GROUP):
+        up_ref[k] = total
+    up_copy = pltpu.make_async_copy(up_ref, up_hbm, sems.at[0])
+    up_copy.start()
     level = place_ref[0] // QUARTERS
     width = 1
-    sums = [got_ref[k, 0:PART, :].astype(F32) for k in range(GROUP)]
+    sums = [got_ref[k, LOWER, :].astype(F32) for k in range(GROUP)]
     while width < GROUP:
         sums = [sums[2 * k] + sums[2 * k + 1] for k in range(len(sums) // 2)]
         width *= 2
@@ -143,26 +165,29 @@
             for k in range(GROUP):
                 low_ref[k] = (sums[k // width] * gain(own_level)).astype(BF16)
 
-    total = got_ref[0, PART : 2 * PART, :].astype(F32)
-    for k in range(1, GROUP):
-        total += got_ref[k, PART : 2 * PART, :].astype(F32)
-    for k in range(GROUP):
-        up_ref[k] = total.astype(BF16)
+    low_copy = pltpu.make_async_copy(low_ref, back_hbm.at[:, LOWER, :], sems.at[1])
+    low_copy.start()
+    up_copy.wait()
+    low_copy.wait()
 
 
 def lower_sums(place, got):
-    part = pltpu.HBM((GROUP, PART, RANK), BF16)
+    part = (GROUP, PART, RANK)
     return call(
         lower_kernel,
         "lower_sums",
-        in_specs=[SCALARS, whole(SENT.shape)],
-        out_specs=[whole(part.shape)] * 2,
-        out_shape=[part] * 2,
-        grid=(1,),
-    )(place, got)
-
-
-def upper_kernel(place_ref, got_ref, low_ref, sent_ref):
+        in_specs=[SCALARS, IN_VMEM],
+        out_specs=[IN_HBM] * 2,
+        out_shape=[SENT, pltpu.HBM(part, BF16)],
+        scratch_shapes=[
+            pltpu.VMEM(part, BF16),
+            pltpu.VMEM(part, BF16),
+            pltpu.SemaphoreType.DMA((2,)),
+        ],
+    )(place, in_vmem(got))
+
+
+def upper_kernel(place_ref, got_ref, _, back_hbm, up_ref, sem):
     level = place_ref[0] // QUARTERS
     shift = level + 1
     own = lax.shift_right_logical(place_ref[1], shift)
@@ -175,19 +200,25 @@
         scale = jnp.where(level == other, jnp.float32(gain(HALF + other)), scale)
     total = (total * scale).astype(BF16)
     for k in range(GROUP):
-        sent_ref[k, 0:PART, :] = low_ref[k]
-        sent_ref[k, PART : 2 * PART, :] = total
-
-
-def upper_sums(place, got, low):
+        up_ref[k] = total
+    copy = pltpu.make_async_copy(up_ref, back_hbm.at[:, UPPER, :], sem.at[0])
+    copy.start()
+    copy.wait()
+
+
+def upper_sums(place, got, back):
     return call(
         upper_kernel,
         "upper_sums",
-        in_specs=[SCALARS, whole(got.shape), whole(low.shape)],
-        out_specs=whole(SENT.shape),
+        in_specs=[SCALARS, IN_VMEM, IN_HBM],
+        out_specs=IN_HBM,
         out_shape=SENT,
-        grid=(1,),
-    )(place, got, low)
+        input_output_aliases={2: 0},
+        scratch_shapes=[
+            pltpu.VMEM((GROUP, PART, RANK), BF16),
+            pltpu.SemaphoreType.DMA((1,)),
+        ],
+    )(place, in_vmem(got), in_hbm(back))
 
 
 def near_kernel_body(slots_ref, left_hbm, own_hbm, right_hbm, kernel_hbm, *rest):
@@ -272,36 +303,39 @@
 COEFS = pltpu.VMEM((ROWS, LEVELS * RANK), BF16)
 
 
-def residual_kernel(
-    got_ref, near_hbm, basis_ref, out_hbm, low_hbm, sent_ref, *scratch
-):
-    near_ref, out_ref, low_ref, coef_ref, acc_ref, sems = scratch
-
-    arriving, leaving = [], []
+def start_chunks(source_hbm, ref, sems, row):
+    copies = []
     for chunk in range(CHUNKS):
-        panels = pl.ds(chunk * BLK, BLK)
         copy = pltpu.make_async_copy(
-            near_hbm.at[:, panels], near_ref.at[chunk], sems.at[0, chunk]
+            source_hbm.at[:, pl.ds(chunk * BLK, BLK)], ref.at[chunk], sems.at[row, chunk]
         )
         copy.start()
-        arriving.append(copy)
+        copies.append(copy)
+    return copies
+
+
+def residual_kernel(got_ref, near_hbm, basis_ref, out_hbm, low_hbm, sent_hbm, *scratch):
+    near_ref, out_ref, low_ref, sent_ref, coef_ref, sems, sent_sems = scratch
+    arriving = start_chunks(near_hbm, near_ref, sems, 0)
+    leaving = []
     unpack(got_ref, coef_ref)
     for chunk in range(CHUNKS):
         panels = pl.ds(chunk * BLK, BLK)
-        part = basis_ref.at[:, panels, :]
-        far = far_field(coef_ref, part)
+        far = far_field(coef_ref, basis_ref.at[:, panels, :])
         arriving[chunk].wait()
         residual = far + near_ref[chunk]
         out_ref[chunk] = residual
-        values = residual.astype(BF16)
-        low_ref[chunk] = values
+        low_ref[chunk] = residual.astype(BF16)
         for copy in (
             pltpu.make_async_copy(out_ref.at[chunk], out_hbm.at[:, panels], sems.at[1, chunk]),
             pltpu.make_async_copy(low_ref.at[chunk], low_hbm.at[chunk], sems.at[2, chunk]),
         ):
             copy.start()
             leaving.append(copy)
-        add_coefs(chunk, values, part, acc_ref, sent_ref)
+    values = jnp.concatenate([low_ref[chunk] for chunk in range(CHUNKS)], axis=1)
+    for level in range(HALF):
+        pair = jnp.concatenate([basis_ref[level], basis_ref[HALF + level]], axis=1)
+        leaving.append(send_coefs(level, values, pair, sent_ref, sent_hbm, sent_sems.at[level]))
     for copy in leaving:
         copy.wait()
 
@@ -311,49 +345,51 @@
         residual_kernel,
         "residual",
         in_specs=[IN_VMEM, IN_HBM, IN_VMEM],
-        out_specs=[IN_HBM, IN_HBM, IN_VMEM],
+        out_specs=[IN_HBM] * 3,
         out_shape=[FIELD, BLOCKS, SENT],
         scratch_shapes=[
             pltpu.VMEM((CHUNKS, ROWS, BLK), F32),
             pltpu.VMEM((CHUNKS, ROWS, BLK), F32),
-            pltpu.VMEM((CHUNKS, ROWS, BLK), BF16),
+            pltpu.VMEM(BLOCKS.shape, BF16),
+            pltpu.VMEM(SENT.shape, BF16),
             COEFS,
-            ACC,
             pltpu.SemaphoreType.DMA((3, CHUNKS)),
+            pltpu.SemaphoreType.DMA((HALF,)),
         ],
     )(in_vmem(got), in_hbm(near), in_vmem(far_basis))
 
 
-def product_kernel(got_ref, near_ref, residual_ref, basis_ref, sums_ref, coef_ref, acc_ref):
-    step = pl.program_id(0)
-
-    @pl.when(step == 0)
-    def _():
-        unpack(got_ref, coef_ref)
-        acc_ref[...] = jnp.zeros_like(acc_ref)
-
-    image = far_field(coef_ref, basis_ref) + near_ref[...]
-    for place, product in enumerate((residual_ref[...] * image, image * image)):
-        by_load = product[0:LOADS] + product[LOADS : 2 * LOADS] + product[2 * LOADS : ROWS]
-        folded = by_load[:, 0:128]
-        for lane in range(128, BLK, 128):
-            folded += by_load[:, lane : lane + 128]
-        acc_ref[place * LOADS : (place + 1) * LOADS, :] += folded
-
-    @pl.when(step == CHUNKS - 1)
-    def _():
-        sums_ref[...] = jnp.sum(acc_ref[...].T, axis=0, keepdims=True)
+def product_kernel(got_ref, near_hbm, residual_hbm, basis_ref, sums_ref, *scratch):
+    near_ref, residual_ref, coef_ref, sems = scratch
+    nears = start_chunks(near_hbm, near_ref, sems, 0)
+    residuals = start_chunks(residual_hbm, residual_ref, sems, 1)
+    unpack(got_ref, coef_ref)
+    totals = [jnp.zeros((LOADS, 128), F32)] * 2
+    for chunk in range(CHUNKS):
+        far = far_field(coef_ref, basis_ref.at[:, pl.ds(chunk * BLK, BLK), :])
+        nears[chunk].wait()
+        residuals[chunk].wait()
+        image = far + near_ref[chunk]
+        for place, product in enumerate((residual_ref[chunk] * image, image * image)):
+            by_load = product[0:LOADS] + product[LOADS : 2 * LOADS] + product[2 * LOADS : ROWS]
+            for lane in range(0, BLK, 128):
+                totals[place] += by_load[:, lane : lane + 128]
+    sums_ref[...] = jnp.sum(jnp.concatenate(totals, axis=0).T, axis=0, keepdims=True)
 
 
 def local_products(got, near, residual, far_basis):
     return call(
         product_kernel,
         "products",
-        grid=(CHUNKS,),
-        in_specs=[whole(SENT.shape), CHUNK, CHUNK, BASIS],
-        out_specs=whole(SUMS.shape),
+        in_specs=[IN_VMEM, IN_HBM, IN_HBM, IN_VMEM],
+        out_specs=IN_VMEM,
         out_shape=SUMS,
-        scratch_shapes=[COEFS, pltpu.VMEM((2 * LOADS, 128), F32)],
+        scratch_shapes=[
+            pltpu.VMEM((CHUNKS, ROWS, BLK), F32),
+            pltpu.VMEM((CHUNKS, ROWS, BLK), F32),
+            COEFS,
+            pltpu.SemaphoreType.DMA((2, CHUNKS)),
+        ],
     )(in_vmem(got), in_hbm(near), in_hbm(residual), in_vmem(far_basis))
 
 
@@ -380,42 +416,54 @@
         grid=(CHUNKS,),
         in_specs=[pl.BlockSpec((1, BLK), lambda b: (0, b)), whole(values.shape)],
         out_specs=PANEL_ROWS,
-        out_shape=jax.ShapeDtypeStruct(values.shape, F32),
+        out_shape=pltpu.HBM(values.shape, F32),
     )(order, values)
 
 
-def final_kernel(entries, got_ref, field_ref, residual_ref, sorted_ref, out_ref, step_ref):
+def final_kernel(entries, got_ref, field_ref, residual_ref, sorted_ref, out_hbm, *rest):
+    step_ref, out_ref, sems = rest
     sums = jnp.sum(got_ref[...], axis=0) * (1.0 / entries)
     sums = jnp.broadcast_to(sums, (8, 2 * LOADS))
     square = jnp.concatenate([sums[:, LOADS:], sums[:, LOADS:]], axis=1)
     steps = sums / (square + 1e-06)
     step_ref[...] = steps[0, 0:LOADS]
     column = jnp.concatenate([steps] * 16, axis=0).T[0:LOADS, 0:1]
-    normal, slide_a, slide_b = (
-        field_ref[rows, :] - column * residual_ref[rows, :]
-        for rows in (slice(c * LOADS, (c + 1) * LOADS) for c in range(COMP))
-    )
-    coeff = sorted_ref[3:4, :]
-    live = sorted_ref[4:5, :]
-    slip = jnp.sqrt(slide_a * slide_a + slide_b * slide_b + SLIP_EPS)
-    stick = slip <= coeff * normal
-    slid = jnp.maximum((normal + coeff * slip) / (1.0 + coeff * coeff), 0.0)
-    pressed = jnp.where(stick, normal, slid)
-    factor = jnp.where(stick, jnp.ones_like(slip), coeff * pressed / slip)
-    out_ref[0:LOADS, :] = pressed * live
-    out_ref[LOADS : 2 * LOADS, :] = factor * slide_a * live
-    out_ref[2 * LOADS : ROWS, :] = factor * slide_b * live
+    comps = [slice(c * LOADS, (c + 1) * LOADS) for c in range(COMP)]
+    leaving = []
+    for chunk in range(CHUNKS):
+        panels = pl.ds(chunk * BLK, BLK)
+        normal, slide_a, slide_b = (
+            field_ref[rows, panels] - column * residual_ref[rows, panels] for rows in comps
+        )
+        coeff = sorted_ref[3:4, panels]
+        live = sorted_ref[4:5, panels]
+        slip = jnp.sqrt(slide_a * slide_a + slide_b * slide_b + SLIP_EPS)
+        stick = slip <= coeff * normal
+        slid = jnp.maximum((normal + coeff * slip) / (1.0 + coeff * coeff), 0.0)
+        pressed = jnp.where(stick, normal, slid)
+        factor = jnp.where(stick, jnp.ones_like(slip), coeff * pressed / slip)
+        out_ref[chunk, comps[0], :] = pressed * live
+        out_ref[chunk, comps[1], :] = factor * slide_a * live
+        out_ref[chunk, comps[2], :] = factor * slide_b * live
+        copy = pltpu.make_async_copy(out_ref.at[chunk], out_hbm.at[:, panels], sems.at[chunk])
+        copy.start()
+        leaving.append(copy)
+    for copy in leaving:
+        copy.wait()
 
 
 def final_step(got, field, residual, panel_rows, entries):
     return call(
         functools.partial(final_kernel, entries),
         "final",
-        grid=(CHUNKS,),
-        in_specs=[whole(got.shape), CHUNK, CHUNK, PANEL_ROWS],
-        out_specs=[CHUNK, whole((LOADS,))],
+        in_specs=[IN_VMEM] * 4,
+        out_specs=[IN_HBM, IN_VMEM],
         out_shape=[FIELD, jax.ShapeDtypeStruct((LOADS,), F32)],
-    )(got, in_hbm(field), in_hbm(residual), panel_rows)
+        scratch_shapes=[
+            pltpu.VMEM((CHUNKS, ROWS, BLK), F32),
+            pltpu.SemaphoreType.DMA((CHUNKS,)),
+        ],
+    )(in_vmem(got), in_vmem(field), in_vmem(residual), in_vmem(panel_rows))
 
 
 def swap(blocks, axes):
@@ -429,12 +477,11 @@
     return lax.ppermute(blocks, WIDE_NARROW, up), lax.ppermute(blocks, WIDE_NARROW, down)
 
 
-def operator(place, low, sent, near_field_of):
-    left, right = beside(low)
+def operator(place, low, sent, *early):
+    sides = beside(low)
     lower, up = lower_sums(place, swap(sent, NARROW))
-    near = near_field_of(left, low, right)
-    upper, near = lax.optimization_barrier((swap(up, WIDE), near))
-    return near, swap(upper_sums(place, upper, lower), NARROW)
+    upper, sides, early = lax.optimization_barrier((swap(up, WIDE), sides, early))
+    return sides, swap(upper_sums(place, upper, lower), NARROW), early
 
 
 def body(
@@ -460,15 +507,14 @@
     )
     panel_rows = sort_panels(cluster_order[None], panel_rows)
 
-    def near_of(*target):
-        return lambda left, own, right: near_field(
-            neighbours, left, own, right, near_kernel, *target
-        )
-
     low, sent = first_coefs(field, far_basis)
-    near, coefs = operator(place, low, sent, near_of(approach, panel_rows))
+    (left, right), coefs, (panel_rows,) = operator(place, low, sent, panel_rows)
+    near = near_field(
+        neighbours, left, low, right, near_kernel, approach, in_hbm(panel_rows)
+    )
     residual, low, sent = residual_step(coefs, near, far_basis)
-    near, coefs = operator(place, low, sent, near_of())
+    (left, right), coefs, _ = operator(place, low, sent)
+    near = near_field(neighbours, left, low, right, near_kernel)
     sums = local_products(coefs, near, residual, far_basis)
 
     devices = lax.axis_size(WIDE_NARROW)

time: 150 us -> 138 us (0.920)
  blocking collectives: 53.7 us -> 20.6 us
  waiting for transfers between devices: 3.73 us -> 22.3 us
  starting transfers between devices: 52.1 us -> 56.8 us
    all_to_all x3 -> x1, blocking collectives: 53.7 us -> 20.6 us  [swap(): return lax.all_to_all(blocks, axes, 0, 0)]
    all_to_all x4 -> x6, waiting for transfers between devices: 3.63 us -> 16.4 us  [swap(): return lax.all_to_all(blocks, axes, 0, 0)]
    all_to_all x4 -> x6, starting transfers between devices: 32.3 us -> 37.7 us  [swap(): return lax.all_to_all(blocks, axes, 0, 0)]
    ppermute x2, waiting for transfers between devices: 0.01 us -> 4.52 us  [beside(): lax.ppermute(blocks, WIDE_NARROW, down)]
  transfers between devices with their start and end apart: 8 -> 10, of which waited for: 2 -> 6; matrix products, arithmetic and copies ran while one was open for 0% -> 0% of each run, Pallas kernels for 12% -> 14%
where the time goes in v4:
time: 138 us; the launch traced here: 137 us
  starting transfers between devices  56.8 us (41%)
  Pallas kernels  36.1 us (26%)
  waiting for transfers between devices  22.3 us (16%)
  blocking collectives  20.6 us (15%)
    all_to_all x6, starting transfers between devices, swap(): return lax.all_to_all(blocks, axes, 0, 0)  37.7 us
    all_to_all x1, blocking collectives, swap(): return lax.all_to_all(blocks, axes, 0, 0)  20.6 us
    all_to_all x6, waiting for transfers between devices, swap(): return lax.all_to_all(blocks, axes, 0, 0)  16.4 us
    ppermute x2, starting transfers between devices, beside(): lax.ppermute(blocks, WIDE_NARROW, down)  15.2 us
    pallas_call x2, Pallas kernels, near_field(): call(near_kernel_body, 'near_field', grid=(CHUNKS,), in_specs=[SCALARS] +...  13.6 us
    pallas_call x1, Pallas kernels, first_coefs(): call(coef_kernel, 'first_coefs', in_specs=[IN_HBM] * 2, out_specs=[IN_HBM...  4.75 us
    ppermute x2, waiting for transfers between devices, beside(): lax.ppermute(blocks, WIDE_NARROW, down)  4.52 us
    pallas_call x1, Pallas kernels, residual_step(): call(residual_kernel, 'residual', in_specs=[IN_VMEM, IN_HBM, IN_VMEM], ou...  3.92 us
  transfers between devices with their start and end apart: 10, of which 6 were waited for; matrix products, arithmetic and copies ran while one was open for 0% of the time, Pallas kernels for 14%

profile of v4, /device:TPU:1, one launch (start us, length us, event | category | flops | bytes accessed | tf_op | source)
XLA Modules:
  0.0 137.1 jit_solution(8685655323330405001)
XLA Ops:
  0.6 0.0 copy-start.9
  0.6 0.0 copy-start.10
  0.7 0.0 copy-start.11
  0.7 4.8 %first_coefs.1 = (bf16[3,192,512]{2,1,0:T(8,128)(2,1)}, bf16[16,96,128]{2,1,0:T(8,128)(2,1)}) custom-call(f32[192,1536]{1,0:T(8,128)} %bitcast.6, bf16[8,1536,128]{2,1,0:T(8,128)(2,1)} %basis_ref.3), custom_call_target="tpu_custom_call" | custom-call | tf_op jit(solution)/shard_map/first_coefs/pallas_call | solution.py:124
  5.4 0.0 copy-start.8
  5.4 7.6 %all-to-all-start = ((bf16[16,96,128]{2,1,0:T(8,128)(2,1)}), bf16[16,96,128]{2,1,0:T(8,128)(2,1)S(1)}, u32[]{:S(2)}, u32[]{:S(2)}) async-start(bf16[16,96,128]{2,1,0:T(8,128)(2,1)} %get-tuple-element.21), calls=%async_computation | async-start | bytes 786432 | tf_op jit(solution)/shard_map/all_to_all | solution.py:470
  13.0 7.7 %collective-permute-start.1 = (bf16[3,192,512]{2,1,0:T(8,128)(2,1)}, bf16[3,192,512]{2,1,0:T(8,128)(2,1)S(1)}, u32[]{:S(2)}, u32[]{:S(2)}) collective-permute-start(bf16[3,192,512]{2,1,0:T(8,128)(2,1)} %get-tuple-element.23.own_hbm), channel_id=1, source_target_pairs={{1,0},{2,1},{3,2},{4,3},{5,4},{6,5},{7,6},{8,7},{9,8},{10,9},{11,1... | collective-permute-start | bytes 1769480 | tf_op jit(solution)/shard_map/ppermute | solution.py:477
  20.8 1.9 %collective-permute-start = (bf16[3,192,512]{2,1,0:T(8,128)(2,1)}, bf16[3,192,512]{2,1,0:T(8,128)(2,1)S(1)}, u32[]{:S(2)}, u32[]{:S(2)}) collective-permute-start(bf16[3,192,512]{2,1,0:T(8,128)(2,1)} %get-tuple-element.23.own_hbm), channel_id=1, source_target_pairs={{0,1},{1,2},{2,3},{3,4},{4,5},{5,6},{6,7},{7,8},{8,9},{9,10},{10,1... | collective-permute-start | bytes 1769480 | tf_op jit(solution)/shard_map/ppermute | solution.py:477
  22.7 0.0 copy-done.9
  22.7 0.0 copy-done.10
  22.8 0.1 pad.3.clone
  22.9 0.1 pad_add_fusion.place_ref
  23.0 0.0 all-to-all-done.got_ref
  23.0 1.3 lower_sums.2
  24.3 0.0 copy-start.4
  24.3 0.0 copy-start.5
  24.3 9.3 %all-to-all-start.1 = ((bf16[16,48,128]{2,1,0:T(8,128)(2,1)}), bf16[16,48,128]{2,1,0:T(8,128)(2,1)S(1)}, u32[]{:S(2)}, u32[]{:S(2)}) async-start(bf16[16,48,128]{2,1,0:T(8,128)(2,1)} %get-tuple-element.22), calls=%async_computation.1 | async-start | bytes 393216 | tf_op jit(solution)/shard_map/all_to_all | solution.py:470
  33.7 0.1 maximum_maximum_fusion.values_ref
  33.8 2.9 %sort_panels.1.rest_1_.sorted_ref = f32[8,1536]{1,0:T(8,128)} custom-call(s32[1,1536]{1,0:T(1,128)S(1)} %broadcast_in_dim.20.order_ref, f32[8,1536]{1,0:T(8,128)S(1)} %maximum_maximum_fusion.values_ref), custom_call_target="tpu_custom_call" | custom-call | tf_op jit(solution)/shard_map/sort_panels/pallas_call | solution.py:413
  36.6 0.0 collective-permute-done.1.right_hbm
  36.7 0.0 collective-permute-done.left_hbm
  36.7 0.0 copy-start.7
  36.7 7.3 %all-to-all-done.1.got_ref = bf16[16,48,128]{2,1,0:T(8,128)(2,1)S(1)} async-done(((bf16[16,48,128]{2,1,0:T(8,128)(2,1)}), bf16[16,48,128]{2,1,0:T(8,128)(2,1)S(1)}, u32[]{:S(2)}, u32[]{:S(2)}) %all-to-all-start.1) | async-done | bytes 196640 | tf_op jit(solution)/shard_map/all_to_all | solution.py:470
  44.0 1.3 upper_sums.2
  45.3 0.0 copy-done.6
  45.3 0.0 copy-done.7
  45.3 5.7 %all-to-all-start.2 = ((bf16[16,96,128]{2,1,0:T(8,128)(2,1)}), bf16[16,96,128]{2,1,0:T(8,128)(2,1)S(1)}, u32[]{:S(2)}, u32[]{:S(2)}) async-start(bf16[16,96,128]{2,1,0:T(8,128)(2,1)} %upper_sums.2), calls=%async_computation.2 | async-start | bytes 786432 | tf_op jit(solution)/shard_map/all_to_all | solution.py:470
  51.0 0.0 copy-start
  51.1 7.0 %near_field.2.near_hbm = f32[192,1536]{1,0:T(8,128)} custom-call(s32[3,4]{1,0:T(4,128)S(1)} %copy-done.4, bf16[3,192,512]{2,1,0:T(8,128)(2,1)} %copy-done.7, bf16[3,192,512]{2,1,0:T(8,128)(2,1)} %get-tuple-element.23.own_hbm, bf16[3,192,512]{2,1,0:T(8,128)(2,1)} %copy-done.6, bf16[3,4,512,512]{3,2,1,0:T(8,128)(2,1)} %kernel_hbm.3, f32[3,64]{1,0:T(4,128)S(1)} %copy-done.5, ...), custom_call_target="tpu_custom_call" | custom-call | tf_op jit(solution)/shard_map/near_field/pallas_call | solution.py:271
  58.1 2.2 %all-to-all-done.2.got_ref = bf16[16,96,128]{2,1,0:T(8,128)(2,1)S(1)} async-done(((bf16[16,96,128]{2,1,0:T(8,128)(2,1)}), bf16[16,96,128]{2,1,0:T(8,128)(2,1)S(1)}, u32[]{:S(2)}, u32[]{:S(2)}) %all-to-all-start.2) | async-done | bytes 393248 | tf_op jit(solution)/shard_map/all_to_all | solution.py:470
  60.3 3.9 %residual.1 = (f32[192,1536]{1,0:T(8,128)}, bf16[3,192,512]{2,1,0:T(8,128)(2,1)}, bf16[16,96,128]{2,1,0:T(8,128)(2,1)}) custom-call(bf16[16,96,128]{2,1,0:T(8,128)(2,1)S(1)} %all-to-all-done.2.got_ref, f32[192,1536]{1,0:T(8,128)} %near_field.2.near_hbm, bf16[8,1536,128]{2,1,0:T(8,128)(2,1)S(1)} %copy-done), custom_call_target="tpu_custom_call" | custom-call | tf_op jit(solution)/shard_map/residual/pallas_call | solution.py:344
  64.2 4.5 %all-to-all-start.3 = ((bf16[16,96,128]{2,1,0:T(8,128)(2,1)}), bf16[16,96,128]{2,1,0:T(8,128)(2,1)S(1)}, u32[]{:S(2)}, u32[]{:S(2)}) async-start(bf16[16,96,128]{2,1,0:T(8,128)(2,1)} %get-tuple-element.29), calls=%async_computation.3 | async-start | bytes 786432 | tf_op jit(solution)/shard_map/all_to_all | solution.py:470
  68.7 7.5 %collective-permute-start.3 = (bf16[3,192,512]{2,1,0:T(8,128)(2,1)}, bf16[3,192,512]{2,1,0:T(8,128)(2,1)}, u32[]{:S(2)}, u32[]{:S(2)}) collective-permute-start(bf16[3,192,512]{2,1,0:T(8,128)(2,1)} %get-tuple-element.31.own_hbm), channel_id=1, source_target_pairs={{1,0},{2,1},{3,2},{4,3},{5,4},{6,5},{7,6},{8,7},{9,8},{10,9},{11,1... | collective-permute-start | bytes 1769480 | tf_op jit(solution)/shard_map/ppermute | solution.py:477
  76.2 1.9 %collective-permute-start.2 = (bf16[3,192,512]{2,1,0:T(8,128)(2,1)}, bf16[3,192,512]{2,1,0:T(8,128)(2,1)}, u32[]{:S(2)}, u32[]{:S(2)}) collective-permute-start(bf16[3,192,512]{2,1,0:T(8,128)(2,1)} %get-tuple-element.31.own_hbm), channel_id=1, source_target_pairs={{0,1},{1,2},{2,3},{3,4},{4,5},{5,6},{6,7},{7,8},{8,9},{9,10},{10,1... | collective-permute-start | bytes 1769480 | tf_op jit(solution)/shard_map/ppermute | solution.py:477
  78.2 0.0 all-to-all-done.3.got_ref
  78.2 1.4 lower_sums.3
  79.5 5.6 %all-to-all-start.4 = ((bf16[16,48,128]{2,1,0:T(8,128)(2,1)}), bf16[16,48,128]{2,1,0:T(8,128)(2,1)S(1)}, u32[]{:S(2)}, u32[]{:S(2)}) async-start(bf16[16,48,128]{2,1,0:T(8,128)(2,1)} %get-tuple-element.30), calls=%async_computation.4 | async-start | bytes 393216 | tf_op jit(solution)/shard_map/all_to_all | solution.py:470
  85.2 4.5 %collective-permute-done.3.right_hbm = bf16[3,192,512]{2,1,0:T(8,128)(2,1)} collective-permute-done((bf16[3,192,512]{2,1,0:T(8,128)(2,1)}, bf16[3,192,512]{2,1,0:T(8,128)(2,1)}, u32[]{:S(2)}, u32[]{:S(2)}) %collective-permute-start.3) | collective-permute-done | bytes 589856 | tf_op jit(solution)/shard_map/ppermute | solution.py:477
  89.7 1.4 %collective-permute-done.2.left_hbm = bf16[3,192,512]{2,1,0:T(8,128)(2,1)} collective-permute-done((bf16[3,192,512]{2,1,0:T(8,128)(2,1)}, bf16[3,192,512]{2,1,0:T(8,128)(2,1)}, u32[]{:S(2)}, u32[]{:S(2)}) %collective-permute-start.2) | collective-permute-done | bytes 589856 | tf_op jit(solution)/shard_map/ppermute | solution.py:477
  91.1 4.4 %all-to-all-done.4.got_ref = bf16[16,48,128]{2,1,0:T(8,128)(2,1)S(1)} async-done(((bf16[16,48,128]{2,1,0:T(8,128)(2,1)}), bf16[16,48,128]{2,1,0:T(8,128)(2,1)S(1)}, u32[]{:S(2)}, u32[]{:S(2)}) %all-to-all-start.4) | async-done | bytes 196640 | tf_op jit(solution)/shard_map/all_to_all | solution.py:470
  95.5 1.3 upper_sums.3
  96.8 5.0 %all-to-all-start.5 = ((bf16[16,96,128]{2,1,0:T(8,128)(2,1)}), bf16[16,96,128]{2,1,0:T(8,128)(2,1)S(1)}, u32[]{:S(2)}, u32[]{:S(2)}) async-start(bf16[16,96,128]{2,1,0:T(8,128)(2,1)} %upper_sums.3), calls=%async_computation.5 | async-start | bytes 786432 | tf_op jit(solution)/shard_map/all_to_all | solution.py:470
  101.8 6.6 %near_field.3.near_hbm = f32[192,1536]{1,0:T(8,128)} custom-call(s32[3,4]{1,0:T(4,128)S(1)} %copy-done.4, bf16[3,192,512]{2,1,0:T(8,128)(2,1)} %collective-permute-done.2.left_hbm, bf16[3,192,512]{2,1,0:T(8,128)(2,1)} %get-tuple-element.31.own_hbm, bf16[3,192,512]{2,1,0:T(8,128)(2,1)} %collective-permute-done.3.right_hbm, bf16[3,4,512,512]{3,2,1,0:T(8,128)(2,1)} %kernel_hbm.3), custom_call_target="tpu_custom_call" | custom-call | tf_op jit(solution)/shard_map/near_field/pallas_call | solution.py:271
  108.4 2.4 %all-to-all-done.5.got_ref = bf16[16,96,128]{2,1,0:T(8,128)(2,1)S(1)} async-done(((bf16[16,96,128]{2,1,0:T(8,128)(2,1)}), bf16[16,96,128]{2,1,0:T(8,128)(2,1)S(1)}, u32[]{:S(2)}, u32[]{:S(2)}) %all-to-all-start.5) | async-done | bytes 393248 | tf_op jit(solution)/shard_map/all_to_all | solution.py:470
  110.8 3.3 %products.1 = f32[1,128]{1,0:T(1,128)S(1)} custom-call(bf16[16,96,128]{2,1,0:T(8,128)(2,1)S(1)} %all-to-all-done.5.got_ref, f32[192,1536]{1,0:T(8,128)} %near_field.3.near_hbm, f32[192,1536]{1,0:T(8,128)} %get-tuple-element.36.residual_hbm.residual_ref, bf16[8,1536,128]{2,1,0:T(8,128)(2,1)S(1)} %copy-done), custom_call_target="tpu_custom_call" | custom-call | tf_op jit(solution)/shard_map/products/pallas_call | solution.py:381
  114.1 0.1 broadcast_in_dim.25
  114.1 20.6 %all_to_all.35.got_ref = f32[256,1,128]{2,1,0:T(1,128)S(1)} all-to-all(f32[256,1,128]{2,1,0:T(1,128)S(1)} %broadcast_in_dim.25), channel_id=1, replica_groups=mesh['wide_0'=8,'wide_1'=2,'narrow_0'=4,'narrow_1'=4] {'wide_0','wide_1'..., dimensions={0} | all-to-all | bytes 262144 | tf_op jit(solution)/shard_map/all_to_all | solution.py:470
  134.7 2.3 %final.1 = (f32[192,1536]{1,0:T(8,128)}, f32[64]{0:T(128)}) custom-call(f32[256,1,128]{2,1,0:T(1,128)S(1)} %all_to_all.35.got_ref, f32[192,1536]{1,0:T(8,128)S(1)} %bitcast.7, f32[192,1536]{1,0:T(8,128)S(1)} %copy-done.2, f32[8,1536]{1,0:T(8,128)S(1)} %copy-done.3), custom_call_target="tpu_custom_call" | custom-call | tf_op jit(solution)/shard_map/final/pallas_call | solution.py:456
  (17 shorter events, 0.0 us)
Async XLA Ops:
  0.6 22.1 %copy-start.9 = (f32[1536]{0:T(1024)S(1)}, f32[1536]{0:T(1024)}, u32[]{:S(2)}) copy-start(f32[1536]{0:T(1024)} %param.14) | copy-start | bytes 18436
  0.6 22.1 %copy-start.10 = (s32[1536]{0:T(1024)S(1)}, s32[1536]{0:T(1024)}, u32[]{:S(2)}) copy-start(s32[1536]{0:T(1024)} %param.16) | copy-start | bytes 18436
  0.7 22.1 %copy-start.11 = (s32[1536]{0:T(1024)S(1)}, s32[1536]{0:T(1024)}, u32[]{:S(2)}) copy-start(s32[1536]{0:T(1024)} %param.15) | copy-start | bytes 18436
  5.4 28.3 %copy-start.8 = (f32[3,1536]{1,0:T(4,128)S(1)}, f32[3,1536]{1,0:T(4,128)}, u32[]{:S(2)}) copy-start(f32[3,1536]{1,0:T(4,128)} %param.13) | copy-start | bytes 55300
  5.4 17.5 %all-to-all-start = ((bf16[16,96,128]{2,1,0:T(8,128)(2,1)}), bf16[16,96,128]{2,1,0:T(8,128)(2,1)S(1)}, u32[]{:S(2)}, u32[]{:S(2)}) async-start(bf16[16,96,128]{2,1,0:T(8,128)(2,1)} %get-tuple-element.21), calls=%async_computation | async-start | bytes 786432 | tf_op jit(solution)/shard_map/all_to_all | solution.py:470
  13.0 23.6 %collective-permute-start.1 = (bf16[3,192,512]{2,1,0:T(8,128)(2,1)}, bf16[3,192,512]{2,1,0:T(8,128)(2,1)S(1)}, u32[]{:S(2)}, u32[]{:S(2)}) collective-permute-start(bf16[3,192,512]{2,1,0:T(8,128)(2,1)} %get-tuple-element.23.own_hbm), channel_id=1, source_target_pairs={{1,0},{2,1},{3,2},{4,3},{5,4},{6,5},{7,6},{8,7},{9,8},{10,9},{11,1... | collective-permute-start | bytes 1769480 | tf_op jit(solution)/shard_map/ppermute | solution.py:477
  20.8 15.9 %collective-permute-start = (bf16[3,192,512]{2,1,0:T(8,128)(2,1)}, bf16[3,192,512]{2,1,0:T(8,128)(2,1)S(1)}, u32[]{:S(2)}, u32[]{:S(2)}) collective-permute-start(bf16[3,192,512]{2,1,0:T(8,128)(2,1)} %get-tuple-element.23.own_hbm), channel_id=1, source_target_pairs={{0,1},{1,2},{2,3},{3,4},{4,5},{5,6},{6,7},{7,8},{8,9},{9,10},{10,1... | collective-permute-start | bytes 1769480 | tf_op jit(solution)/shard_map/ppermute | solution.py:477
  24.3 26.7 %copy-start.4 = (s32[3,4]{1,0:T(4,128)S(1)}, s32[3,4]{1,0:T(4,128)}, u32[]{:S(2)}) copy-start(s32[3,4]{1,0:T(4,128)} %slots_ref.3) | copy-start | bytes 148
  24.3 26.7 %copy-start.5 = (f32[3,64]{1,0:T(4,128)S(1)}, f32[3,64]{1,0:T(4,128)}, u32[]{:S(2)}) copy-start(f32[3,64]{1,0:T(4,128)} %rest_0_.1) | copy-start | bytes 2308
  24.3 19.7 %all-to-all-start.1 = ((bf16[16,48,128]{2,1,0:T(8,128)(2,1)}), bf16[16,48,128]{2,1,0:T(8,128)(2,1)S(1)}, u32[]{:S(2)}, u32[]{:S(2)}) async-start(bf16[16,48,128]{2,1,0:T(8,128)(2,1)} %get-tuple-element.22), calls=%async_computation.1 | async-start | bytes 393216 | tf_op jit(solution)/shard_map/all_to_all | solution.py:470
  36.7 8.6 %copy-start.6 = (bf16[3,192,512]{2,1,0:T(8,128)(2,1)}, bf16[3,192,512]{2,1,0:T(8,128)(2,1)S(1)}, u32[]{:S(2)}) copy-start(bf16[3,192,512]{2,1,0:T(8,128)(2,1)S(1)} %collective-permute-done.1.right_hbm) | copy-start | bytes 1769476
  36.7 8.7 %copy-start.7 = (bf16[3,192,512]{2,1,0:T(8,128)(2,1)}, bf16[3,192,512]{2,1,0:T(8,128)(2,1)S(1)}, u32[]{:S(2)}) copy-start(bf16[3,192,512]{2,1,0:T(8,128)(2,1)S(1)} %collective-permute-done.left_hbm) | copy-start | bytes 1769476
  45.3 15.0 %all-to-all-start.2 = ((bf16[16,96,128]{2,1,0:T(8,128)(2,1)}), bf16[16,96,128]{2,1,0:T(8,128)(2,1)S(1)}, u32[]{:S(2)}, u32[]{:S(2)}) async-start(bf16[16,96,128]{2,1,0:T(8,128)(2,1)} %upper_sums.2), calls=%async_computation.2 | async-start | bytes 786432 | tf_op jit(solution)/shard_map/all_to_all | solution.py:470
  51.0 9.2 %copy-start = (bf16[8,1536,128]{2,1,0:T(8,128)(2,1)S(1)}, bf16[8,1536,128]{2,1,0:T(8,128)(2,1)}, u32[]{:S(2)}) copy-start(bf16[8,1536,128]{2,1,0:T(8,128)(2,1)} %basis_ref.3) | copy-start | bytes 9437188
  64.2 13.9 %all-to-all-start.3 = ((bf16[16,96,128]{2,1,0:T(8,128)(2,1)}), bf16[16,96,128]{2,1,0:T(8,128)(2,1)S(1)}, u32[]{:S(2)}, u32[]{:S(2)}) async-start(bf16[16,96,128]{2,1,0:T(8,128)(2,1)} %get-tuple-element.29), calls=%async_computation.3 | async-start | bytes 786432 | tf_op jit(solution)/shard_map/all_to_all | solution.py:470
  68.7 21.0 %collective-permute-start.3 = (bf16[3,192,512]{2,1,0:T(8,128)(2,1)}, bf16[3,192,512]{2,1,0:T(8,128)(2,1)}, u32[]{:S(2)}, u32[]{:S(2)}) collective-permute-start(bf16[3,192,512]{2,1,0:T(8,128)(2,1)} %get-tuple-element.31.own_hbm), channel_id=1, source_target_pairs={{1,0},{2,1},{3,2},{4,3},{5,4},{6,5},{7,6},{8,7},{9,8},{10,9},{11,1... | collective-permute-start | bytes 1769480 | tf_op jit(solution)/shard_map/ppermute | solution.py:477
  76.2 14.8 %collective-permute-start.2 = (bf16[3,192,512]{2,1,0:T(8,128)(2,1)}, bf16[3,192,512]{2,1,0:T(8,128)(2,1)}, u32[]{:S(2)}, u32[]{:S(2)}) collective-permute-start(bf16[3,192,512]{2,1,0:T(8,128)(2,1)} %get-tuple-element.31.own_hbm), channel_id=1, source_target_pairs={{0,1},{1,2},{2,3},{3,4},{4,5},{5,6},{6,7},{7,8},{8,9},{9,10},{10,1... | collective-permute-start | bytes 1769480 | tf_op jit(solution)/shard_map/ppermute | solution.py:477
  79.5 15.9 %all-to-all-start.4 = ((bf16[16,48,128]{2,1,0:T(8,128)(2,1)}), bf16[16,48,128]{2,1,0:T(8,128)(2,1)S(1)}, u32[]{:S(2)}, u32[]{:S(2)}) async-start(bf16[16,48,128]{2,1,0:T(8,128)(2,1)} %get-tuple-element.30), calls=%async_computation.4 | async-start | bytes 393216 | tf_op jit(solution)/shard_map/all_to_all | solution.py:470
  96.8 14.0 %all-to-all-start.5 = ((bf16[16,96,128]{2,1,0:T(8,128)(2,1)}), bf16[16,96,128]{2,1,0:T(8,128)(2,1)S(1)}, u32[]{:S(2)}, u32[]{:S(2)}) async-start(bf16[16,96,128]{2,1,0:T(8,128)(2,1)} %upper_sums.3), calls=%async_computation.5 | async-start | bytes 786432 | tf_op jit(solution)/shard_map/all_to_all | solution.py:470
  110.8 23.9 %copy-start.1 = (f32[3,64,1536]{2,1,0:T(8,128)S(1)}, f32[3,64,1536]{2,1,0:T(8,128)}, u32[]{:S(2)}) copy-start(f32[3,64,1536]{2,1,0:T(8,128)} %param.9) | copy-start | bytes 3538948
  110.8 23.9 %copy-start.2 = (f32[192,1536]{1,0:T(8,128)S(1)}, f32[192,1536]{1,0:T(8,128)}, u32[]{:S(2)}) copy-start(f32[192,1536]{1,0:T(8,128)} %get-tuple-element.36.residual_hbm.residual_ref) | copy-start | bytes 3538948
  110.8 23.9 %copy-start.3 = (f32[8,1536]{1,0:T(8,128)S(1)}, f32[8,1536]{1,0:T(8,128)}, u32[]{:S(2)}) copy-start(f32[8,1536]{1,0:T(8,128)} %sort_panels.1.rest_1_.sorted_ref) | copy-start | bytes 147460

commit v5 on v4

--- a/solution.py
+++ b/solution.py
@@ -31,6 +31,7 @@
 BF16 = jnp.bfloat16
 NT = (((1,), (1,)), ((), ()))
 LIMIT = 16 * 2**20
+IN_FLIGHT = 5
 
 
 def gain(level):
@@ -65,8 +66,8 @@
 PANEL_ROWS = pl.BlockSpec((8, BLK), lambda b: (0, b))
 
 
-def send_coefs(level, values, pair, sent_ref, sent_hbm, sem):
-    coefs = jnp.dot(values, pair, preferred_element_type=F32).astype(BF16)
+def send_coefs(level, coefs, sent_ref, sent_hbm, sem):
+    coefs = coefs.astype(BF16)
     for quarter in range(QUARTERS):
         rows = slice(quarter * PART, (quarter + 1) * PART)
         slot = level * QUARTERS + quarter
@@ -79,37 +80,41 @@
 
 
 def coef_kernel(field_hbm, basis_hbm, low_hbm, sent_hbm, *scratch):
-    field_ref, low_ref, basis_ref, sent_ref, field_sems, basis_sems, low_sems, sent_sems = scratch
-    fields, bases, leaving = [], [], []
+    field_ref, low_ref, basis_ref, acc_ref, sent_ref, sems, sent_sems = scratch
+    arriving, leaving = [], []
     for chunk in range(CHUNKS):
         panels = pl.ds(chunk * BLK, BLK)
-        fields.append(
-            pltpu.make_async_copy(
-                field_hbm.at[:, panels], field_ref.at[chunk], field_sems.at[chunk]
+        arriving.append(
+            (
+                pltpu.make_async_copy(
+                    field_hbm.at[:, panels], field_ref.at[chunk], sems.at[0, chunk]
+                ),
+                pltpu.make_async_copy(
+                    basis_hbm.at[:, panels, :], basis_ref.at[chunk], sems.at[1, chunk]
+                ),
             )
         )
-        fields[-1].start()
-    for level in range(HALF):
-        bases.append(
-            [
-                pltpu.make_async_copy(basis_hbm.at[at], basis_ref.at[at], basis_sems.at[at])
-                for at in (level, HALF + level)
-            ]
-        )
-        for copy in bases[-1]:
+        for copy in arriving[-1]:
             copy.start()
     for chunk in range(CHUNKS):
-        fields[chunk].wait()
-        low_ref[chunk] = field_ref[chunk].astype(BF16)
-        copy = pltpu.make_async_copy(low_ref.at[chunk], low_hbm.at[chunk], low_sems.at[chunk])
+        for copy in arriving[chunk]:
+            copy.wait()
+        values = field_ref[chunk].astype(BF16)
+        low_ref[chunk] = values
+        copy = pltpu.make_async_copy(low_ref.at[chunk], low_hbm.at[chunk], sems.at[2, chunk])
         copy.start()
         leaving.append(copy)
-    values = jnp.concatenate([low_ref[chunk] for chunk in range(CHUNKS)], axis=1)
-    for level in range(HALF):
-        for copy in bases[level]:
-            copy.wait()
-        pair = jnp.concatenate([basis_ref[level], basis_ref[HALF + level]], axis=1)
-        leaving.append(send_coefs(level, values, pair, sent_ref, sent_hbm, sent_sems.at[level]))
+        for level in range(HALF):
+            pair = jnp.concatenate(
+                [basis_ref[chunk, level], basis_ref[chunk, HALF + level]], axis=1
+            )
+            part = jnp.dot(values, pair, preferred_element_type=F32)
+            if chunk > 0:
+                part += acc_ref[level]
+            if chunk < CHUNKS - 1:
+                acc_ref[level] = part
+            else:
+                leaving.append(send_coefs(level, part, sent_ref, sent_hbm, sent_sems.at[level]))
     for copy in leaving:
         copy.wait()
 
@@ -130,11 +135,10 @@
         scratch_shapes=[
             pltpu.VMEM((CHUNKS, ROWS, BLK), F32),
             pltpu.VMEM(BLOCKS.shape, BF16),
-            pltpu.VMEM((LEVELS, PAN, RANK), BF16),
+            pltpu.VMEM((CHUNKS, LEVELS, BLK, RANK), BF16),
+            pltpu.VMEM((HALF, ROWS, 2 * RANK), F32),
             pltpu.VMEM(SENT.shape, BF16),
-            pltpu.SemaphoreType.DMA((CHUNKS,)),
-            pltpu.SemaphoreType.DMA((LEVELS,)),
-            pltpu.SemaphoreType.DMA((CHUNKS,)),
+            pltpu.SemaphoreType.DMA((3, CHUNKS)),
             pltpu.SemaphoreType.DMA((HALF,)),
         ],
     )(in_hbm(field), in_hbm(far_basis))
@@ -222,63 +226,88 @@
 
 
 def near_kernel_body(slots_ref, left_hbm, own_hbm, right_hbm, kernel_hbm, *rest):
-    out_ref, ext_ref, kernel_ref, ext_sems, kernel_sems = rest[-5:]
-    block = pl.program_id(0)
-
-    def sides():
-        for side, source in enumerate((own_hbm, left_hbm, right_hbm)):
-            place = ((1, 0, 2)[side]) * CHUNKS
-            yield pltpu.make_async_copy(
-                source, ext_ref.at[pl.ds(place, CHUNKS)], ext_sems.at[side]
+    out_hbm, ext_ref, kernel_ref, out_ref, ext_sems, kernel_sems, out_sems = rest[-7:]
+    count = kernel_ref.shape[1]
+
+    def side_copy(place, source):
+        copy = pltpu.make_async_copy(
+            source, ext_ref.at[pl.ds(place * CHUNKS, CHUNKS)], ext_sems.at[place]
+        )
+        copy.start()
+        return copy
+
+    own_copy = side_copy(1, own_hbm)
+    order = [(block, 0) for block in range(CHUNKS)]
+    order += [(block, k) for block in range(CHUNKS) for k in range(1, count)]
+    kernels = {}
+
+    def fetch(place):
+        if place < len(order):
+            block, k = order[place]
+            kernels[block, k] = pltpu.make_async_copy(
+                kernel_hbm.at[block, k], kernel_ref.at[block, k], kernel_sems.at[block, k]
             )
-
-    def kernel_copy(at):
-        return pltpu.make_async_copy(kernel_hbm.at[at], kernel_ref.at[at], kernel_sems.at[at])
-
-    @pl.when(block == 0)
-    def _():
-        for copy in sides():
-            copy.start()
-        for at in range(CHUNKS):
-            kernel_copy(at).start()
-        for copy in sides():
-            copy.wait()
-
-    kernel_copy(block).wait()
-    total = jnp.zeros((ROWS, BLK), F32)
-    for k in range(kernel_ref.shape[1]):
-        slot = slots_ref[block, k] - slots_ref[block, 0] + block + CHUNKS
-        total += lax.dot_general(
+            kernels[block, k].start()
+
+    for place in range(IN_FLIGHT):
+        fetch(place)
+    side_copies = [side_copy(0, left_hbm), side_copy(2, right_hbm)]
+
+    def product(block, k, slot):
+        kernels[block, k].wait()
+        fetch(order.index((block, k)) + IN_FLIGHT)
+        return lax.dot_general(
             ext_ref[slot], kernel_ref[block, k], NT, preferred_element_type=F32
         )
-    if len(rest) == 5:
-        out_ref[...] = total
-        return
-    approach_ref, gap_ref = rest[:2]
-    square = (LOADS, LOADS)
-    diagonal = lax.broadcasted_iota(jnp.int32, square, 0) == lax.broadcasted_iota(
-        jnp.int32, square, 1
-    )
-    for comp in range(COMP):
-        rows = slice(comp * LOADS, (comp + 1) * LOADS)
-        row = jnp.broadcast_to(approach_ref[comp : comp + 1, :], square)
-        column = jnp.sum(jnp.where(diagonal, row, 0.0), axis=1, keepdims=True)
-        out_ref[rows, :] = total[rows] - (column - gap_ref[comp : comp + 1, :])
+
+    own_copy.wait()
+    for block in range(CHUNKS):
+        total = product(block, 0, CHUNKS + block)
+        if len(rest) > 7:
+            approach_ref, gap_ref = rest[:2]
+            square = (LOADS, LOADS)
+            diagonal = lax.broadcasted_iota(jnp.int32, square, 0) == lax.broadcasted_iota(
+                jnp.int32, square, 1
+            )
+            gaps = gap_ref[0:COMP, pl.ds(block * BLK, BLK)]
+            for comp in range(COMP):
+                rows = slice(comp * LOADS, (comp + 1) * LOADS)
+                row = jnp.broadcast_to(approach_ref[comp : comp + 1, :], square)
+                column = jnp.sum(jnp.where(diagonal, row, 0.0), axis=1, keepdims=True)
+                out_ref[block, rows, :] = total[rows] - (column - gaps[comp : comp + 1])
+        else:
+            out_ref[block] = total
+    for copy in side_copies:
+        copy.wait()
+    leaving = []
+    for block in range(CHUNKS):
+        total = out_ref[block]
+        for k in range(1, count):
+            slot = slots_ref[block, k] - slots_ref[block, 0] + (block + CHUNKS)
+            total += product(block, k, slot)
+        out_ref[block] = total
+        copy = pltpu.make_async_copy(
+            out_ref.at[block], out_hbm.at[:, pl.ds(block * BLK, BLK)], out_sems.at[block]
+        )
+        copy.start()
+        leaving.append(copy)
+    for copy in leaving:
+        copy.wait()
 
 
 def near_field(neighbours, left, own, right, near_kernel, *target):
-    specs = [whole((COMP, LOADS)), PANEL_ROWS] if target else []
     return call(
         near_kernel_body,
         "near_field",
-        grid=(CHUNKS,),
-        in_specs=[SCALARS] + [IN_HBM] * 4 + specs,
-        out_specs=CHUNK,
+        in_specs=[SCALARS] + [IN_HBM] * 4 + [IN_VMEM] * len(target),
+        out_specs=IN_HBM,
         out_shape=FIELD,
         scratch_shapes=[
             pltpu.VMEM((3 * CHUNKS, ROWS, BLK), BF16),
             pltpu.VMEM(near_kernel.shape, BF16),
+            pltpu.VMEM((CHUNKS, ROWS, BLK), F32),
             pltpu.SemaphoreType.DMA((3,)),
+            pltpu.SemaphoreType.DMA(near_kernel.shape[:2]),
             pltpu.SemaphoreType.DMA((CHUNKS,)),
         ],
     )(neighbours, *map(in_hbm, (left, own, right, near_kernel)), *target)
@@ -321,9 +350,11 @@
     unpack(got_ref, coef_ref)
     for chunk in range(CHUNKS):
         panels = pl.ds(chunk * BLK, BLK)
-        far = far_field(coef_ref, basis_ref.at[:, panels, :])
+        out_ref[chunk] = far_field(coef_ref, basis_ref.at[:, panels, :])
+    for chunk in range(CHUNKS):
+        panels = pl.ds(chunk * BLK, BLK)
         arriving[chunk].wait()
-        residual = far + near_ref[chunk]
+        residual = out_ref[chunk] + near_ref[chunk]
         out_ref[chunk] = residual
         low_ref[chunk] = residual.astype(BF16)
         for copy in (
@@ -335,7 +366,8 @@
     values = jnp.concatenate([low_ref[chunk] for chunk in range(CHUNKS)], axis=1)
     for level in range(HALF):
         pair = jnp.concatenate([basis_ref[level], basis_ref[HALF + level]], axis=1)
-        leaving.append(send_coefs(level, values, pair, sent_ref, sent_hbm, sent_sems.at[level]))
+        coefs = jnp.dot(values, pair, preferred_element_type=F32)
+        leaving.append(send_coefs(level, coefs, sent_ref, sent_hbm, sent_sems.at[level]))
     for copy in leaving:
         copy.wait()
 
@@ -360,16 +392,17 @@
 
 
 def product_kernel(got_ref, near_hbm, residual_hbm, basis_ref, sums_ref, *scratch):
-    near_ref, residual_ref, coef_ref, sems = scratch
+    near_ref, residual_ref, far_ref, coef_ref, sems = scratch
     nears = start_chunks(near_hbm, near_ref, sems, 0)
     residuals = start_chunks(residual_hbm, residual_ref, sems, 1)
     unpack(got_ref, coef_ref)
     totals = [jnp.zeros((LOADS, 128), F32)] * 2
     for chunk in range(CHUNKS):
-        far = far_field(coef_ref, basis_ref.at[:, pl.ds(chunk * BLK, BLK), :])
+        far_ref[chunk] = far_field(coef_ref, basis_ref.at[:, pl.ds(chunk * BLK, BLK), :])
+    for chunk in range(CHUNKS):
         nears[chunk].wait()
         residuals[chunk].wait()
-        image = far + near_ref[chunk]
+        image = far_ref[chunk] + near_ref[chunk]
         for place, product in enumerate((residual_ref[chunk] * image, image * image)):
             by_load = product[0:LOADS] + product[LOADS : 2 * LOADS] + product[2 * LOADS : ROWS]
             for lane in range(0, BLK, 128):
@@ -387,6 +420,7 @@
         scratch_shapes=[
             pltpu.VMEM((CHUNKS, ROWS, BLK), F32),
             pltpu.VMEM((CHUNKS, ROWS, BLK), F32),
+            pltpu.VMEM((CHUNKS, ROWS, BLK), F32),
             COEFS,
             pltpu.SemaphoreType.DMA((2, CHUNKS)),
         ],
@@ -398,15 +432,15 @@
     local = lax.rem(order_ref[...], PAN)
     chosen = lax.broadcasted_iota(jnp.int32, (rows, cols), 0) == local
     matrix = jnp.where(chosen, 1.0, 0.0).astype(BF16)
-    values = values_ref[...]
-    high = values.astype(BF16)
-    left_over = values - high.astype(F32)
-    middle = left_over.astype(BF16)
-    low = (left_over - middle.astype(F32)).astype(BF16)
-    out_ref[...] = (
-        jnp.dot(high, matrix, preferred_element_type=F32)
-        + jnp.dot(middle, matrix, preferred_element_type=F32)
-    ) + jnp.dot(low, matrix, preferred_element_type=F32)
+    left_over = values_ref[...]
+    pieces = []
+    for _ in range(3):
+        pieces.append(left_over.astype(BF16).astype(F32))
+        left_over = left_over - pieces[-1]
+    pieces = jnp.concatenate(pieces, axis=0).astype(BF16)
+    moved = jnp.dot(pieces, matrix, preferred_element_type=F32)
+    count = out_ref.shape[0]
+    out_ref[...] = (moved[:count] + moved[count : 2 * count]) + moved[2 * count :]
 
 
 def sort_panels(order, values):

time: 138 us -> 135 us (0.978)
  Pallas kernels: 36.1 us -> 31.5 us
  waiting for transfers between devices: 22.3 us -> 24.1 us
    all_to_all x6, waiting for transfers between devices: 16.4 us -> 17.9 us  [swap(): return lax.all_to_all(blocks, axes, 0, 0)]
  transfers between devices with their start and end apart: 10 -> 10, of which waited for: 6 -> 6; matrix products, arithmetic and copies ran while one was open for 0% -> 0% of each run, Pallas kernels for 14% -> 13%
where the time goes in v5:
time: 135 us; the launch traced here: 134 us
  starting transfers between devices  56.7 us (42%)
  Pallas kernels  31.5 us (23%)
  waiting for transfers between devices  24.1 us (18%)
  blocking collectives  20.4 us (15%)
    all_to_all x6, starting transfers between devices, swap(): return lax.all_to_all(blocks, axes, 0, 0)  37.3 us
    all_to_all x1, blocking collectives, swap(): return lax.all_to_all(blocks, axes, 0, 0)  20.4 us
    all_to_all x6, waiting for transfers between devices, swap(): return lax.all_to_all(blocks, axes, 0, 0)  17.9 us
    ppermute x2, starting transfers between devices, beside(): lax.ppermute(blocks, WIDE_NARROW, down)  15.6 us
    pallas_call x2, Pallas kernels, near_field(): call(near_kernel_body, 'near_field', in_specs=[SCALARS] + [IN_HBM] * 4 +...  12.8 us
    ppermute x2, waiting for transfers between devices, beside(): lax.ppermute(blocks, WIDE_NARROW, down)  4.82 us
    ppermute x2, starting transfers between devices, beside(): lax.ppermute(blocks, WIDE_NARROW, up)  3.84 us
    pallas_call x1, Pallas kernels, first_coefs(): call(coef_kernel, 'first_coefs', in_specs=[IN_HBM] * 2, out_specs=[IN_HBM...  3.4 us
  transfers between devices with their start and end apart: 10, of which 6 were waited for; matrix products, arithmetic and copies ran while one was open for 0% of the time, Pallas kernels for 13%

profile of v5, /device:TPU:1, one launch (start us, length us, event | category | flops | bytes accessed | tf_op | source)
XLA Modules:
  0.0 134.1 jit_solution(13710879827599086181)
XLA Ops:
  0.6 0.0 copy-start.9
  0.6 0.0 copy-start.10
  0.7 0.0 copy-start.11
  0.7 3.4 %first_coefs.1 = (bf16[3,192,512]{2,1,0:T(8,128)(2,1)}, bf16[16,96,128]{2,1,0:T(8,128)(2,1)}) custom-call(f32[192,1536]{1,0:T(8,128)} %bitcast.6, bf16[8,1536,128]{2,1,0:T(8,128)(2,1)} %basis_ref.3), custom_call_target="tpu_custom_call" | custom-call | tf_op jit(solution)/shard_map/first_coefs/pallas_call | solution.py:129
  4.1 0.0 copy-start.8
  4.1 7.6 %all-to-all-start = ((bf16[16,96,128]{2,1,0:T(8,128)(2,1)}), bf16[16,96,128]{2,1,0:T(8,128)(2,1)S(1)}, u32[]{:S(2)}, u32[]{:S(2)}) async-start(bf16[16,96,128]{2,1,0:T(8,128)(2,1)} %get-tuple-element.21), calls=%async_computation | async-start | bytes 786432 | tf_op jit(solution)/shard_map/all_to_all | solution.py:504
  11.7 7.7 %collective-permute-start.1 = (bf16[3,192,512]{2,1,0:T(8,128)(2,1)}, bf16[3,192,512]{2,1,0:T(8,128)(2,1)S(1)}, u32[]{:S(2)}, u32[]{:S(2)}) collective-permute-start(bf16[3,192,512]{2,1,0:T(8,128)(2,1)} %get-tuple-element.23.own_hbm), channel_id=1, source_target_pairs={{1,0},{2,1},{3,2},{4,3},{5,4},{6,5},{7,6},{8,7},{9,8},{10,9},{11,1... | collective-permute-start | bytes 1769480 | tf_op jit(solution)/shard_map/ppermute | solution.py:511
  19.4 1.9 %collective-permute-start = (bf16[3,192,512]{2,1,0:T(8,128)(2,1)}, bf16[3,192,512]{2,1,0:T(8,128)(2,1)S(1)}, u32[]{:S(2)}, u32[]{:S(2)}) collective-permute-start(bf16[3,192,512]{2,1,0:T(8,128)(2,1)} %get-tuple-element.23.own_hbm), channel_id=1, source_target_pairs={{0,1},{1,2},{2,3},{3,4},{4,5},{5,6},{6,7},{7,8},{8,9},{9,10},{10,1... | collective-permute-start | bytes 1769480 | tf_op jit(solution)/shard_map/ppermute | solution.py:511
  21.3 0.0 copy-done.9
  21.4 0.0 copy-done.10
  21.4 0.1 pad.3.clone
  21.5 0.1 pad_add_fusion.place_ref
  21.6 0.0 all-to-all-done.got_ref
  21.6 1.3 lower_sums.2
  22.9 0.0 copy-start.4
  23.0 0.0 copy-start.5
  23.0 9.3 %all-to-all-start.1 = ((bf16[16,48,128]{2,1,0:T(8,128)(2,1)}), bf16[16,48,128]{2,1,0:T(8,128)(2,1)S(1)}, u32[]{:S(2)}, u32[]{:S(2)}) async-start(bf16[16,48,128]{2,1,0:T(8,128)(2,1)} %get-tuple-element.22), calls=%async_computation.1 | async-start | bytes 393216 | tf_op jit(solution)/shard_map/all_to_all | solution.py:504
  32.3 0.1 maximum_maximum_fusion.values_ref
  32.4 2.0 %sort_panels.1.rest_1_.sorted_ref = f32[8,1536]{1,0:T(8,128)} custom-call(s32[1,1536]{1,0:T(1,128)S(1)} %broadcast_in_dim.20.order_ref, f32[8,1536]{1,0:T(8,128)S(1)} %maximum_maximum_fusion.values_ref), custom_call_target="tpu_custom_call" | custom-call | tf_op jit(solution)/shard_map/sort_panels/pallas_call | solution.py:447
  34.4 0.0 collective-permute-done.1.right_hbm
  34.4 0.0 collective-permute-done.left_hbm
  34.4 0.0 copy-start.7
  34.4 8.2 %all-to-all-done.1.got_ref = bf16[16,48,128]{2,1,0:T(8,128)(2,1)S(1)} async-done(((bf16[16,48,128]{2,1,0:T(8,128)(2,1)}), bf16[16,48,128]{2,1,0:T(8,128)(2,1)S(1)}, u32[]{:S(2)}, u32[]{:S(2)}) %all-to-all-start.1) | async-done | bytes 196640 | tf_op jit(solution)/shard_map/all_to_all | solution.py:504
  42.6 1.3 upper_sums.2
  43.9 0.0 copy-done.6
  44.0 0.0 copy-done.7
  44.0 5.7 %all-to-all-start.2 = ((bf16[16,96,128]{2,1,0:T(8,128)(2,1)}), bf16[16,96,128]{2,1,0:T(8,128)(2,1)S(1)}, u32[]{:S(2)}, u32[]{:S(2)}) async-start(bf16[16,96,128]{2,1,0:T(8,128)(2,1)} %upper_sums.2), calls=%async_computation.2 | async-start | bytes 786432 | tf_op jit(solution)/shard_map/all_to_all | solution.py:504
  49.7 0.0 copy-start
  49.7 6.7 %near_field.2.near_hbm = f32[192,1536]{1,0:T(8,128)} custom-call(s32[3,4]{1,0:T(4,128)S(1)} %copy-done.4, bf16[3,192,512]{2,1,0:T(8,128)(2,1)} %copy-done.7, bf16[3,192,512]{2,1,0:T(8,128)(2,1)} %get-tuple-element.23.own_hbm, bf16[3,192,512]{2,1,0:T(8,128)(2,1)} %copy-done.6, bf16[3,4,512,512]{3,2,1,0:T(8,128)(2,1)} %kernel_hbm.3, f32[3,64]{1,0:T(4,128)S(1)} %copy-done.5, ...), custom_call_target="tpu_custom_call" | custom-call | tf_op jit(solution)/shard_map/near_field/pallas_call | solution.py:299
  56.4 2.6 %all-to-all-done.2.got_ref = bf16[16,96,128]{2,1,0:T(8,128)(2,1)S(1)} async-done(((bf16[16,96,128]{2,1,0:T(8,128)(2,1)}), bf16[16,96,128]{2,1,0:T(8,128)(2,1)S(1)}, u32[]{:S(2)}, u32[]{:S(2)}) %all-to-all-start.2) | async-done | bytes 393248 | tf_op jit(solution)/shard_map/all_to_all | solution.py:504
  58.9 2.9 %residual.1 = (f32[192,1536]{1,0:T(8,128)}, bf16[3,192,512]{2,1,0:T(8,128)(2,1)}, bf16[16,96,128]{2,1,0:T(8,128)(2,1)}) custom-call(bf16[16,96,128]{2,1,0:T(8,128)(2,1)S(1)} %all-to-all-done.2.got_ref, f32[192,1536]{1,0:T(8,128)} %near_field.2.near_hbm, bf16[8,1536,128]{2,1,0:T(8,128)(2,1)S(1)} %copy-done), custom_call_target="tpu_custom_call" | custom-call | tf_op jit(solution)/shard_map/residual/pallas_call | solution.py:376
  61.8 4.1 %all-to-all-start.3 = ((bf16[16,96,128]{2,1,0:T(8,128)(2,1)}), bf16[16,96,128]{2,1,0:T(8,128)(2,1)S(1)}, u32[]{:S(2)}, u32[]{:S(2)}) async-start(bf16[16,96,128]{2,1,0:T(8,128)(2,1)} %get-tuple-element.29), calls=%async_computation.3 | async-start | bytes 786432 | tf_op jit(solution)/shard_map/all_to_all | solution.py:504
  66.0 7.9 %collective-permute-start.3 = (bf16[3,192,512]{2,1,0:T(8,128)(2,1)}, bf16[3,192,512]{2,1,0:T(8,128)(2,1)}, u32[]{:S(2)}, u32[]{:S(2)}) collective-permute-start(bf16[3,192,512]{2,1,0:T(8,128)(2,1)} %get-tuple-element.31.own_hbm), channel_id=1, source_target_pairs={{1,0},{2,1},{3,2},{4,3},{5,4},{6,5},{7,6},{8,7},{9,8},{10,9},{11,1... | collective-permute-start | bytes 1769480 | tf_op jit(solution)/shard_map/ppermute | solution.py:511
  73.8 1.9 %collective-permute-start.2 = (bf16[3,192,512]{2,1,0:T(8,128)(2,1)}, bf16[3,192,512]{2,1,0:T(8,128)(2,1)}, u32[]{:S(2)}, u32[]{:S(2)}) collective-permute-start(bf16[3,192,512]{2,1,0:T(8,128)(2,1)} %get-tuple-element.31.own_hbm), channel_id=1, source_target_pairs={{0,1},{1,2},{2,3},{3,4},{4,5},{5,6},{6,7},{7,8},{8,9},{9,10},{10,1... | collective-permute-start | bytes 1769480 | tf_op jit(solution)/shard_map/ppermute | solution.py:511
  75.8 0.0 all-to-all-done.3.got_ref
  75.8 1.4 %lower_sums.3 = (bf16[16,96,128]{2,1,0:T(8,128)(2,1)}, bf16[16,48,128]{2,1,0:T(8,128)(2,1)}) custom-call(s32[2]{0:T(128)S(1)} %pad_add_fusion.place_ref, bf16[16,96,128]{2,1,0:T(8,128)(2,1)S(1)} %all-to-all-done.3.got_ref), custom_call_target="tpu_custom_call" | custom-call | tf_op jit(solution)/shard_map/lower_sums/pallas_call | solution.py:180
  77.1 5.3 %all-to-all-start.4 = ((bf16[16,48,128]{2,1,0:T(8,128)(2,1)}), bf16[16,48,128]{2,1,0:T(8,128)(2,1)S(1)}, u32[]{:S(2)}, u32[]{:S(2)}) async-start(bf16[16,48,128]{2,1,0:T(8,128)(2,1)} %get-tuple-element.30), calls=%async_computation.4 | async-start | bytes 393216 | tf_op jit(solution)/shard_map/all_to_all | solution.py:504
  82.5 4.8 %collective-permute-done.3.right_hbm = bf16[3,192,512]{2,1,0:T(8,128)(2,1)} collective-permute-done((bf16[3,192,512]{2,1,0:T(8,128)(2,1)}, bf16[3,192,512]{2,1,0:T(8,128)(2,1)}, u32[]{:S(2)}, u32[]{:S(2)}) %collective-permute-start.3) | collective-permute-done | bytes 589856 | tf_op jit(solution)/shard_map/ppermute | solution.py:511
  87.3 1.4 %collective-permute-done.2.left_hbm = bf16[3,192,512]{2,1,0:T(8,128)(2,1)} collective-permute-done((bf16[3,192,512]{2,1,0:T(8,128)(2,1)}, bf16[3,192,512]{2,1,0:T(8,128)(2,1)}, u32[]{:S(2)}, u32[]{:S(2)}) %collective-permute-start.2) | collective-permute-done | bytes 589856 | tf_op jit(solution)/shard_map/ppermute | solution.py:511
  88.7 4.1 %all-to-all-done.4.got_ref = bf16[16,48,128]{2,1,0:T(8,128)(2,1)S(1)} async-done(((bf16[16,48,128]{2,1,0:T(8,128)(2,1)}), bf16[16,48,128]{2,1,0:T(8,128)(2,1)S(1)}, u32[]{:S(2)}, u32[]{:S(2)}) %all-to-all-start.4) | async-done | bytes 196640 | tf_op jit(solution)/shard_map/all_to_all | solution.py:504
  92.8 1.3 upper_sums.3
  94.1 5.2 %all-to-all-start.5 = ((bf16[16,96,128]{2,1,0:T(8,128)(2,1)}), bf16[16,96,128]{2,1,0:T(8,128)(2,1)S(1)}, u32[]{:S(2)}, u32[]{:S(2)}) async-start(bf16[16,96,128]{2,1,0:T(8,128)(2,1)} %upper_sums.3), calls=%async_computation.5 | async-start | bytes 786432 | tf_op jit(solution)/shard_map/all_to_all | solution.py:504
  99.3 6.1 %near_field.3.near_hbm = f32[192,1536]{1,0:T(8,128)} custom-call(s32[3,4]{1,0:T(4,128)S(1)} %copy-done.4, bf16[3,192,512]{2,1,0:T(8,128)(2,1)} %collective-permute-done.2.left_hbm, bf16[3,192,512]{2,1,0:T(8,128)(2,1)} %get-tuple-element.31.own_hbm, bf16[3,192,512]{2,1,0:T(8,128)(2,1)} %collective-permute-done.3.right_hbm, bf16[3,4,512,512]{3,2,1,0:T(8,128)(2,1)} %kernel_hbm.3), custom_call_target="tpu_custom_call" | custom-call | tf_op jit(solution)/shard_map/near_field/pallas_call | solution.py:299
  105.5 3.0 %all-to-all-done.5.got_ref = bf16[16,96,128]{2,1,0:T(8,128)(2,1)S(1)} async-done(((bf16[16,96,128]{2,1,0:T(8,128)(2,1)}), bf16[16,96,128]{2,1,0:T(8,128)(2,1)S(1)}, u32[]{:S(2)}, u32[]{:S(2)}) %all-to-all-start.5) | async-done | bytes 393248 | tf_op jit(solution)/shard_map/all_to_all | solution.py:504
  108.5 2.8 %products.1 = f32[1,128]{1,0:T(1,128)S(1)} custom-call(bf16[16,96,128]{2,1,0:T(8,128)(2,1)S(1)} %all-to-all-done.5.got_ref, f32[192,1536]{1,0:T(8,128)} %near_field.3.near_hbm, f32[192,1536]{1,0:T(8,128)} %get-tuple-element.36.residual_hbm.residual_ref, bf16[8,1536,128]{2,1,0:T(8,128)(2,1)S(1)} %copy-done), custom_call_target="tpu_custom_call" | custom-call | tf_op jit(solution)/shard_map/products/pallas_call | solution.py:414
  111.3 0.1 broadcast_in_dim.25
  111.3 20.4 %all_to_all.35.got_ref = f32[256,1,128]{2,1,0:T(1,128)S(1)} all-to-all(f32[256,1,128]{2,1,0:T(1,128)S(1)} %broadcast_in_dim.25), channel_id=1, replica_groups=mesh['wide_0'=8,'wide_1'=2,'narrow_0'=4,'narrow_1'=4] {'wide_0','wide_1'..., dimensions={0} | all-to-all | bytes 262144 | tf_op jit(solution)/shard_map/all_to_all | solution.py:504
  131.7 2.3 %final.1 = (f32[192,1536]{1,0:T(8,128)}, f32[64]{0:T(128)}) custom-call(f32[256,1,128]{2,1,0:T(1,128)S(1)} %all_to_all.35.got_ref, f32[192,1536]{1,0:T(8,128)S(1)} %bitcast.7, f32[192,1536]{1,0:T(8,128)S(1)} %copy-done.2, f32[8,1536]{1,0:T(8,128)S(1)} %copy-done.3), custom_call_target="tpu_custom_call" | custom-call | tf_op jit(solution)/shard_map/final/pallas_call | solution.py:490
  (17 shorter events, 0.0 us)
Async XLA Ops:
  0.6 20.7 %copy-start.9 = (f32[1536]{0:T(1024)S(1)}, f32[1536]{0:T(1024)}, u32[]{:S(2)}) copy-start(f32[1536]{0:T(1024)} %param.14) | copy-start | bytes 18436
  0.6 20.7 %copy-start.10 = (s32[1536]{0:T(1024)S(1)}, s32[1536]{0:T(1024)}, u32[]{:S(2)}) copy-start(s32[1536]{0:T(1024)} %param.16) | copy-start | bytes 18436
  0.7 20.7 %copy-start.11 = (s32[1536]{0:T(1024)S(1)}, s32[1536]{0:T(1024)}, u32[]{:S(2)}) copy-start(s32[1536]{0:T(1024)} %param.15) | copy-start | bytes 18436
  4.1 28.3 %copy-start.8 = (f32[3,1536]{1,0:T(4,128)S(1)}, f32[3,1536]{1,0:T(4,128)}, u32[]{:S(2)}) copy-start(f32[3,1536]{1,0:T(4,128)} %param.13) | copy-start | bytes 55300
  4.1 17.5 %all-to-all-start = ((bf16[16,96,128]{2,1,0:T(8,128)(2,1)}), bf16[16,96,128]{2,1,0:T(8,128)(2,1)S(1)}, u32[]{:S(2)}, u32[]{:S(2)}) async-start(bf16[16,96,128]{2,1,0:T(8,128)(2,1)} %get-tuple-element.21), calls=%async_computation | async-start | bytes 786432 | tf_op jit(solution)/shard_map/all_to_all | solution.py:504
  11.7 22.7 %collective-permute-start.1 = (bf16[3,192,512]{2,1,0:T(8,128)(2,1)}, bf16[3,192,512]{2,1,0:T(8,128)(2,1)S(1)}, u32[]{:S(2)}, u32[]{:S(2)}) collective-permute-start(bf16[3,192,512]{2,1,0:T(8,128)(2,1)} %get-tuple-element.23.own_hbm), channel_id=1, source_target_pairs={{1,0},{2,1},{3,2},{4,3},{5,4},{6,5},{7,6},{8,7},{9,8},{10,9},{11,1... | collective-permute-start | bytes 1769480 | tf_op jit(solution)/shard_map/ppermute | solution.py:511
  19.4 15.0 %collective-permute-start = (bf16[3,192,512]{2,1,0:T(8,128)(2,1)}, bf16[3,192,512]{2,1,0:T(8,128)(2,1)S(1)}, u32[]{:S(2)}, u32[]{:S(2)}) collective-permute-start(bf16[3,192,512]{2,1,0:T(8,128)(2,1)} %get-tuple-element.23.own_hbm), channel_id=1, source_target_pairs={{0,1},{1,2},{2,3},{3,4},{4,5},{5,6},{6,7},{7,8},{8,9},{9,10},{10,1... | collective-permute-start | bytes 1769480 | tf_op jit(solution)/shard_map/ppermute | solution.py:511
  22.9 26.7 %copy-start.4 = (s32[3,4]{1,0:T(4,128)S(1)}, s32[3,4]{1,0:T(4,128)}, u32[]{:S(2)}) copy-start(s32[3,4]{1,0:T(4,128)} %slots_ref.3) | copy-start | bytes 148
  23.0 26.7 %copy-start.5 = (f32[3,64]{1,0:T(4,128)S(1)}, f32[3,64]{1,0:T(4,128)}, u32[]{:S(2)}) copy-start(f32[3,64]{1,0:T(4,128)} %rest_0_.1) | copy-start | bytes 2308
  23.0 19.7 %all-to-all-start.1 = ((bf16[16,48,128]{2,1,0:T(8,128)(2,1)}), bf16[16,48,128]{2,1,0:T(8,128)(2,1)S(1)}, u32[]{:S(2)}, u32[]{:S(2)}) async-start(bf16[16,48,128]{2,1,0:T(8,128)(2,1)} %get-tuple-element.22), calls=%async_computation.1 | async-start | bytes 393216 | tf_op jit(solution)/shard_map/all_to_all | solution.py:504
  34.4 9.6 %copy-start.6 = (bf16[3,192,512]{2,1,0:T(8,128)(2,1)}, bf16[3,192,512]{2,1,0:T(8,128)(2,1)S(1)}, u32[]{:S(2)}) copy-start(bf16[3,192,512]{2,1,0:T(8,128)(2,1)S(1)} %collective-permute-done.1.right_hbm) | copy-start | bytes 1769476
  34.4 9.6 %copy-start.7 = (bf16[3,192,512]{2,1,0:T(8,128)(2,1)}, bf16[3,192,512]{2,1,0:T(8,128)(2,1)S(1)}, u32[]{:S(2)}) copy-start(bf16[3,192,512]{2,1,0:T(8,128)(2,1)S(1)} %collective-permute-done.left_hbm) | copy-start | bytes 1769476
  44.0 15.0 %all-to-all-start.2 = ((bf16[16,96,128]{2,1,0:T(8,128)(2,1)}), bf16[16,96,128]{2,1,0:T(8,128)(2,1)S(1)}, u32[]{:S(2)}, u32[]{:S(2)}) async-start(bf16[16,96,128]{2,1,0:T(8,128)(2,1)} %upper_sums.2), calls=%async_computation.2 | async-start | bytes 786432 | tf_op jit(solution)/shard_map/all_to_all | solution.py:504
  49.7 9.2 %copy-start = (bf16[8,1536,128]{2,1,0:T(8,128)(2,1)S(1)}, bf16[8,1536,128]{2,1,0:T(8,128)(2,1)}, u32[]{:S(2)}) copy-start(bf16[8,1536,128]{2,1,0:T(8,128)(2,1)} %basis_ref.3) | copy-start | bytes 9437188
  61.8 13.9 %all-to-all-start.3 = ((bf16[16,96,128]{2,1,0:T(8,128)(2,1)}), bf16[16,96,128]{2,1,0:T(8,128)(2,1)S(1)}, u32[]{:S(2)}, u32[]{:S(2)}) async-start(bf16[16,96,128]{2,1,0:T(8,128)(2,1)} %get-tuple-element.29), calls=%async_computation.3 | async-start | bytes 786432 | tf_op jit(solution)/shard_map/all_to_all | solution.py:504
  66.0 21.3 %collective-permute-start.3 = (bf16[3,192,512]{2,1,0:T(8,128)(2,1)}, bf16[3,192,512]{2,1,0:T(8,128)(2,1)}, u32[]{:S(2)}, u32[]{:S(2)}) collective-permute-start(bf16[3,192,512]{2,1,0:T(8,128)(2,1)} %get-tuple-element.31.own_hbm), channel_id=1, source_target_pairs={{1,0},{2,1},{3,2},{4,3},{5,4},{6,5},{7,6},{8,7},{9,8},{10,9},{11,1... | collective-permute-start | bytes 1769480 | tf_op jit(solution)/shard_map/ppermute | solution.py:511
  73.8 14.8 %collective-permute-start.2 = (bf16[3,192,512]{2,1,0:T(8,128)(2,1)}, bf16[3,192,512]{2,1,0:T(8,128)(2,1)}, u32[]{:S(2)}, u32[]{:S(2)}) collective-permute-start(bf16[3,192,512]{2,1,0:T(8,128)(2,1)} %get-tuple-element.31.own_hbm), channel_id=1, source_target_pairs={{0,1},{1,2},{2,3},{3,4},{4,5},{5,6},{6,7},{7,8},{8,9},{9,10},{10,1... | collective-permute-start | bytes 1769480 | tf_op jit(solution)/shard_map/ppermute | solution.py:511
  77.1 15.6 %all-to-all-start.4 = ((bf16[16,48,128]{2,1,0:T(8,128)(2,1)}), bf16[16,48,128]{2,1,0:T(8,128)(2,1)S(1)}, u32[]{:S(2)}, u32[]{:S(2)}) async-start(bf16[16,48,128]{2,1,0:T(8,128)(2,1)} %get-tuple-element.30), calls=%async_computation.4 | async-start | bytes 393216 | tf_op jit(solution)/shard_map/all_to_all | solution.py:504
  94.1 14.4 %all-to-all-start.5 = ((bf16[16,96,128]{2,1,0:T(8,128)(2,1)}), bf16[16,96,128]{2,1,0:T(8,128)(2,1)S(1)}, u32[]{:S(2)}, u32[]{:S(2)}) async-start(bf16[16,96,128]{2,1,0:T(8,128)(2,1)} %upper_sums.3), calls=%async_computation.5 | async-start | bytes 786432 | tf_op jit(solution)/shard_map/all_to_all | solution.py:504
  108.5 23.3 %copy-start.1 = (f32[3,64,1536]{2,1,0:T(8,128)S(1)}, f32[3,64,1536]{2,1,0:T(8,128)}, u32[]{:S(2)}) copy-start(f32[3,64,1536]{2,1,0:T(8,128)} %param.9) | copy-start | bytes 3538948
  108.5 23.3 %copy-start.2 = (f32[192,1536]{1,0:T(8,128)S(1)}, f32[192,1536]{1,0:T(8,128)}, u32[]{:S(2)}) copy-start(f32[192,1536]{1,0:T(8,128)} %get-tuple-element.36.residual_hbm.residual_ref) | copy-start | bytes 3538948
  108.5 23.3 %copy-start.3 = (f32[8,1536]{1,0:T(8,128)S(1)}, f32[8,1536]{1,0:T(8,128)}, u32[]{:S(2)}) copy-start(f32[8,1536]{1,0:T(8,128)} %sort_panels.1.rest_1_.sorted_ref) | copy-start | bytes 147460

commit v6 on v5

--- a/solution.py
+++ b/solution.py
@@ -147,15 +147,31 @@
 LOWER, UPPER = pl.ds(0, PART), pl.ds(PART, PART)
 
 
-def lower_kernel(place_ref, got_ref, back_hbm, up_hbm, low_ref, up_ref, sems):
+def plane_kernel(got_ref, up_hbm, up_ref, sem):
     total = got_ref[0, UPPER, :].astype(F32)
     for k in range(1, GROUP):
         total += got_ref[k, UPPER, :].astype(F32)
     total = total.astype(BF16)
     for k in range(GROUP):
         up_ref[k] = total
-    up_copy = pltpu.make_async_copy(up_ref, up_hbm, sems.at[0])
-    up_copy.start()
+    copy = pltpu.make_async_copy(up_ref, up_hbm, sem.at[0])
+    copy.start()
+    copy.wait()
+
+
+def plane_sums(got):
+    part = (GROUP, PART, RANK)
+    return call(
+        plane_kernel,
+        "plane_sums",
+        in_specs=[IN_VMEM],
+        out_specs=IN_HBM,
+        out_shape=pltpu.HBM(part, BF16),
+        scratch_shapes=[pltpu.VMEM(part, BF16), pltpu.SemaphoreType.DMA((1,))],
+    )(in_vmem(got))
+
+
+def lower_kernel(place_ref, got_ref, back_hbm, low_ref, sem):
     level = place_ref[0] // QUARTERS
     width = 1
     sums = [got_ref[k, LOWER, :].astype(F32) for k in range(GROUP)]
@@ -169,24 +185,21 @@
             for k in range(GROUP):
                 low_ref[k] = (sums[k // width] * gain(own_level)).astype(BF16)
 
-    low_copy = pltpu.make_async_copy(low_ref, back_hbm.at[:, LOWER, :], sems.at[1])
-    low_copy.start()
-    up_copy.wait()
-    low_copy.wait()
+    copy = pltpu.make_async_copy(low_ref, back_hbm.at[:, LOWER, :], sem.at[0])
+    copy.start()
+    copy.wait()
 
 
 def lower_sums(place, got):
-    part = (GROUP, PART, RANK)
     return call(
         lower_kernel,
         "lower_sums",
         in_specs=[SCALARS, IN_VMEM],
-        out_specs=[IN_HBM] * 2,
-        out_shape=[SENT, pltpu.HBM(part, BF16)],
-        scratch_shapes=[
-            pltpu.VMEM(part, BF16),
-            pltpu.VMEM(part, BF16),
-            pltpu.SemaphoreType.DMA((2,)),
+        out_specs=IN_HBM,
+        out_shape=SENT,
+        scratch_shapes=[
+            pltpu.VMEM((GROUP, PART, RANK), BF16),
+            pltpu.SemaphoreType.DMA((1,)),
         ],
     )(place, in_vmem(got))
 
@@ -513,7 +526,9 @@
 
 def operator(place, low, sent, *early):
     sides = beside(low)
-    lower, up = lower_sums(place, swap(sent, NARROW))
+    got = swap(sent, NARROW)
+    up = plane_sums(got)
+    lower = lower_sums(place, got)
     upper, sides, early = lax.optimization_barrier((swap(up, WIDE), sides, early))
     return sides, swap(upper_sums(place, upper, lower), NARROW), early
 

time: 135 us -> 135 us (level)
  waiting for transfers between devices: 24.1 us -> 21.4 us
  Pallas kernels: 31.5 us -> 33.3 us
    all_to_all x6, waiting for transfers between devices: 17.9 us -> 15.8 us  [swap(): return lax.all_to_all(blocks, axes, 0, 0)]
    pallas_call x2 -> x4, Pallas kernels: 2.69 us -> 4.03 us  [the longest x2 2.59 us: lower_sums(): call(lower_kernel, 'lower_sums', in_specs=[SCALARS, IN_VMEM], out_specs=I...]
  transfers between devices with their start and end apart: 10 -> 10, of which waited for: 6 -> 6; matrix products, arithmetic and copies ran while one was open for 0% -> 0% of each run, Pallas kernels for 13% -> 14%
where the time goes in v6:
time: 135 us; the launch traced here: 134 us
  starting transfers between devices  57.1 us (42%)
  Pallas kernels  33.3 us (25%)
  waiting for transfers between devices  21.4 us (16%)
  blocking collectives  20.5 us (15%)
    all_to_all x6, starting transfers between devices, swap(): return lax.all_to_all(blocks, axes, 0, 0)  37.7 us
    all_to_all x1, blocking collectives, swap(): return lax.all_to_all(blocks, axes, 0, 0)  20.5 us
    all_to_all x6, waiting for transfers between devices, swap(): return lax.all_to_all(blocks, axes, 0, 0)  15.8 us
    ppermute x2, starting transfers between devices, beside(): lax.ppermute(blocks, WIDE_NARROW, down)  15.6 us
    pallas_call x2, Pallas kernels, near_field(): call(near_kernel_body, 'near_field', in_specs=[SCALARS] + [IN_HBM] * 4 +...  12.8 us
    ppermute x2, waiting for transfers between devices, beside(): lax.ppermute(blocks, WIDE_NARROW, down)  4.09 us
    ppermute x2, starting transfers between devices, beside(): lax.ppermute(blocks, WIDE_NARROW, up)  3.84 us
    pallas_call x1, Pallas kernels, first_coefs(): call(coef_kernel, 'first_coefs', in_specs=[IN_HBM] * 2, out_specs=[IN_HBM...  3.4 us
  transfers between devices with their start and end apart: 10, of which 6 were waited for; matrix products, arithmetic and copies ran while one was open for 0% of the time, Pallas kernels for 14%

profile of v6, /device:TPU:1, one launch (start us, length us, event | category | flops | bytes accessed | tf_op | source)
XLA Modules:
  0.0 133.7 jit_solution(14894710908509589124)
XLA Ops:
  0.6 0.0 copy-start.9
  0.6 0.0 copy-start.10
  0.7 0.0 copy-start.11
  0.7 3.4 %first_coefs.1 = (bf16[3,192,512]{2,1,0:T(8,128)(2,1)}, bf16[16,96,128]{2,1,0:T(8,128)(2,1)}) custom-call(f32[192,1536]{1,0:T(8,128)} %bitcast.6, bf16[8,1536,128]{2,1,0:T(8,128)(2,1)} %basis_ref.3), custom_call_target="tpu_custom_call" | custom-call | tf_op jit(solution)/shard_map/first_coefs/pallas_call | solution.py:129
  4.1 0.0 copy-start.8
  4.1 7.6 %all-to-all-start = ((bf16[16,96,128]{2,1,0:T(8,128)(2,1)}), bf16[16,96,128]{2,1,0:T(8,128)(2,1)S(1)}, u32[]{:S(2)}, u32[]{:S(2)}) async-start(bf16[16,96,128]{2,1,0:T(8,128)(2,1)} %get-tuple-element.17), calls=%async_computation | async-start | bytes 786432 | tf_op jit(solution)/shard_map/all_to_all | solution.py:517
  11.7 7.7 %collective-permute-start.1 = (bf16[3,192,512]{2,1,0:T(8,128)(2,1)}, bf16[3,192,512]{2,1,0:T(8,128)(2,1)S(1)}, u32[]{:S(2)}, u32[]{:S(2)}) collective-permute-start(bf16[3,192,512]{2,1,0:T(8,128)(2,1)} %get-tuple-element.18.own_hbm), channel_id=1, source_target_pairs={{1,0},{2,1},{3,2},{4,3},{5,4},{6,5},{7,6},{8,7},{9,8},{10,9},{11,1... | collective-permute-start | bytes 1769480 | tf_op jit(solution)/shard_map/ppermute | solution.py:524
  19.4 1.9 %collective-permute-start = (bf16[3,192,512]{2,1,0:T(8,128)(2,1)}, bf16[3,192,512]{2,1,0:T(8,128)(2,1)S(1)}, u32[]{:S(2)}, u32[]{:S(2)}) collective-permute-start(bf16[3,192,512]{2,1,0:T(8,128)(2,1)} %get-tuple-element.18.own_hbm), channel_id=1, source_target_pairs={{0,1},{1,2},{2,3},{3,4},{4,5},{5,6},{6,7},{7,8},{8,9},{9,10},{10,1... | collective-permute-start | bytes 1769480 | tf_op jit(solution)/shard_map/ppermute | solution.py:524
  21.4 0.0 copy-done.10
  21.4 0.1 pad.3.clone
  21.5 0.0 all-to-all-done.got_ref
  21.5 0.7 plane_sums.2
  22.3 9.4 %all-to-all-start.1 = ((bf16[16,48,128]{2,1,0:T(8,128)(2,1)}), bf16[16,48,128]{2,1,0:T(8,128)(2,1)S(1)}, u32[]{:S(2)}, u32[]{:S(2)}) async-start(bf16[16,48,128]{2,1,0:T(8,128)(2,1)} %plane_sums.2), calls=%async_computation.1 | async-start | bytes 393216 | tf_op jit(solution)/shard_map/all_to_all | solution.py:517
  31.7 0.0 copy-done.8
  31.7 0.1 maximum_maximum_fusion.values_ref
  31.8 2.0 %sort_panels.1.rest_1_.sorted_ref = f32[8,1536]{1,0:T(8,128)} custom-call(s32[1,1536]{1,0:T(1,128)S(1)} %broadcast_in_dim.20.order_ref, f32[8,1536]{1,0:T(8,128)S(1)} %maximum_maximum_fusion.values_ref), custom_call_target="tpu_custom_call" | custom-call | tf_op jit(solution)/shard_map/sort_panels/pallas_call | solution.py:460
  33.7 0.1 pad_add_fusion.place_ref
  33.8 1.3 lower_sums.2._
  35.1 0.0 collective-permute-done.1.right_hbm
  35.2 0.0 collective-permute-done.left_hbm
  35.2 0.0 copy-start.7
  35.2 6.8 %all-to-all-done.1.got_ref = bf16[16,48,128]{2,1,0:T(8,128)(2,1)S(1)} async-done(((bf16[16,48,128]{2,1,0:T(8,128)(2,1)}), bf16[16,48,128]{2,1,0:T(8,128)(2,1)S(1)}, u32[]{:S(2)}, u32[]{:S(2)}) %all-to-all-start.1) | async-done | bytes 196640 | tf_op jit(solution)/shard_map/all_to_all | solution.py:517
  42.0 1.3 %upper_sums.2 = bf16[16,96,128]{2,1,0:T(8,128)(2,1)} custom-call(s32[2]{0:T(128)S(1)} %pad_add_fusion.place_ref, bf16[16,48,128]{2,1,0:T(8,128)(2,1)S(1)} %all-to-all-done.1.got_ref, bf16[16,96,128]{2,1,0:T(8,128)(2,1)} %lower_sums.2._), custom_call_target="tpu_custom_call", output_to_operand_aliasing={{}: (2, {})} | custom-call | tf_op jit(solution)/shard_map/upper_sums/pallas_call | solution.py:227
  43.4 5.6 %all-to-all-start.2 = ((bf16[16,96,128]{2,1,0:T(8,128)(2,1)}), bf16[16,96,128]{2,1,0:T(8,128)(2,1)S(1)}, u32[]{:S(2)}, u32[]{:S(2)}) async-start(bf16[16,96,128]{2,1,0:T(8,128)(2,1)} %upper_sums.2), calls=%async_computation.2 | async-start | bytes 786432 | tf_op jit(solution)/shard_map/all_to_all | solution.py:517
  49.0 0.0 copy-start
  49.0 6.7 %near_field.2.near_hbm = f32[192,1536]{1,0:T(8,128)} custom-call(s32[3,4]{1,0:T(4,128)S(1)} %copy-done.4, bf16[3,192,512]{2,1,0:T(8,128)(2,1)} %copy-done.7, bf16[3,192,512]{2,1,0:T(8,128)(2,1)} %get-tuple-element.18.own_hbm, bf16[3,192,512]{2,1,0:T(8,128)(2,1)} %copy-done.6, bf16[3,4,512,512]{3,2,1,0:T(8,128)(2,1)} %kernel_hbm.3, f32[3,64]{1,0:T(4,128)S(1)} %copy-done.5, ...), custom_call_target="tpu_custom_call" | custom-call | tf_op jit(solution)/shard_map/near_field/pallas_call | solution.py:312
  55.7 2.5 %all-to-all-done.2.got_ref = bf16[16,96,128]{2,1,0:T(8,128)(2,1)S(1)} async-done(((bf16[16,96,128]{2,1,0:T(8,128)(2,1)}), bf16[16,96,128]{2,1,0:T(8,128)(2,1)S(1)}, u32[]{:S(2)}, u32[]{:S(2)}) %all-to-all-start.2) | async-done | bytes 393248 | tf_op jit(solution)/shard_map/all_to_all | solution.py:517
  58.3 0.0 copy-done
  58.3 2.9 %residual.1 = (f32[192,1536]{1,0:T(8,128)}, bf16[3,192,512]{2,1,0:T(8,128)(2,1)}, bf16[16,96,128]{2,1,0:T(8,128)(2,1)}) custom-call(bf16[16,96,128]{2,1,0:T(8,128)(2,1)S(1)} %all-to-all-done.2.got_ref, f32[192,1536]{1,0:T(8,128)} %near_field.2.near_hbm, bf16[8,1536,128]{2,1,0:T(8,128)(2,1)S(1)} %copy-done), custom_call_target="tpu_custom_call" | custom-call | tf_op jit(solution)/shard_map/residual/pallas_call | solution.py:389
  61.2 4.1 %all-to-all-start.3 = ((bf16[16,96,128]{2,1,0:T(8,128)(2,1)}), bf16[16,96,128]{2,1,0:T(8,128)(2,1)S(1)}, u32[]{:S(2)}, u32[]{:S(2)}) async-start(bf16[16,96,128]{2,1,0:T(8,128)(2,1)} %get-tuple-element.23), calls=%async_computation.3 | async-start | bytes 786432 | tf_op jit(solution)/shard_map/all_to_all | solution.py:517
  65.3 7.9 %collective-permute-start.3 = (bf16[3,192,512]{2,1,0:T(8,128)(2,1)}, bf16[3,192,512]{2,1,0:T(8,128)(2,1)}, u32[]{:S(2)}, u32[]{:S(2)}) collective-permute-start(bf16[3,192,512]{2,1,0:T(8,128)(2,1)} %get-tuple-element.24.own_hbm), channel_id=1, source_target_pairs={{1,0},{2,1},{3,2},{4,3},{5,4},{6,5},{7,6},{8,7},{9,8},{10,9},{11,1... | collective-permute-start | bytes 1769480 | tf_op jit(solution)/shard_map/ppermute | solution.py:524
  73.2 1.9 %collective-permute-start.2 = (bf16[3,192,512]{2,1,0:T(8,128)(2,1)}, bf16[3,192,512]{2,1,0:T(8,128)(2,1)}, u32[]{:S(2)}, u32[]{:S(2)}) collective-permute-start(bf16[3,192,512]{2,1,0:T(8,128)(2,1)} %get-tuple-element.24.own_hbm), channel_id=1, source_target_pairs={{0,1},{1,2},{2,3},{3,4},{4,5},{5,6},{6,7},{7,8},{8,9},{9,10},{10,1... | collective-permute-start | bytes 1769480 | tf_op jit(solution)/shard_map/ppermute | solution.py:524
  75.1 0.0 all-to-all-done.3.got_ref
  75.1 0.7 plane_sums.3
  75.8 5.4 %all-to-all-start.4 = ((bf16[16,48,128]{2,1,0:T(8,128)(2,1)}), bf16[16,48,128]{2,1,0:T(8,128)(2,1)}, u32[]{:S(2)}, u32[]{:S(2)}) async-start(bf16[16,48,128]{2,1,0:T(8,128)(2,1)} %plane_sums.3), calls=%async_computation.4 | async-start | bytes 393216 | tf_op jit(solution)/shard_map/all_to_all | solution.py:517
  81.2 1.3 lower_sums.3._
  82.5 4.1 %collective-permute-done.3.right_hbm = bf16[3,192,512]{2,1,0:T(8,128)(2,1)} collective-permute-done((bf16[3,192,512]{2,1,0:T(8,128)(2,1)}, bf16[3,192,512]{2,1,0:T(8,128)(2,1)}, u32[]{:S(2)}, u32[]{:S(2)}) %collective-permute-start.3) | collective-permute-done | bytes 589856 | tf_op jit(solution)/shard_map/ppermute | solution.py:524
  86.6 1.5 %collective-permute-done.2.left_hbm = bf16[3,192,512]{2,1,0:T(8,128)(2,1)} collective-permute-done((bf16[3,192,512]{2,1,0:T(8,128)(2,1)}, bf16[3,192,512]{2,1,0:T(8,128)(2,1)}, u32[]{:S(2)}, u32[]{:S(2)}) %collective-permute-start.2) | collective-permute-done | bytes 589856 | tf_op jit(solution)/shard_map/ppermute | solution.py:524
  88.1 3.5 %all-to-all-done.4.got_ref = bf16[16,48,128]{2,1,0:T(8,128)(2,1)} async-done(((bf16[16,48,128]{2,1,0:T(8,128)(2,1)}), bf16[16,48,128]{2,1,0:T(8,128)(2,1)}, u32[]{:S(2)}, u32[]{:S(2)}) %all-to-all-start.4) | async-done | bytes 196640 | tf_op jit(solution)/shard_map/all_to_all | solution.py:517
  91.7 1.7 %upper_sums.3 = bf16[16,96,128]{2,1,0:T(8,128)(2,1)} custom-call(s32[2]{0:T(128)S(1)} %pad_add_fusion.place_ref, bf16[16,48,128]{2,1,0:T(8,128)(2,1)} %all-to-all-done.4.got_ref, bf16[16,96,128]{2,1,0:T(8,128)(2,1)} %lower_sums.3._), custom_call_target="tpu_custom_call", output_to_operand_aliasing={{}: (2, {})} | custom-call | tf_op jit(solution)/shard_map/upper_sums/pallas_call | solution.py:227
  93.4 5.5 %all-to-all-start.5 = ((bf16[16,96,128]{2,1,0:T(8,128)(2,1)}), bf16[16,96,128]{2,1,0:T(8,128)(2,1)S(1)}, u32[]{:S(2)}, u32[]{:S(2)}) async-start(bf16[16,96,128]{2,1,0:T(8,128)(2,1)} %upper_sums.3), calls=%async_computation.5 | async-start | bytes 786432 | tf_op jit(solution)/shard_map/all_to_all | solution.py:517
  98.9 6.1 %near_field.3.near_hbm = f32[192,1536]{1,0:T(8,128)} custom-call(s32[3,4]{1,0:T(4,128)S(1)} %copy-done.4, bf16[3,192,512]{2,1,0:T(8,128)(2,1)} %collective-permute-done.2.left_hbm, bf16[3,192,512]{2,1,0:T(8,128)(2,1)} %get-tuple-element.24.own_hbm, bf16[3,192,512]{2,1,0:T(8,128)(2,1)} %collective-permute-done.3.right_hbm, bf16[3,4,512,512]{3,2,1,0:T(8,128)(2,1)} %kernel_hbm.3), custom_call_target="tpu_custom_call" | custom-call | tf_op jit(solution)/shard_map/near_field/pallas_call | solution.py:312
  105.1 2.9 %all-to-all-done.5.got_ref = bf16[16,96,128]{2,1,0:T(8,128)(2,1)S(1)} async-done(((bf16[16,96,128]{2,1,0:T(8,128)(2,1)}), bf16[16,96,128]{2,1,0:T(8,128)(2,1)S(1)}, u32[]{:S(2)}, u32[]{:S(2)}) %all-to-all-start.5) | async-done | bytes 393248 | tf_op jit(solution)/shard_map/all_to_all | solution.py:517
  108.0 2.8 %products.1 = f32[1,128]{1,0:T(1,128)S(1)} custom-call(bf16[16,96,128]{2,1,0:T(8,128)(2,1)S(1)} %all-to-all-done.5.got_ref, f32[192,1536]{1,0:T(8,128)} %near_field.3.near_hbm, f32[192,1536]{1,0:T(8,128)} %get-tuple-element.28.residual_hbm.residual_ref, bf16[8,1536,128]{2,1,0:T(8,128)(2,1)S(1)} %copy-done), custom_call_target="tpu_custom_call" | custom-call | tf_op jit(solution)/shard_map/products/pallas_call | solution.py:427
  110.8 0.1 broadcast_in_dim.25
  110.9 20.5 %all_to_all.35.got_ref = f32[256,1,128]{2,1,0:T(1,128)S(1)} all-to-all(f32[256,1,128]{2,1,0:T(1,128)S(1)} %broadcast_in_dim.25), channel_id=1, replica_groups=mesh['wide_0'=8,'wide_1'=2,'narrow_0'=4,'narrow_1'=4] {'wide_0','wide_1'..., dimensions={0} | all-to-all | bytes 262144 | tf_op jit(solution)/shard_map/all_to_all | solution.py:517
  131.4 0.0 copy-done.2
  131.4 2.3 %final.1 = (f32[192,1536]{1,0:T(8,128)}, f32[64]{0:T(128)}) custom-call(f32[256,1,128]{2,1,0:T(1,128)S(1)} %all_to_all.35.got_ref, f32[192,1536]{1,0:T(8,128)S(1)} %bitcast.7, f32[192,1536]{1,0:T(8,128)S(1)} %copy-done.2, f32[8,1536]{1,0:T(8,128)S(1)} %copy-done.3), custom_call_target="tpu_custom_call" | custom-call | tf_op jit(solution)/shard_map/final/pallas_call | solution.py:503
  (19 shorter events, 0.1 us)
Async XLA Ops:
  0.6 20.7 %copy-start.9 = (f32[1536]{0:T(1024)S(1)}, f32[1536]{0:T(1024)}, u32[]{:S(2)}) copy-start(f32[1536]{0:T(1024)} %param.14) | copy-start | bytes 18436
  0.6 20.7 %copy-start.10 = (s32[1536]{0:T(1024)S(1)}, s32[1536]{0:T(1024)}, u32[]{:S(2)}) copy-start(s32[1536]{0:T(1024)} %param.16) | copy-start | bytes 18436
  0.7 20.7 %copy-start.11 = (s32[1536]{0:T(1024)S(1)}, s32[1536]{0:T(1024)}, u32[]{:S(2)}) copy-start(s32[1536]{0:T(1024)} %param.15) | copy-start | bytes 18436
  4.1 27.6 %copy-start.8 = (f32[3,1536]{1,0:T(4,128)S(1)}, f32[3,1536]{1,0:T(4,128)}, u32[]{:S(2)}) copy-start(f32[3,1536]{1,0:T(4,128)} %param.13) | copy-start | bytes 55300
  4.1 17.4 %all-to-all-start = ((bf16[16,96,128]{2,1,0:T(8,128)(2,1)}), bf16[16,96,128]{2,1,0:T(8,128)(2,1)S(1)}, u32[]{:S(2)}, u32[]{:S(2)}) async-start(bf16[16,96,128]{2,1,0:T(8,128)(2,1)} %get-tuple-element.17), calls=%async_computation | async-start | bytes 786432 | tf_op jit(solution)/shard_map/all_to_all | solution.py:517
  11.7 23.5 %collective-permute-start.1 = (bf16[3,192,512]{2,1,0:T(8,128)(2,1)}, bf16[3,192,512]{2,1,0:T(8,128)(2,1)S(1)}, u32[]{:S(2)}, u32[]{:S(2)}) collective-permute-start(bf16[3,192,512]{2,1,0:T(8,128)(2,1)} %get-tuple-element.18.own_hbm), channel_id=1, source_target_pairs={{1,0},{2,1},{3,2},{4,3},{5,4},{6,5},{7,6},{8,7},{9,8},{10,9},{11,1... | collective-permute-start | bytes 1769480 | tf_op jit(solution)/shard_map/ppermute | solution.py:524
  19.4 15.8 %collective-permute-start = (bf16[3,192,512]{2,1,0:T(8,128)(2,1)}, bf16[3,192,512]{2,1,0:T(8,128)(2,1)S(1)}, u32[]{:S(2)}, u32[]{:S(2)}) collective-permute-start(bf16[3,192,512]{2,1,0:T(8,128)(2,1)} %get-tuple-element.18.own_hbm), channel_id=1, source_target_pairs={{0,1},{1,2},{2,3},{3,4},{4,5},{5,6},{6,7},{7,8},{8,9},{9,10},{10,1... | collective-permute-start | bytes 1769480 | tf_op jit(solution)/shard_map/ppermute | solution.py:524
  22.3 19.7 %all-to-all-start.1 = ((bf16[16,48,128]{2,1,0:T(8,128)(2,1)}), bf16[16,48,128]{2,1,0:T(8,128)(2,1)S(1)}, u32[]{:S(2)}, u32[]{:S(2)}) async-start(bf16[16,48,128]{2,1,0:T(8,128)(2,1)} %plane_sums.2), calls=%async_computation.1 | async-start | bytes 393216 | tf_op jit(solution)/shard_map/all_to_all | solution.py:517
  33.8 15.2 %copy-start.4 = (s32[3,4]{1,0:T(4,128)S(1)}, s32[3,4]{1,0:T(4,128)}, u32[]{:S(2)}) copy-start(s32[3,4]{1,0:T(4,128)} %slots_ref.3) | copy-start | bytes 148
  33.8 15.2 %copy-start.5 = (f32[3,64]{1,0:T(4,128)S(1)}, f32[3,64]{1,0:T(4,128)}, u32[]{:S(2)}) copy-start(f32[3,64]{1,0:T(4,128)} %rest_0_.1) | copy-start | bytes 2308
  35.1 8.2 %copy-start.6 = (bf16[3,192,512]{2,1,0:T(8,128)(2,1)}, bf16[3,192,512]{2,1,0:T(8,128)(2,1)S(1)}, u32[]{:S(2)}) copy-start(bf16[3,192,512]{2,1,0:T(8,128)(2,1)S(1)} %collective-permute-done.1.right_hbm) | copy-start | bytes 1769476
  35.2 8.2 %copy-start.7 = (bf16[3,192,512]{2,1,0:T(8,128)(2,1)}, bf16[3,192,512]{2,1,0:T(8,128)(2,1)S(1)}, u32[]{:S(2)}) copy-start(bf16[3,192,512]{2,1,0:T(8,128)(2,1)S(1)} %collective-permute-done.left_hbm) | copy-start | bytes 1769476
  43.4 14.9 %all-to-all-start.2 = ((bf16[16,96,128]{2,1,0:T(8,128)(2,1)}), bf16[16,96,128]{2,1,0:T(8,128)(2,1)S(1)}, u32[]{:S(2)}, u32[]{:S(2)}) async-start(bf16[16,96,128]{2,1,0:T(8,128)(2,1)} %upper_sums.2), calls=%async_computation.2 | async-start | bytes 786432 | tf_op jit(solution)/shard_map/all_to_all | solution.py:517
  49.0 9.2 %copy-start = (bf16[8,1536,128]{2,1,0:T(8,128)(2,1)S(1)}, bf16[8,1536,128]{2,1,0:T(8,128)(2,1)}, u32[]{:S(2)}) copy-start(bf16[8,1536,128]{2,1,0:T(8,128)(2,1)} %basis_ref.3) | copy-start | bytes 9437188
  61.2 13.9 %all-to-all-start.3 = ((bf16[16,96,128]{2,1,0:T(8,128)(2,1)}), bf16[16,96,128]{2,1,0:T(8,128)(2,1)S(1)}, u32[]{:S(2)}, u32[]{:S(2)}) async-start(bf16[16,96,128]{2,1,0:T(8,128)(2,1)} %get-tuple-element.23), calls=%async_computation.3 | async-start | bytes 786432 | tf_op jit(solution)/shard_map/all_to_all | solution.py:517
  65.3 21.3 %collective-permute-start.3 = (bf16[3,192,512]{2,1,0:T(8,128)(2,1)}, bf16[3,192,512]{2,1,0:T(8,128)(2,1)}, u32[]{:S(2)}, u32[]{:S(2)}) collective-permute-start(bf16[3,192,512]{2,1,0:T(8,128)(2,1)} %get-tuple-element.24.own_hbm), channel_id=1, source_target_pairs={{1,0},{2,1},{3,2},{4,3},{5,4},{6,5},{7,6},{8,7},{9,8},{10,9},{11,1... | collective-permute-start | bytes 1769480 | tf_op jit(solution)/shard_map/ppermute | solution.py:524
  73.2 15.0 %collective-permute-start.2 = (bf16[3,192,512]{2,1,0:T(8,128)(2,1)}, bf16[3,192,512]{2,1,0:T(8,128)(2,1)}, u32[]{:S(2)}, u32[]{:S(2)}) collective-permute-start(bf16[3,192,512]{2,1,0:T(8,128)(2,1)} %get-tuple-element.24.own_hbm), channel_id=1, source_target_pairs={{0,1},{1,2},{2,3},{3,4},{4,5},{5,6},{6,7},{7,8},{8,9},{9,10},{10,1... | collective-permute-start | bytes 1769480 | tf_op jit(solution)/shard_map/ppermute | solution.py:524
  75.8 15.8 %all-to-all-start.4 = ((bf16[16,48,128]{2,1,0:T(8,128)(2,1)}), bf16[16,48,128]{2,1,0:T(8,128)(2,1)}, u32[]{:S(2)}, u32[]{:S(2)}) async-start(bf16[16,48,128]{2,1,0:T(8,128)(2,1)} %plane_sums.3), calls=%async_computation.4 | async-start | bytes 393216 | tf_op jit(solution)/shard_map/all_to_all | solution.py:517
  93.4 14.6 %all-to-all-start.5 = ((bf16[16,96,128]{2,1,0:T(8,128)(2,1)}), bf16[16,96,128]{2,1,0:T(8,128)(2,1)S(1)}, u32[]{:S(2)}, u32[]{:S(2)}) async-start(bf16[16,96,128]{2,1,0:T(8,128)(2,1)} %upper_sums.3), calls=%async_computation.5 | async-start | bytes 786432 | tf_op jit(solution)/shard_map/all_to_all | solution.py:517
  107.9 23.4 %copy-start.1 = (f32[3,64,1536]{2,1,0:T(8,128)S(1)}, f32[3,64,1536]{2,1,0:T(8,128)}, u32[]{:S(2)}) copy-start(f32[3,64,1536]{2,1,0:T(8,128)} %param.9) | copy-start | bytes 3538948
  107.9 23.4 %copy-start.2 = (f32[192,1536]{1,0:T(8,128)S(1)}, f32[192,1536]{1,0:T(8,128)}, u32[]{:S(2)}) copy-start(f32[192,1536]{1,0:T(8,128)} %get-tuple-element.28.residual_hbm.residual_ref) | copy-start | bytes 3538948
  108.0 23.4 %copy-start.3 = (f32[8,1536]{1,0:T(8,128)S(1)}, f32[8,1536]{1,0:T(8,128)}, u32[]{:S(2)}) copy-start(f32[8,1536]{1,0:T(8,128)} %sort_panels.1.rest_1_.sorted_ref) | copy-start | bytes 147460

commit v7 on v6

--- a/solution.py
+++ b/solution.py
@@ -20,6 +20,8 @@
 PAN = 1536
 BLK = 512
 CHUNKS = PAN // BLK
+PIECE = 256
+PIECES = PAN // PIECE
 LEVELS = 8
 HALF = LEVELS // 2
 RANK = 128
@@ -82,8 +84,8 @@
 def coef_kernel(field_hbm, basis_hbm, low_hbm, sent_hbm, *scratch):
     field_ref, low_ref, basis_ref, acc_ref, sent_ref, sems, sent_sems = scratch
     arriving, leaving = [], []
-    for chunk in range(CHUNKS):
-        panels = pl.ds(chunk * BLK, BLK)
+    for chunk in range(PIECES):
+        panels = pl.ds(chunk * PIECE, PIECE)
         arriving.append(
             (
                 pltpu.make_async_copy(
@@ -96,14 +98,16 @@
         )
         for copy in arriving[-1]:
             copy.start()
-    for chunk in range(CHUNKS):
+    for chunk in range(PIECES):
         for copy in arriving[chunk]:
             copy.wait()
         values = field_ref[chunk].astype(BF16)
-        low_ref[chunk] = values
-        copy = pltpu.make_async_copy(low_ref.at[chunk], low_hbm.at[chunk], sems.at[2, chunk])
-        copy.start()
-        leaving.append(copy)
+        block, start = divmod(chunk * PIECE, BLK)
+        low_ref[block, :, start : start + PIECE] = values
+        if start + PIECE == BLK:
+            copy = pltpu.make_async_copy(low_ref.at[block], low_hbm.at[block], sems.at[2, block])
+            copy.start()
+            leaving.append(copy)
         for level in range(HALF):
             pair = jnp.concatenate(
                 [basis_ref[chunk, level], basis_ref[chunk, HALF + level]], axis=1
@@ -111,7 +115,7 @@
             part = jnp.dot(values, pair, preferred_element_type=F32)
             if chunk > 0:
                 part += acc_ref[level]
-            if chunk < CHUNKS - 1:
+            if chunk < PIECES - 1:
                 acc_ref[level] = part
             else:
                 leaving.append(send_coefs(level, part, sent_ref, sent_hbm, sent_sems.at[level]))
@@ -133,12 +137,12 @@
         out_specs=[IN_HBM] * 2,
         out_shape=[BLOCKS, SENT],
         scratch_shapes=[
-            pltpu.VMEM((CHUNKS, ROWS, BLK), F32),
+            pltpu.VMEM((PIECES, ROWS, PIECE), F32),
             pltpu.VMEM(BLOCKS.shape, BF16),
-            pltpu.VMEM((CHUNKS, LEVELS, BLK, RANK), BF16),
+            pltpu.VMEM((PIECES, LEVELS, PIECE, RANK), BF16),
             pltpu.VMEM((HALF, ROWS, 2 * RANK), F32),
             pltpu.VMEM(SENT.shape, BF16),
-            pltpu.SemaphoreType.DMA((3, CHUNKS)),
+            pltpu.SemaphoreType.DMA((3, PIECES)),
             pltpu.SemaphoreType.DMA((HALF,)),
         ],
     )(in_hbm(field), in_hbm(far_basis))

time: 135 us -> 135 us (level)
  no operation moved by 1% of the time
where the time goes in v7:
time: 135 us; the launch traced here: 134 us
  starting transfers between devices  57.2 us (42%)
  Pallas kernels  33.3 us (25%)
  waiting for transfers between devices  21.4 us (16%)
  blocking collectives  20.5 us (15%)
    all_to_all x6, starting transfers between devices, swap(): return lax.all_to_all(blocks, axes, 0, 0)  37.7 us
    all_to_all x1, blocking collectives, swap(): return lax.all_to_all(blocks, axes, 0, 0)  20.5 us
    all_to_all x6, waiting for transfers between devices, swap(): return lax.all_to_all(blocks, axes, 0, 0)  15.8 us
    ppermute x2, starting transfers between devices, beside(): lax.ppermute(blocks, WIDE_NARROW, down)  15.6 us
    pallas_call x2, Pallas kernels, near_field(): call(near_kernel_body, 'near_field', in_specs=[SCALARS] + [IN_HBM] * 4 +...  12.8 us
    ppermute x2, waiting for transfers between devices, beside(): lax.ppermute(blocks, WIDE_NARROW, down)  4.07 us
    ppermute x2, starting transfers between devices, beside(): lax.ppermute(blocks, WIDE_NARROW, up)  3.84 us
    pallas_call x1, Pallas kernels, first_coefs(): call(coef_kernel, 'first_coefs', in_specs=[IN_HBM] * 2, out_specs=[IN_HBM...  3.4 us
  transfers between devices with their start and end apart: 10, of which 6 were waited for; matrix products, arithmetic and copies ran while one was open for 0% of the time, Pallas kernels for 14%

profile of v7, /device:TPU:1, one launch (start us, length us, event | category | flops | bytes accessed | tf_op | source)
XLA Modules:
  0.0 133.7 jit_solution(16615752742748673977)
XLA Ops:
  0.6 0.0 copy-start.9
  0.6 0.0 copy-start.10
  0.7 3.4 %first_coefs.1 = (bf16[3,192,512]{2,1,0:T(8,128)(2,1)}, bf16[16,96,128]{2,1,0:T(8,128)(2,1)}) custom-call(f32[192,1536]{1,0:T(8,128)} %bitcast.6, bf16[8,1536,128]{2,1,0:T(8,128)(2,1)} %basis_ref.3), custom_call_target="tpu_custom_call" | custom-call | tf_op jit(solution)/shard_map/first_coefs/pallas_call | solution.py:133
  4.1 0.0 copy-start.8
  4.1 7.6 %all-to-all-start = ((bf16[16,96,128]{2,1,0:T(8,128)(2,1)}), bf16[16,96,128]{2,1,0:T(8,128)(2,1)S(1)}, u32[]{:S(2)}, u32[]{:S(2)}) async-start(bf16[16,96,128]{2,1,0:T(8,128)(2,1)} %get-tuple-element.17), calls=%async_computation | async-start | bytes 786432 | tf_op jit(solution)/shard_map/all_to_all | solution.py:521
  11.7 7.7 %collective-permute-start.1 = (bf16[3,192,512]{2,1,0:T(8,128)(2,1)}, bf16[3,192,512]{2,1,0:T(8,128)(2,1)S(1)}, u32[]{:S(2)}, u32[]{:S(2)}) collective-permute-start(bf16[3,192,512]{2,1,0:T(8,128)(2,1)} %get-tuple-element.18.own_hbm), channel_id=1, source_target_pairs={{1,0},{2,1},{3,2},{4,3},{5,4},{6,5},{7,6},{8,7},{9,8},{10,9},{11,1... | collective-permute-start | bytes 1769480 | tf_op jit(solution)/shard_map/ppermute | solution.py:528
  19.4 1.9 %collective-permute-start = (bf16[3,192,512]{2,1,0:T(8,128)(2,1)}, bf16[3,192,512]{2,1,0:T(8,128)(2,1)S(1)}, u32[]{:S(2)}, u32[]{:S(2)}) collective-permute-start(bf16[3,192,512]{2,1,0:T(8,128)(2,1)} %get-tuple-element.18.own_hbm), channel_id=1, source_target_pairs={{0,1},{1,2},{2,3},{3,4},{4,5},{5,6},{6,7},{7,8},{8,9},{9,10},{10,1... | collective-permute-start | bytes 1769480 | tf_op jit(solution)/shard_map/ppermute | solution.py:528
  21.3 0.0 copy-done.9
  21.4 0.0 copy-done.11
  21.4 0.1 pad.3.clone
  21.5 0.0 all-to-all-done.got_ref
  21.5 0.7 plane_sums.2
  22.3 9.4 %all-to-all-start.1 = ((bf16[16,48,128]{2,1,0:T(8,128)(2,1)}), bf16[16,48,128]{2,1,0:T(8,128)(2,1)S(1)}, u32[]{:S(2)}, u32[]{:S(2)}) async-start(bf16[16,48,128]{2,1,0:T(8,128)(2,1)} %plane_sums.2), calls=%async_computation.1 | async-start | bytes 393216 | tf_op jit(solution)/shard_map/all_to_all | solution.py:521
  31.7 0.1 maximum_maximum_fusion.values_ref
  31.8 2.0 %sort_panels.1.rest_1_.sorted_ref = f32[8,1536]{1,0:T(8,128)} custom-call(s32[1,1536]{1,0:T(1,128)S(1)} %broadcast_in_dim.20.order_ref, f32[8,1536]{1,0:T(8,128)S(1)} %maximum_maximum_fusion.values_ref), custom_call_target="tpu_custom_call" | custom-call | tf_op jit(solution)/shard_map/sort_panels/pallas_call | solution.py:464
  33.7 0.1 pad_add_fusion.place_ref
  33.8 1.3 lower_sums.2._
  35.1 0.0 collective-permute-done.1.right_hbm
  35.2 0.0 copy-start.6
  35.2 0.0 collective-permute-done.left_hbm
  35.2 6.8 %all-to-all-done.1.got_ref = bf16[16,48,128]{2,1,0:T(8,128)(2,1)S(1)} async-done(((bf16[16,48,128]{2,1,0:T(8,128)(2,1)}), bf16[16,48,128]{2,1,0:T(8,128)(2,1)S(1)}, u32[]{:S(2)}, u32[]{:S(2)}) %all-to-all-start.1) | async-done | bytes 196640 | tf_op jit(solution)/shard_map/all_to_all | solution.py:521
  42.0 1.3 %upper_sums.2 = bf16[16,96,128]{2,1,0:T(8,128)(2,1)} custom-call(s32[2]{0:T(128)S(1)} %pad_add_fusion.place_ref, bf16[16,48,128]{2,1,0:T(8,128)(2,1)S(1)} %all-to-all-done.1.got_ref, bf16[16,96,128]{2,1,0:T(8,128)(2,1)} %lower_sums.2._), custom_call_target="tpu_custom_call", output_to_operand_aliasing={{}: (2, {})} | custom-call | tf_op jit(solution)/shard_map/upper_sums/pallas_call | solution.py:231
  43.4 5.6 %all-to-all-start.2 = ((bf16[16,96,128]{2,1,0:T(8,128)(2,1)}), bf16[16,96,128]{2,1,0:T(8,128)(2,1)S(1)}, u32[]{:S(2)}, u32[]{:S(2)}) async-start(bf16[16,96,128]{2,1,0:T(8,128)(2,1)} %upper_sums.2), calls=%async_computation.2 | async-start | bytes 786432 | tf_op jit(solution)/shard_map/all_to_all | solution.py:521
  49.0 0.0 copy-done.4
  49.0 0.0 copy-done.5
  49.0 0.0 copy-start
  49.0 6.7 %near_field.2.near_hbm = f32[192,1536]{1,0:T(8,128)} custom-call(s32[3,4]{1,0:T(4,128)S(1)} %copy-done.4, bf16[3,192,512]{2,1,0:T(8,128)(2,1)} %copy-done.7, bf16[3,192,512]{2,1,0:T(8,128)(2,1)} %get-tuple-element.18.own_hbm, bf16[3,192,512]{2,1,0:T(8,128)(2,1)} %copy-done.6, bf16[3,4,512,512]{3,2,1,0:T(8,128)(2,1)} %kernel_hbm.3, f32[3,64]{1,0:T(4,128)S(1)} %copy-done.5, ...), custom_call_target="tpu_custom_call" | custom-call | tf_op jit(solution)/shard_map/near_field/pallas_call | solution.py:316
  55.7 2.6 %all-to-all-done.2.got_ref = bf16[16,96,128]{2,1,0:T(8,128)(2,1)S(1)} async-done(((bf16[16,96,128]{2,1,0:T(8,128)(2,1)}), bf16[16,96,128]{2,1,0:T(8,128)(2,1)S(1)}, u32[]{:S(2)}, u32[]{:S(2)}) %all-to-all-start.2) | async-done | bytes 393248 | tf_op jit(solution)/shard_map/all_to_all | solution.py:521
  58.3 0.0 copy-done
  58.3 2.9 %residual.1 = (f32[192,1536]{1,0:T(8,128)}, bf16[3,192,512]{2,1,0:T(8,128)(2,1)}, bf16[16,96,128]{2,1,0:T(8,128)(2,1)}) custom-call(bf16[16,96,128]{2,1,0:T(8,128)(2,1)S(1)} %all-to-all-done.2.got_ref, f32[192,1536]{1,0:T(8,128)} %near_field.2.near_hbm, bf16[8,1536,128]{2,1,0:T(8,128)(2,1)S(1)} %copy-done), custom_call_target="tpu_custom_call" | custom-call | tf_op jit(solution)/shard_map/residual/pallas_call | solution.py:393
  61.2 4.1 %all-to-all-start.3 = ((bf16[16,96,128]{2,1,0:T(8,128)(2,1)}), bf16[16,96,128]{2,1,0:T(8,128)(2,1)S(1)}, u32[]{:S(2)}, u32[]{:S(2)}) async-start(bf16[16,96,128]{2,1,0:T(8,128)(2,1)} %get-tuple-element.23), calls=%async_computation.3 | async-start | bytes 786432 | tf_op jit(solution)/shard_map/all_to_all | solution.py:521
  65.3 7.9 %collective-permute-start.3 = (bf16[3,192,512]{2,1,0:T(8,128)(2,1)}, bf16[3,192,512]{2,1,0:T(8,128)(2,1)}, u32[]{:S(2)}, u32[]{:S(2)}) collective-permute-start(bf16[3,192,512]{2,1,0:T(8,128)(2,1)} %get-tuple-element.24.own_hbm), channel_id=1, source_target_pairs={{1,0},{2,1},{3,2},{4,3},{5,4},{6,5},{7,6},{8,7},{9,8},{10,9},{11,1... | collective-permute-start | bytes 1769480 | tf_op jit(solution)/shard_map/ppermute | solution.py:528
  73.2 1.9 %collective-permute-start.2 = (bf16[3,192,512]{2,1,0:T(8,128)(2,1)}, bf16[3,192,512]{2,1,0:T(8,128)(2,1)}, u32[]{:S(2)}, u32[]{:S(2)}) collective-permute-start(bf16[3,192,512]{2,1,0:T(8,128)(2,1)} %get-tuple-element.24.own_hbm), channel_id=1, source_target_pairs={{0,1},{1,2},{2,3},{3,4},{4,5},{5,6},{6,7},{7,8},{8,9},{9,10},{10,1... | collective-permute-start | bytes 1769480 | tf_op jit(solution)/shard_map/ppermute | solution.py:528
  75.1 0.0 all-to-all-done.3.got_ref
  75.1 0.7 plane_sums.3
  75.8 5.4 %all-to-all-start.4 = ((bf16[16,48,128]{2,1,0:T(8,128)(2,1)}), bf16[16,48,128]{2,1,0:T(8,128)(2,1)}, u32[]{:S(2)}, u32[]{:S(2)}) async-start(bf16[16,48,128]{2,1,0:T(8,128)(2,1)} %plane_sums.3), calls=%async_computation.4 | async-start | bytes 393216 | tf_op jit(solution)/shard_map/all_to_all | solution.py:521
  81.2 1.3 lower_sums.3._
  82.5 4.1 %collective-permute-done.3.right_hbm = bf16[3,192,512]{2,1,0:T(8,128)(2,1)} collective-permute-done((bf16[3,192,512]{2,1,0:T(8,128)(2,1)}, bf16[3,192,512]{2,1,0:T(8,128)(2,1)}, u32[]{:S(2)}, u32[]{:S(2)}) %collective-permute-start.3) | collective-permute-done | bytes 589856 | tf_op jit(solution)/shard_map/ppermute | solution.py:528
  86.6 1.5 %collective-permute-done.2.left_hbm = bf16[3,192,512]{2,1,0:T(8,128)(2,1)} collective-permute-done((bf16[3,192,512]{2,1,0:T(8,128)(2,1)}, bf16[3,192,512]{2,1,0:T(8,128)(2,1)}, u32[]{:S(2)}, u32[]{:S(2)}) %collective-permute-start.2) | collective-permute-done | bytes 589856 | tf_op jit(solution)/shard_map/ppermute | solution.py:528
  88.1 3.5 %all-to-all-done.4.got_ref = bf16[16,48,128]{2,1,0:T(8,128)(2,1)} async-done(((bf16[16,48,128]{2,1,0:T(8,128)(2,1)}), bf16[16,48,128]{2,1,0:T(8,128)(2,1)}, u32[]{:S(2)}, u32[]{:S(2)}) %all-to-all-start.4) | async-done | bytes 196640 | tf_op jit(solution)/shard_map/all_to_all | solution.py:521
  91.7 1.7 %upper_sums.3 = bf16[16,96,128]{2,1,0:T(8,128)(2,1)} custom-call(s32[2]{0:T(128)S(1)} %pad_add_fusion.place_ref, bf16[16,48,128]{2,1,0:T(8,128)(2,1)} %all-to-all-done.4.got_ref, bf16[16,96,128]{2,1,0:T(8,128)(2,1)} %lower_sums.3._), custom_call_target="tpu_custom_call", output_to_operand_aliasing={{}: (2, {})} | custom-call | tf_op jit(solution)/shard_map/upper_sums/pallas_call | solution.py:231
  93.4 5.5 %all-to-all-start.5 = ((bf16[16,96,128]{2,1,0:T(8,128)(2,1)}), bf16[16,96,128]{2,1,0:T(8,128)(2,1)S(1)}, u32[]{:S(2)}, u32[]{:S(2)}) async-start(bf16[16,96,128]{2,1,0:T(8,128)(2,1)} %upper_sums.3), calls=%async_computation.5 | async-start | bytes 786432 | tf_op jit(solution)/shard_map/all_to_all | solution.py:521
  98.9 6.1 %near_field.3.near_hbm = f32[192,1536]{1,0:T(8,128)} custom-call(s32[3,4]{1,0:T(4,128)S(1)} %copy-done.4, bf16[3,192,512]{2,1,0:T(8,128)(2,1)} %collective-permute-done.2.left_hbm, bf16[3,192,512]{2,1,0:T(8,128)(2,1)} %get-tuple-element.24.own_hbm, bf16[3,192,512]{2,1,0:T(8,128)(2,1)} %collective-permute-done.3.right_hbm, bf16[3,4,512,512]{3,2,1,0:T(8,128)(2,1)} %kernel_hbm.3), custom_call_target="tpu_custom_call" | custom-call | tf_op jit(solution)/shard_map/near_field/pallas_call | solution.py:316
  105.1 2.9 %all-to-all-done.5.got_ref = bf16[16,96,128]{2,1,0:T(8,128)(2,1)S(1)} async-done(((bf16[16,96,128]{2,1,0:T(8,128)(2,1)}), bf16[16,96,128]{2,1,0:T(8,128)(2,1)S(1)}, u32[]{:S(2)}, u32[]{:S(2)}) %all-to-all-start.5) | async-done | bytes 393248 | tf_op jit(solution)/shard_map/all_to_all | solution.py:521
  108.0 2.8 %products.1 = f32[1,128]{1,0:T(1,128)S(1)} custom-call(bf16[16,96,128]{2,1,0:T(8,128)(2,1)S(1)} %all-to-all-done.5.got_ref, f32[192,1536]{1,0:T(8,128)} %near_field.3.near_hbm, f32[192,1536]{1,0:T(8,128)} %get-tuple-element.28.residual_hbm.residual_ref, bf16[8,1536,128]{2,1,0:T(8,128)(2,1)S(1)} %copy-done), custom_call_target="tpu_custom_call" | custom-call | tf_op jit(solution)/shard_map/products/pallas_call | solution.py:431
  110.8 0.1 broadcast_in_dim.25
  110.9 20.5 %all_to_all.35.got_ref = f32[256,1,128]{2,1,0:T(1,128)S(1)} all-to-all(f32[256,1,128]{2,1,0:T(1,128)S(1)} %broadcast_in_dim.25), channel_id=1, replica_groups=mesh['wide_0'=8,'wide_1'=2,'narrow_0'=4,'narrow_1'=4] {'wide_0','wide_1'..., dimensions={0} | all-to-all | bytes 262144 | tf_op jit(solution)/shard_map/all_to_all | solution.py:521
  131.4 2.3 %final.1 = (f32[192,1536]{1,0:T(8,128)}, f32[64]{0:T(128)}) custom-call(f32[256,1,128]{2,1,0:T(1,128)S(1)} %all_to_all.35.got_ref, f32[192,1536]{1,0:T(8,128)S(1)} %bitcast.7, f32[192,1536]{1,0:T(8,128)S(1)} %copy-done.2, f32[8,1536]{1,0:T(8,128)S(1)} %copy-done.3), custom_call_target="tpu_custom_call" | custom-call | tf_op jit(solution)/shard_map/final/pallas_call | solution.py:507
  (19 shorter events, 0.1 us)
Async XLA Ops:
  0.6 20.7 %copy-start.9 = (f32[1536]{0:T(1024)S(1)}, f32[1536]{0:T(1024)}, u32[]{:S(2)}) copy-start(f32[1536]{0:T(1024)} %param.14) | copy-start | bytes 18436
  0.6 20.7 %copy-start.10 = (s32[1536]{0:T(1024)S(1)}, s32[1536]{0:T(1024)}, u32[]{:S(2)}) copy-start(s32[1536]{0:T(1024)} %param.16) | copy-start | bytes 18436
  0.7 20.7 %copy-start.11 = (s32[1536]{0:T(1024)S(1)}, s32[1536]{0:T(1024)}, u32[]{:S(2)}) copy-start(s32[1536]{0:T(1024)} %param.15) | copy-start | bytes 18436
  4.1 27.6 %copy-start.8 = (f32[3,1536]{1,0:T(4,128)S(1)}, f32[3,1536]{1,0:T(4,128)}, u32[]{:S(2)}) copy-start(f32[3,1536]{1,0:T(4,128)} %param.13) | copy-start | bytes 55300
  4.1 17.4 %all-to-all-start = ((bf16[16,96,128]{2,1,0:T(8,128)(2,1)}), bf16[16,96,128]{2,1,0:T(8,128)(2,1)S(1)}, u32[]{:S(2)}, u32[]{:S(2)}) async-start(bf16[16,96,128]{2,1,0:T(8,128)(2,1)} %get-tuple-element.17), calls=%async_computation | async-start | bytes 786432 | tf_op jit(solution)/shard_map/all_to_all | solution.py:521
  11.7 23.5 %collective-permute-start.1 = (bf16[3,192,512]{2,1,0:T(8,128)(2,1)}, bf16[3,192,512]{2,1,0:T(8,128)(2,1)S(1)}, u32[]{:S(2)}, u32[]{:S(2)}) collective-permute-start(bf16[3,192,512]{2,1,0:T(8,128)(2,1)} %get-tuple-element.18.own_hbm), channel_id=1, source_target_pairs={{1,0},{2,1},{3,2},{4,3},{5,4},{6,5},{7,6},{8,7},{9,8},{10,9},{11,1... | collective-permute-start | bytes 1769480 | tf_op jit(solution)/shard_map/ppermute | solution.py:528
  19.4 15.8 %collective-permute-start = (bf16[3,192,512]{2,1,0:T(8,128)(2,1)}, bf16[3,192,512]{2,1,0:T(8,128)(2,1)S(1)}, u32[]{:S(2)}, u32[]{:S(2)}) collective-permute-start(bf16[3,192,512]{2,1,0:T(8,128)(2,1)} %get-tuple-element.18.own_hbm), channel_id=1, source_target_pairs={{0,1},{1,2},{2,3},{3,4},{4,5},{5,6},{6,7},{7,8},{8,9},{9,10},{10,1... | collective-permute-start | bytes 1769480 | tf_op jit(solution)/shard_map/ppermute | solution.py:528
  22.3 19.8 %all-to-all-start.1 = ((bf16[16,48,128]{2,1,0:T(8,128)(2,1)}), bf16[16,48,128]{2,1,0:T(8,128)(2,1)S(1)}, u32[]{:S(2)}, u32[]{:S(2)}) async-start(bf16[16,48,128]{2,1,0:T(8,128)(2,1)} %plane_sums.2), calls=%async_computation.1 | async-start | bytes 393216 | tf_op jit(solution)/shard_map/all_to_all | solution.py:521
  33.8 15.2 %copy-start.4 = (s32[3,4]{1,0:T(4,128)S(1)}, s32[3,4]{1,0:T(4,128)}, u32[]{:S(2)}) copy-start(s32[3,4]{1,0:T(4,128)} %slots_ref.3) | copy-start | bytes 148
  33.8 15.2 %copy-start.5 = (f32[3,64]{1,0:T(4,128)S(1)}, f32[3,64]{1,0:T(4,128)}, u32[]{:S(2)}) copy-start(f32[3,64]{1,0:T(4,128)} %rest_0_.1) | copy-start | bytes 2308
  35.2 8.2 %copy-start.6 = (bf16[3,192,512]{2,1,0:T(8,128)(2,1)}, bf16[3,192,512]{2,1,0:T(8,128)(2,1)S(1)}, u32[]{:S(2)}) copy-start(bf16[3,192,512]{2,1,0:T(8,128)(2,1)S(1)} %collective-permute-done.1.right_hbm) | copy-start | bytes 1769476
  35.2 8.2 %copy-start.7 = (bf16[3,192,512]{2,1,0:T(8,128)(2,1)}, bf16[3,192,512]{2,1,0:T(8,128)(2,1)S(1)}, u32[]{:S(2)}) copy-start(bf16[3,192,512]{2,1,0:T(8,128)(2,1)S(1)} %collective-permute-done.left_hbm) | copy-start | bytes 1769476
  43.4 14.9 %all-to-all-start.2 = ((bf16[16,96,128]{2,1,0:T(8,128)(2,1)}), bf16[16,96,128]{2,1,0:T(8,128)(2,1)S(1)}, u32[]{:S(2)}, u32[]{:S(2)}) async-start(bf16[16,96,128]{2,1,0:T(8,128)(2,1)} %upper_sums.2), calls=%async_computation.2 | async-start | bytes 786432 | tf_op jit(solution)/shard_map/all_to_all | solution.py:521
  49.0 9.2 %copy-start = (bf16[8,1536,128]{2,1,0:T(8,128)(2,1)S(1)}, bf16[8,1536,128]{2,1,0:T(8,128)(2,1)}, u32[]{:S(2)}) copy-start(bf16[8,1536,128]{2,1,0:T(8,128)(2,1)} %basis_ref.3) | copy-start | bytes 9437188
  61.2 13.9 %all-to-all-start.3 = ((bf16[16,96,128]{2,1,0:T(8,128)(2,1)}), bf16[16,96,128]{2,1,0:T(8,128)(2,1)S(1)}, u32[]{:S(2)}, u32[]{:S(2)}) async-start(bf16[16,96,128]{2,1,0:T(8,128)(2,1)} %get-tuple-element.23), calls=%async_computation.3 | async-start | bytes 786432 | tf_op jit(solution)/shard_map/all_to_all | solution.py:521
  65.3 21.3 %collective-permute-start.3 = (bf16[3,192,512]{2,1,0:T(8,128)(2,1)}, bf16[3,192,512]{2,1,0:T(8,128)(2,1)}, u32[]{:S(2)}, u32[]{:S(2)}) collective-permute-start(bf16[3,192,512]{2,1,0:T(8,128)(2,1)} %get-tuple-element.24.own_hbm), channel_id=1, source_target_pairs={{1,0},{2,1},{3,2},{4,3},{5,4},{6,5},{7,6},{8,7},{9,8},{10,9},{11,1... | collective-permute-start | bytes 1769480 | tf_op jit(solution)/shard_map/ppermute | solution.py:528
  73.2 15.0 %collective-permute-start.2 = (bf16[3,192,512]{2,1,0:T(8,128)(2,1)}, bf16[3,192,512]{2,1,0:T(8,128)(2,1)}, u32[]{:S(2)}, u32[]{:S(2)}) collective-permute-start(bf16[3,192,512]{2,1,0:T(8,128)(2,1)} %get-tuple-element.24.own_hbm), channel_id=1, source_target_pairs={{0,1},{1,2},{2,3},{3,4},{4,5},{5,6},{6,7},{7,8},{8,9},{9,10},{10,1... | collective-permute-start | bytes 1769480 | tf_op jit(solution)/shard_map/ppermute | solution.py:528
  75.8 15.8 %all-to-all-start.4 = ((bf16[16,48,128]{2,1,0:T(8,128)(2,1)}), bf16[16,48,128]{2,1,0:T(8,128)(2,1)}, u32[]{:S(2)}, u32[]{:S(2)}) async-start(bf16[16,48,128]{2,1,0:T(8,128)(2,1)} %plane_sums.3), calls=%async_computation.4 | async-start | bytes 393216 | tf_op jit(solution)/shard_map/all_to_all | solution.py:521
  93.4 14.6 %all-to-all-start.5 = ((bf16[16,96,128]{2,1,0:T(8,128)(2,1)}), bf16[16,96,128]{2,1,0:T(8,128)(2,1)S(1)}, u32[]{:S(2)}, u32[]{:S(2)}) async-start(bf16[16,96,128]{2,1,0:T(8,128)(2,1)} %upper_sums.3), calls=%async_computation.5 | async-start | bytes 786432 | tf_op jit(solution)/shard_map/all_to_all | solution.py:521
  108.0 23.4 %copy-start.1 = (f32[3,64,1536]{2,1,0:T(8,128)S(1)}, f32[3,64,1536]{2,1,0:T(8,128)}, u32[]{:S(2)}) copy-start(f32[3,64,1536]{2,1,0:T(8,128)} %param.9) | copy-start | bytes 3538948
  108.0 23.4 %copy-start.2 = (f32[192,1536]{1,0:T(8,128)S(1)}, f32[192,1536]{1,0:T(8,128)}, u32[]{:S(2)}) copy-start(f32[192,1536]{1,0:T(8,128)} %get-tuple-element.28.residual_hbm.residual_ref) | copy-start | bytes 3538948
  108.0 23.4 %copy-start.3 = (f32[8,1536]{1,0:T(8,128)S(1)}, f32[8,1536]{1,0:T(8,128)}, u32[]{:S(2)}) copy-start(f32[8,1536]{1,0:T(8,128)} %sort_panels.1.rest_1_.sorted_ref) | copy-start | bytes 147460
